TPU v7x, 32 devices: a whole 2x2x4 slice. The times are simulated.
32 devices in a mesh: space: 8 (over z, x), tile: 4 (over y, core).
Axes of the slice: x: 2, y: 2, z: 4, core: 2. Of those that a mesh axis runs over, the one named last changes fastest.
Arguments:
- eigenvectors: float32 [2, 256, 3, 32768], P(None, None, None, ('space', 'tile')), may hold values from -6 to 6
- perambulator: float32 [2, 1024, 1024], P(None, 'space'), may hold values from -6 to 6
- momenta: int32 [2, 3], replicated, may hold values from 1 to 2
- graph_blocks: int32 [32, 2], replicated, may hold values from 0 to 7
Outputs:
- elementals: float32 [2, 2, 256, 256], P(None, None, 'tile', 'space')
- contractions: float32 [32, 2, 256, 256], P(('space', 'tile'))
All inputs are finite; a program needn't handle non-finite values.
Results may differ from a plain program's by a relative error of at most 0.00016.
Values sent between devices are 32-bit elements; how exact they have to be, the bound alone decides.
No kernel may reach another device: no remote copies, remote signals or barrier semaphores. Data moves between devices by JAX's collectives and lax.ppermute only.
A program may use at most 64 MiB of HBM per device.

v0:
```python
import math

import jax
import jax.numpy as jnp
from jax import lax
from jax.sharding import PartitionSpec as P

NEV = 256
NC = 3
SPIN = 4
GRAPH_DEV = 1


lattice_edge = 64


def inner_product(left, right):
    return lax.dot_general(
        left,
        right,
        (((1,), (1,)), ((), ())),
        precision=lax.Precision.HIGHEST,
        preferred_element_type=jnp.float32,
    )


def phased_gram(vectors, momenta, first_site):
    vector_count = vectors.shape[1]
    site_index = first_site + lax.iota(jnp.int32, vectors.shape[3])
    x_pos = site_index % lattice_edge
    y_pos = site_index // lattice_edge % lattice_edge
    z_pos = site_index // (lattice_edge * lattice_edge)
    wave_number = (
        momenta[:, 0:1] * x_pos[None, :]
        + momenta[:, 1:2] * y_pos[None, :]
        + momenta[:, 2:3] * z_pos[None, :]
    ) % lattice_edge
    phase_angle = wave_number.astype(jnp.float32) * (2.0 * math.pi / lattice_edge)
    cosine = jnp.cos(phase_angle)
    sine_part = jnp.sin(phase_angle)
    real_part = vectors[0]
    imag_part = vectors[1]
    flat_real = real_part.reshape(vector_count, -1)
    flat_imag = imag_part.reshape(vector_count, -1)
    stacked = []
    for moment in range(momenta.shape[0]):
        cos_row = cosine[moment][None, None, :]
        sin_row = sine_part[moment][None, None, :]
        phased_real = (cos_row * real_part + sin_row * imag_part).reshape(vector_count, -1)
        phased_imag = (cos_row * imag_part - sin_row * real_part).reshape(vector_count, -1)
        gram_real = inner_product(flat_real, phased_real) + inner_product(flat_imag, phased_imag)
        gram_imag = inner_product(flat_real, phased_imag) - inner_product(flat_imag, phased_real)
        stacked.append(jnp.stack([gram_real, gram_imag]))
    return jnp.stack(stacked)


def transport(elementals_rows, perambulator_part):
    sources = perambulator_part.shape[1]
    vector_count = elementals_rows.shape[3]
    tensor = perambulator_part.reshape(2, sources, vector_count, -1)

    def apply_part(tau_part, phi_part):
        return jnp.einsum(
            "cja,mij->mcia",
            tau_part,
            phi_part,
            precision=lax.Precision.HIGHEST,
            preferred_element_type=jnp.float32,
        )

    mixed_real = apply_part(tensor[0], elementals_rows[:, 0]) - apply_part(
        tensor[1], elementals_rows[:, 1]
    )
    mixed_imag = apply_part(tensor[0], elementals_rows[:, 1]) + apply_part(
        tensor[1], elementals_rows[:, 0]
    )
    row_total = elementals_rows.shape[2] * tensor.shape[3]
    result = jnp.stack([mixed_real, mixed_imag], axis=1)
    return result.reshape(result.shape[0], 2, sources, row_total) * (1.0 / math.sqrt(vector_count))


def pair_product(left, right):

    def contract(first, second):
        return jnp.einsum(
            "gcr,gcs->grs",
            first,
            second,
            precision=lax.Precision.HIGHEST,
            preferred_element_type=jnp.float32,
        )

    pair_real = contract(left[:, 0], right[:, 0]) - contract(left[:, 1], right[:, 1])
    pair_imag = contract(left[:, 0], right[:, 1]) + contract(left[:, 1], right[:, 0])
    return jnp.stack([pair_real, pair_imag], axis=1)


def per_device(eigenvectors, perambulator, momenta, graph_blocks):
    space_count = lax.axis_size("space")
    tile_count = lax.axis_size("tile")
    space_index = lax.axis_index("space")
    tile_index = lax.axis_index("tile")
    local_sites = eigenvectors.shape[3]
    first_site = (space_index * tile_count + tile_index) * local_sites
    norm_factor = 1.0 / math.sqrt(NC * local_sites * space_count * tile_count)
    partial_value = phased_gram(eigenvectors, momenta, first_site) * norm_factor
    col_width = NEV // space_count
    row_sum = lax.psum_scatter(partial_value, "tile", scatter_dimension=2, tiled=True)
    row_block = lax.psum(row_sum, "space")
    elementals = lax.dynamic_slice_in_dim(row_block, space_index * col_width, col_width, 3)
    mixed_rows = transport(row_block, perambulator)
    gathered = lax.all_gather(mixed_rows[:, None], "tile", axis=1, tiled=True)
    blocks = gathered.reshape(-1, 2, mixed_rows.shape[2], mixed_rows.shape[3])
    group_list = lax.dynamic_slice_in_dim(
        graph_blocks.reshape(space_count, tile_count, GRAPH_DEV, 2), tile_index, 1, 1
    ).reshape(-1, 2)
    inverse_root = 1.0 / math.sqrt(SPIN * NEV)
    outgoing = blocks[group_list].reshape(
        space_count, GRAPH_DEV, 2, 2, blocks.shape[2], blocks.shape[3]
    )
    pieces_now = lax.all_to_all(outgoing, "space", split_axis=0, concat_axis=4, tiled=True)[0]
    contractions = pair_product(pieces_now[:, 0], pieces_now[:, 1]) * inverse_root
    return (elementals, contractions)


def solution(mesh):
    in_specs = (P(None, None, None, ("space", "tile")), P(None, "space", None), P(), P())
    out_specs = (P(None, None, "tile", "space"), P(("space", "tile"), None, None, None))
    return jax.shard_map(
        per_device, mesh=mesh, in_specs=in_specs, out_specs=out_specs, check_vma=False
    )
```

profile of v0, /device:TPU:0, one launch (start us, length us, event | category | flops | bytes accessed | tf_op | source)
XLA Modules:
  0.0 306.3 jit_solution(17258528459394033669)
XLA Ops:
  7.3 1.0 slice_reduce_fusion.2
  8.7 9.8 %fusion.83 = f32[256,256]{1,0:T(8,128)S(1)} fusion(f32[2,256,3,1024]{3,1,2,0:T(8,128)} %param.4, f32[1024]{0:T(1024)S(1)} %bitcast.251, f32[1024]{0:T(1024)S(1)} %bitcast.243), kind=kOutput, calls=%fused_computation.72 | convolution fusion | flops 2418278400 | bytes 9707520 | tf_op jit(solution)/shard_map/dot_general | solution.py:18
  18.5 3.0 fusion.78
  21.5 3.0 fusion.63
  24.5 3.0 fusion.58
  27.5 3.3 %fusion.105 = f32[1,256,256]{1,2,0:T(8,128)S(1)} fusion(f32[256,256]{1,0:T(8,128)S(1)} %fusion.83, f32[2,256,3,1024]{3,1,2,0:T(8,128)S(1)} %copy-done, f32[1024]{0:T(1024)S(1)} %bitcast.253, f32[1024]{0:T(1024)S(1)} %bitcast.245), kind=kOutput, calls=%fused_computation.80 | convolution fusion | flops 2418343936 | bytes 9969664 | tf_op jit(solution)/shard_map/dot_general | solution.py:18
  30.8 3.0 fusion.115
  33.8 3.0 fusion.125
  36.9 3.0 fusion.135
  40.1 1.3 copy.39
  41.5 0.6 dynamic-slice
  42.7 37.6 %all-reduce.6.cloned.1.call-done = f32[2,2,256,256]{3,1,0,2:T(2,128)} async-done(((f32[2,2,256,256]{3,1,0,2:T(2,128)}), f32[2,2,256,256]{3,1,0,2:T(2,128)}) %all-reduce.6.cloned.1.call-update) | async-done | bytes 1048592
  80.4 1.0 constant_dynamic-slice_fusion
  81.3 0.8 copy.40
  83.4 72.2 %all-reduce.4.cloned.1.call-done = f32[2,2,64,256]{3,2,0,1:T(8,128)} async-done(((f32[2,2,64,256]{3,2,0,1:T(8,128)}), f32[2,2,64,256]{3,2,0,1:T(8,128)}) %all-reduce.4.cloned.1.call-update) | async-done | bytes 262160 | tf_op jit(solution)/shard_map/psum | solution.py:109
  155.6 1.6 fusion.144
  157.2 1.5 fusion.56
  159.0 1.5 fusion.146
  160.5 0.6 fusion.57
  161.4 1.0 copy.49
  162.9 21.5 %all-gather.2.cloned.1.call-done = f32[2,4,2,128,256]{4,3,2,0,1:T(8,128)} async-done(((f32[2,1,2,128,256]{4,3,2,0,1:T(8,128)}), f32[2,4,2,128,256]{4,3,2,0,1:T(8,128)}) %all-gather.2.cloned.1.call-update) | async-done | bytes 2097168 | tf_op jit(solution)/shard_map/all_gather | solution.py:112
  184.5 1.8 copy.50
  186.3 2.8 gather_fusion
  189.1 5.5 %all-to-all-start = ((f32[8,1,2,2,128,256]{5,4,3,2,1,0:T(8,128)}), f32[8,1,2,2,128,256]{5,4,3,2,1,0:T(8,128)}, u32[]{:S(2)}, u32[]{:S(2)}) async-start(f32[8,1,2,2,128,256]{5,4,3,2,1,0:T(8,128)} %bitcast.234), calls=%async_computation | async-start | bytes 8388608 | tf_op jit(solution)/shard_map/all_to_all | solution.py:121
  194.7 0.7 copy.54
  195.4 92.9 %all-to-all-done = f32[8,1,2,2,128,256]{5,4,3,2,1,0:T(8,128)} async-done(((f32[8,1,2,2,128,256]{5,4,3,2,1,0:T(8,128)}), f32[8,1,2,2,128,256]{5,4,3,2,1,0:T(8,128)}, u32[]{:S(2)}, u32[]{:S(2)}) %all-to-all-start) | async-done | bytes 4194336 | tf_op jit(solution)/shard_map/all_to_all | solution.py:121
  288.3 2.5 copy.53
  291.2 1.8 fusion.140
  293.0 1.8 fusion.141
  294.8 1.8 fusion.98
  296.7 1.8 fusion.99
  298.5 0.8 maximum_multiply_fusion.2
  (41 shorter events, 3.2 us)
Async XLA Ops:
  7.2 73.2 %all-reduce.6.cloned.1.call-start = ((), (), s32[]{:S(2)}) async-start(), calls=%async_computation.3 | async-start | bytes 2097152
  8.6 9.8 %copy-start = (f32[2,256,3,1024]{3,1,2,0:T(8,128)S(1)}, f32[2,256,3,1024]{3,1,2,0:T(8,128)}, u32[]{:S(2)}) copy-start(f32[2,256,3,1024]{3,1,2,0:T(8,128)} %param.4) | copy-start | bytes 18874372
  39.9 1.6 copy-start.4
  40.0 42.4 %copy-start.2 = (f32[2,128,1024]{2,1,0:T(8,128)S(1)}, f32[2,128,1024]{2,1,0:T(8,128)}, u32[]{:S(2)}) copy-start(f32[2,128,1024]{2,1,0:T(8,128)} %param.5) | copy-start | bytes 3145732
  41.4 114.2 %all-reduce.4.cloned.1.call-start = ((), (), s32[]{:S(2)}) async-start(), calls=%async_computation.1 | async-start | bytes 524288 | tf_op jit(solution)/shard_map/psum | solution.py:109
  82.1 102.4 %all-gather.2.cloned.1.call-start = ((), (), s32[]{:S(2)}) async-start(), calls=%async_computation.2 | async-start | bytes 2621440 | tf_op jit(solution)/shard_map/all_gather | solution.py:112
  155.6 4.9 %copy-start.1 = (f32[2,2,64,256]{3,2,0,1:T(8,128)S(1)}, f32[2,2,64,256]{3,2,0,1:T(8,128)}, u32[]{:S(2)}) copy-start(f32[2,2,64,256]{3,2,0,1:T(8,128)} %all-reduce.4.cloned.1.call-done) | copy-start | bytes 786436
  158.8 3.6 %copy-start.3 = (s32[32,2]{0,1:T(2,128)S(1)}, s32[32,2]{0,1:T(2,128)}, u32[]{:S(2)}) copy-start(s32[32,2]{0,1:T(2,128)} %param.7) | copy-start | bytes 772
  189.1 99.2 %all-to-all-start = ((f32[8,1,2,2,128,256]{5,4,3,2,1,0:T(8,128)}), f32[8,1,2,2,128,256]{5,4,3,2,1,0:T(8,128)}, u32[]{:S(2)}, u32[]{:S(2)}) async-start(f32[8,1,2,2,128,256]{5,4,3,2,1,0:T(8,128)} %bitcast.234), calls=%async_computation | async-start | bytes 8388608 | tf_op jit(solution)/shard_map/all_to_all | solution.py:121
Sparse Core Ops, SparseCore 0:
  41.6 38.7 all-reduce.5
  84.7 70.9 all-reduce.3
  162.6 21.8 all-gather.1
where the time goes:
time: 310 us; the launch traced here: 306 us
  waiting for transfers between devices  224 us (72%)
  matrix products  43.8 us (14%)
  local copies, waits for them, and re-layouts  15.8 us (5%)
  between operations  15.2 us (5%)
  starting transfers between devices  5.88 us (2%)
    all_to_all x1, waiting for transfers between devices, per_device(): lax.all_to_all(outgoing, 'space', split_axis=0, concat_axis=4, tiled=True)  92.9 us
    psum x1, waiting for transfers between devices, per_device(): row_block = lax.psum(row_sum, 'space')  72.2 us
    unnamed x4, waiting for transfers between devices  37.7 us
    dot_general x8, matrix products, inner_product(): lax.dot_general(left, right, (((1,), (1,)), ((), ())), precision=lax.Prec...  31.1 us
    all_gather x1, waiting for transfers between devices, per_device(): gathered = lax.all_gather(mixed_rows[:, None], 'tile', axis=1, tiled=True)  21.5 us
    dot_general x4, matrix products, contract(): jnp.einsum('gcr,gcs->grs', first, second, precision=lax.Precision.HIGHEST...  7.3 us
  transfers between devices with their start and end apart: 4, of which 4 were waited for; matrix products, arithmetic and copies ran while one was open for 1% of the time, Pallas kernels for 0%

commit v1 on v0

v1 whole, which is shorter than its diff:
```python
import functools
import math

import jax
import jax.numpy as jnp
from jax import lax
from jax.experimental import pallas as pl
from jax.experimental.pallas import tpu as pltpu
from jax.sharding import PartitionSpec as P

LATTICE_EDGE = 64
LANES = 128
F32 = jnp.float32
BF16 = jnp.bfloat16
VMEM_LIMIT = 48 * 1024 * 1024


def bits_of(count):
    return range(count.bit_length() - 1)


def split(value):
    high = value.astype(BF16)
    return high, (value - high.astype(F32)).astype(BF16)


def dot_nt(left, right):
    return lax.dot_general(left, right, (((1,), (1,)), ((), ())), preferred_element_type=F32)


def dot_tn(left, right):
    return lax.dot_general(left, right, (((0,), (0,)), ((), ())), preferred_element_type=F32)


def gram_kernel(momenta, first_site, vectors, total, *, chunks, norm):
    step = pl.program_id(0)
    width = vectors.shape[3]

    @pl.when(step == 0)
    def _():
        total[...] = jnp.zeros_like(total)

    site = first_site[0] + (step % chunks) * width + lax.broadcasted_iota(jnp.int32, (1, width), 1)
    x_pos = site % LATTICE_EDGE
    y_pos = site // LATTICE_EDGE % LATTICE_EDGE
    z_pos = site // (LATTICE_EDGE * LATTICE_EDGE)
    real = vectors[0, 0]
    imag = vectors[1, 0]
    real_hi, real_lo = split(real)
    imag_hi, imag_lo = split(imag)
    left_hi = jnp.concatenate([real_hi, imag_hi], axis=0)
    left_lo = jnp.concatenate([real_lo, imag_lo], axis=0)
    count = real.shape[0]

    def product(right):
        hi, lo = split(right)
        return dot_nt(left_hi, hi) + dot_nt(left_hi, lo) + dot_nt(left_lo, hi)

    for p in range(total.shape[0]):
        wave = (momenta[p, 0] * x_pos + momenta[p, 1] * y_pos + momenta[p, 2] * z_pos) % LATTICE_EDGE
        theta = wave.astype(F32) * (2.0 * math.pi / LATTICE_EDGE)
        cosine, sine = jnp.cos(theta), jnp.sin(theta)
        by_real = product(cosine * real + sine * imag)
        by_imag = product(cosine * imag - sine * real)
        total[p, 0] += by_real[:count] + by_imag[count:]
        total[p, 1] += by_imag[:count] - by_real[count:]

    @pl.when(step == pl.num_programs(0) - 1)
    def _():
        total[...] *= norm


def local_gram(vectors, momenta, first_site, norm):
    planes = vectors.transpose(0, 2, 1, 3)
    _, colours, count, sites = planes.shape
    width = min(sites, 512)
    chunks = sites // width
    moments = momenta.shape[0]
    return pl.pallas_call(
        functools.partial(gram_kernel, chunks=chunks, norm=norm),
        grid=(colours * chunks,),
        in_specs=[
            pl.BlockSpec(memory_space=pltpu.SMEM),
            pl.BlockSpec(memory_space=pltpu.SMEM),
            pl.BlockSpec((2, 1, count, width), lambda s: (0, s // chunks, 0, s % chunks)),
        ],
        out_specs=pl.BlockSpec((moments, 2, count, count), lambda s: (0, 0, 0, 0)),
        out_shape=jax.ShapeDtypeStruct((moments, 2, count, count), F32),
        compiler_params=pltpu.CompilerParams(vmem_limit_bytes=VMEM_LIMIT),
        cost_estimate=pl.CostEstimate(
            flops=24 * moments * count * count * colours * sites,
            bytes_accessed=8 * count * colours * sites,
            transcendentals=0,
        ),
        name="local_gram",
    )(momenta, first_site, planes)


def swap(value, axis, bit):
    size = lax.axis_size(axis)
    return lax.ppermute(value, axis, [(i, i ^ (1 << bit)) for i in range(size)])


def shift(value, axis, by):
    size = lax.axis_size(axis)
    return lax.ppermute(value, axis, [(i, i + by) for i in range(size) if 0 <= i + by < size])


def own_bit(axis, bit):
    return (lax.axis_index(axis) >> bit) & 1


def halve(value, axis, bit):
    mine = own_bit(axis, bit)
    half = value.shape[0] // 2
    away = lax.dynamic_slice_in_dim(value, (1 - mine) * half, half, 0)
    kept = lax.dynamic_slice_in_dim(value, mine * half, half, 0)
    return kept + swap(away, axis, bit)


def double(value, axis, bit):
    other = swap(value, axis, bit)
    return jnp.where(
        own_bit(axis, bit) == 0,
        jnp.concatenate([value, other]),
        jnp.concatenate([other, value]),
    )


def sum_everywhere(rows):
    tile_bits = [("tile", b) for b in bits_of(lax.axis_size("tile"))]
    space_bits = [("space", b) for b in bits_of(lax.axis_size("space"))]
    scattered = tile_bits + space_bits[:1]
    for axis, bit in scattered:
        rows = halve(rows, axis, bit)
    for axis, bit in space_bits[1:]:
        rows = rows + swap(rows, axis, bit)
    for axis, bit in scattered[::-1]:
        rows = double(rows, axis, bit)
    return rows


def gather_perambulator(part):
    half = part.shape[1] // 2
    part = lax.dynamic_slice_in_dim(part, own_bit("tile", 0) * half, half, 1)
    spin = 4
    own = part.reshape(2, half, -1, spin).transpose(0, 3, 1, 2)
    length = lax.axis_size("space") // 2
    place = lax.axis_index("space") // 2
    below, above = [own], [own]
    for _ in range(length - 1):
        below.append(shift(below[-1], "space", 2))
        above.append(shift(above[-1], "space", -2))
    column = [own]
    for s in range(1, length):
        column.append(jnp.where(place >= s, below[s], above[length - s]))
    plane = column + [swap(piece, "space", 0) for piece in column]
    return plane + [swap(piece, "tile", 0) for piece in plane]


def pair_kernel(blocks, elementals, order, *refs, pieces, scale):
    sources = refs[:pieces]
    out = refs[pieces]
    tau, left_hi, left_lo, right_hi, right_lo, woven, arrived = refs[pieces + 1 :]
    for n in range(pieces):
        pltpu.make_async_copy(sources[n], tau.at[n], arrived.at[n]).start()
    _, spin, depth, count = tau.shape[1:]
    rows = left_hi.shape[1] // (2 * spin)
    tiles = count // rows
    real_rows, imag_rows = [], []
    for side in range(2):
        block = blocks[side]
        p = block // tiles
        first = pl.multiple_of(block % tiles * rows, rows)
        real = elementals[p, 0, pl.ds(first, rows), :]
        imag = elementals[p, 1, pl.ds(first, rows), :]
        real_rows += [real, imag]
        imag_rows += [-imag, real]
    weights = jnp.concatenate(
        [jnp.concatenate(real_rows, axis=0), jnp.concatenate(imag_rows, axis=0)], axis=1
    )
    weights_hi, weights_lo = split(weights)
    for n in range(pieces):
        pltpu.make_async_copy(sources[n], tau.at[n], arrived.at[n]).wait()
        given = jnp.concatenate(
            [tau[n, 0].reshape(spin * depth, count), tau[n, 1].reshape(spin * depth, count)], axis=1
        )
        given_hi, given_lo = split(given)
        mixed = dot_nt(given_hi, weights_hi) + dot_nt(given_hi, weights_lo) + dot_nt(given_lo, weights_hi)
        mixed_hi, mixed_lo = split(mixed)
        here = pl.ds(n * depth, depth)
        for a in range(spin):
            lanes = pl.ds(a * 2 * rows, 2 * rows)
            left_hi[here, lanes] = mixed_hi[a * depth : (a + 1) * depth, : 2 * rows]
            left_lo[here, lanes] = mixed_lo[a * depth : (a + 1) * depth, : 2 * rows]
            right_hi[here, lanes] = mixed_hi[a * depth : (a + 1) * depth, 2 * rows :]
            right_lo[here, lanes] = mixed_lo[a * depth : (a + 1) * depth, 2 * rows :]
    pair = (
        dot_tn(left_hi[...], right_hi[...])
        + dot_tn(left_hi[...], right_lo[...])
        + dot_tn(left_lo[...], right_hi[...])
    ) * scale
    pair_hi, pair_lo = split(pair)
    placed = jnp.dot(pair_hi, order[...], preferred_element_type=F32) + jnp.dot(
        pair_lo, order[...], preferred_element_type=F32
    )
    width = rows * spin
    for a in range(spin):
        top = placed[2 * a * rows : (2 * a + 1) * rows]
        low = placed[(2 * a + 1) * rows : (2 * a + 2) * rows]
        parts = top[:, :width] - low[:, width:], top[:, width:] + low[:, :width]
        for n, value in enumerate(parts):
            for c in range(width // LANES):
                woven[n, c, pl.ds(a, rows, stride=spin), :] = value[:, c * LANES : (c + 1) * LANES]
    for n in range(2):
        for c in range(width // LANES):
            out[n, :, c * LANES : (c + 1) * LANES] = woven[n, c]


def lane_order(rows, spin):
    size = 2 * rows * spin
    lane = lax.iota(jnp.int32, size)
    a, part, i = lane // (2 * rows), lane // rows % 2, lane % rows
    target = part * rows * spin + i * spin + a
    return (target[:, None] == lane[None, :]).astype(BF16)


def pair_contraction(blocks, elementals, pieces, scale):
    _, spin, depth, count = pieces[0].shape
    rows = count // lax.axis_size("tile")
    size = 2 * rows * spin
    number = len(pieces)
    stored = pltpu.VMEM((number * depth, size), BF16)
    return pl.pallas_call(
        functools.partial(pair_kernel, pieces=number, scale=scale),
        in_specs=[
            pl.BlockSpec(memory_space=pltpu.SMEM),
            pl.BlockSpec(memory_space=pltpu.VMEM),
            pl.BlockSpec(memory_space=pltpu.VMEM),
        ]
        + [pl.BlockSpec(memory_space=pl.ANY)] * number,
        out_specs=pl.BlockSpec(memory_space=pltpu.VMEM),
        out_shape=jax.ShapeDtypeStruct((2, rows * spin, rows * spin), F32),
        scratch_shapes=[
            pltpu.VMEM((number,) + pieces[0].shape, F32),
            stored,
            stored,
            stored,
            stored,
            pltpu.VMEM((2, rows * spin // LANES, rows * spin, LANES), F32),
            pltpu.SemaphoreType.DMA((number,)),
        ],
        compiler_params=pltpu.CompilerParams(vmem_limit_bytes=VMEM_LIMIT),
        name="pair_contraction",
    )(blocks, elementals, lane_order(rows, spin), *pieces)


def per_device(eigenvectors, perambulator, momenta, graph_blocks):
    space_count = lax.axis_size("space")
    tile_count = lax.axis_size("tile")
    space_index = lax.axis_index("space")
    tile_index = lax.axis_index("tile")
    device = space_index * tile_count + tile_index
    _, count, colours, sites = eigenvectors.shape
    order = perambulator.shape[2]
    first_site = (device * sites).astype(jnp.int32).reshape(1)
    norm = 1.0 / math.sqrt(colours * sites * space_count * tile_count)
    pieces = gather_perambulator(perambulator)
    partial = local_gram(eigenvectors, momenta, first_site, norm)
    full = sum_everywhere(partial.reshape(-1, count)).reshape(partial.shape)
    rows, columns = count // tile_count, count // space_count
    elementals = lax.dynamic_slice(
        full, (0, 0, tile_index * rows, space_index * columns), full.shape[:2] + (rows, columns)
    )
    scale = 1.0 / (count * math.sqrt(order))
    contractions = pair_contraction(graph_blocks[device], full, pieces, scale)
    return elementals, contractions[None]


def solution(mesh):
    in_specs = (P(None, None, None, ("space", "tile")), P(None, "space", None), P(), P())
    out_specs = (P(None, None, "tile", "space"), P(("space", "tile"), None, None, None))
    return jax.shard_map(
        per_device, mesh=mesh, in_specs=in_specs, out_specs=out_specs, check_vma=False
    )
```

time: 310 us -> 138 us (0.45)
  waiting for transfers between devices: 224 us -> 60.9 us
  matrix products: 43.8 us -> 0 us
  Pallas kernels: 0 us -> 28.9 us
  starting transfers between devices: 5.88 us -> 33.8 us
  between operations: 15.2 us -> 1.18 us
  local copies, waits for them, and re-layouts: 15.8 us -> 5.3 us
  other arithmetic: 1.3 us -> 7.25 us
    all_to_all x1 -> x0, waiting for transfers between devices: 92.9 us -> none  [per_device(): lax.all_to_all(outgoing, 'space', split_axis=0, concat_axis=4, tiled=True)]
    psum x1 -> x0, waiting for transfers between devices: 72.2 us -> none  [per_device(): row_block = lax.psum(row_sum, 'space')]
    ppermute x0 -> x26, waiting for transfers between devices: none -> 60.9 us  [the longest x20 53.1 us: swap(): return lax.ppermute(value, axis, [(i, i ^ 1 << bit) for i in range(size)])]
    dot_general x16 -> x0, matrix products: 43.8 us -> none  [the longest x8 31.1 us: inner_product(): lax.dot_general(left, right, (((1,), (1,)), ((), ())), precision=lax.Prec...]
    unnamed x4 -> x0, waiting for transfers between devices: 37.7 us -> none
    ppermute x0 -> x26, starting transfers between devices: none -> 33.8 us  [the longest x6 18.5 us: shift(): lax.ppermute(value, axis, [(i, i + by) for i in range(size) if 0 <= i + b...]
    pallas_call x0 -> x2, Pallas kernels: none -> 28.9 us  [the longest x1 15 us: pair_contraction(): pl.pallas_call(functools.partial(pair_kernel, pieces=number, scale=scale)...]
    all_gather x1 -> x0, waiting for transfers between devices: 21.5 us -> none  [per_device(): gathered = lax.all_gather(mixed_rows[:, None], 'tile', axis=1, tiled=True)]
  transfers between devices with their start and end apart: 4 -> 26, of which waited for: 4 -> 10; matrix products, arithmetic and copies ran while one was open for 1% -> 6% of each run, Pallas kernels for 0% -> 0%
where the time goes in v1:
time: 138 us; the launch traced here: 137 us
  waiting for transfers between devices  60.9 us (44%)
  starting transfers between devices  33.8 us (24%)
  Pallas kernels  28.9 us (21%)
  other arithmetic  7.25 us (5%)
  local copies, waits for them, and re-layouts  5.3 us (4%)
    ppermute x20, waiting for transfers between devices, swap(): return lax.ppermute(value, axis, [(i, i ^ 1 << bit) for i in range(size)])  53.1 us
    ppermute x6, starting transfers between devices, shift(): lax.ppermute(value, axis, [(i, i + by) for i in range(size) if 0 <= i + b...  18.5 us
    ppermute x20, starting transfers between devices, swap(): return lax.ppermute(value, axis, [(i, i ^ 1 << bit) for i in range(size)])  15.2 us
    pallas_call x1, Pallas kernels, pair_contraction(): pl.pallas_call(functools.partial(pair_kernel, pieces=number, scale=scale)...  15 us
    pallas_call x1, Pallas kernels, local_gram(): pl.pallas_call(functools.partial(gram_kernel, chunks=chunks, norm=norm),...  13.9 us
    ppermute x6, waiting for transfers between devices, shift(): lax.ppermute(value, axis, [(i, i + by) for i in range(size) if 0 <= i + b...  7.8 us
    unnamed x21, local copies, waits for them, and re-layouts  3.51 us
    select_n x3, other arithmetic, gather_perambulator(): column.append(jnp.where(place >= s, below[s], above[length - s]))  3.45 us
  transfers between devices with their start and end apart: 26, of which 10 were waited for; matrix products, arithmetic and copies ran while one was open for 6% of the time, Pallas kernels for 0%

profile of v1, /device:TPU:0, one launch (start us, length us, event | category | flops | bytes accessed | tf_op | source)
XLA Modules:
  0.0 137.3 jit_solution(422109559684831551)
XLA Ops:
  0.7 0.8 copy-done.2
  1.4 13.9 %local_gram.1 = f32[2,2,256,256]{3,2,1,0:T(8,128)S(1)} custom-call(s32[2,3]{1,0:T(2,128)S(1)} %copy-done.2, s32[1]{0:T(128)} %bitcast.first_site, f32[2,3,256,1024]{3,2,1,0:T(8,128)} %bitcast.18), custom_call_target="tpu_custom_call" | custom-call | flops 9663676416 | bytes 6291456 | tf_op jit(solution)/shard_map/local_gram/pallas_call | solution.py:79
  15.9 1.5 %collective-permute-done = f32[512,256]{1,0:T(8,128)S(1)} collective-permute-done((f32[512,256]{1,0:T(8,128)S(1)}, f32[512,256]{1,0:T(8,128)S(1)}, u32[]{:S(2)}, u32[]{:S(2)}) %collective-permute-start) | collective-permute-done | bytes 524320 | tf_op jit(solution)/shard_map/ppermute | solution.py:101
  18.2 2.9 %collective-permute-start.1 = (f32[256,256]{1,0:T(8,128)}, f32[256,256]{1,0:T(8,128)}, u32[]{:S(2)}, u32[]{:S(2)}) collective-permute-start(f32[256,256]{1,0:T(8,128)} %constant_dynamic-slice_fusion.4), channel_id=1, source_target_pairs={{0,2},{1,3},{2,0},{3,1},{4,6},{5,7},{6,4},{7,5},{8,10},{9,11},{10,... | collective-permute-start | bytes 786440 | tf_op jit(solution)/shard_map/ppermute | solution.py:101
  21.8 1.3 collective-permute-start.9
  23.1 4.6 %collective-permute-start.8 = (f32[2,4,64,256]{3,2,1,0:T(8,128)S(1)}, f32[2,4,64,256]{3,2,1,0:T(8,128)S(1)}, u32[]{:S(2)}, u32[]{:S(2)}) collective-permute-start(f32[2,4,64,256]{3,2,1,0:T(8,128)S(1)} %bitcast.8), channel_id=1, source_target_pairs={{0,8},{4,12},{8,16},{12,20},{16,24},{20,28},{1,9},{5,13},{9,17},{1... | collective-permute-start | bytes 1572872 | tf_op jit(solution)/shard_map/ppermute | solution.py:106
  28.0 1.0 dynamic-slice_add_fusion.1
  29.0 1.8 %collective-permute-start.2 = (f32[128,256]{1,0:T(8,128)S(1)}, f32[128,256]{1,0:T(8,128)S(1)}, u32[]{:S(2)}, u32[]{:S(2)}) collective-permute-start(f32[128,256]{1,0:T(8,128)S(1)} %constant_dynamic-slice_fusion.3), channel_id=1, source_target_pairs={{0,4},{4,0},{8,12},{12,8},{16,20},{20,16},{24,28},{28,24},{1,5},{5... | collective-permute-start | bytes 393224 | tf_op jit(solution)/shard_map/ppermute | solution.py:101
  31.1 6.3 %collective-permute-done.9 = f32[2,4,64,256]{3,2,1,0:T(8,128)S(1)} collective-permute-done((f32[2,4,64,256]{3,2,1,0:T(8,128)S(1)}, f32[2,4,64,256]{3,2,1,0:T(8,128)S(1)}, u32[]{:S(2)}, u32[]{:S(2)}) %collective-permute-start.9) | collective-permute-done | bytes 524320 | tf_op jit(solution)/shard_map/ppermute | solution.py:106
  37.4 1.3 collective-permute-start.10
  38.7 5.4 %collective-permute-start.12 = (f32[2,4,64,256]{3,2,1,0:T(8,128)S(1)}, f32[2,4,64,256]{3,2,1,0:T(8,128)}, u32[]{:S(2)}, u32[]{:S(2)}) collective-permute-start(f32[2,4,64,256]{3,2,1,0:T(8,128)S(1)} %collective-permute-done.8), channel_id=1, source_target_pairs={{0,8},{4,12},{8,16},{12,20},{16,24},{20,28},{1,9},{5,13},{9,17},{1... | collective-permute-start | bytes 1572872 | tf_op jit(solution)/shard_map/ppermute | solution.py:106
  44.1 0.9 collective-permute-start.3
  45.0 11.3 %collective-permute-done.3 = f32[128,256]{1,0:T(8,128)S(1)} collective-permute-done((f32[128,256]{1,0:T(8,128)S(1)}, f32[128,256]{1,0:T(8,128)S(1)}, u32[]{:S(2)}, u32[]{:S(2)}) %collective-permute-start.3) | collective-permute-done | bytes 131104 | tf_op jit(solution)/shard_map/ppermute | solution.py:101
  56.2 3.4 %collective-permute-start.4 = (f32[128,256]{1,0:T(8,128)S(1)}, f32[128,256]{1,0:T(8,128)S(1)}, u32[]{:S(2)}, u32[]{:S(2)}) collective-permute-start(f32[128,256]{1,0:T(8,128)S(1)} %add.101), channel_id=1, source_target_pairs={{0,16},{4,20},{8,24},{12,28},{16,0},{20,4},{24,8},{28,12},{1,17},{... | collective-permute-start | bytes 393224 | tf_op jit(solution)/shard_map/ppermute | solution.py:101
  59.7 5.0 %collective-permute-done.4 = f32[128,256]{1,0:T(8,128)S(1)} collective-permute-done((f32[128,256]{1,0:T(8,128)S(1)}, f32[128,256]{1,0:T(8,128)S(1)}, u32[]{:S(2)}, u32[]{:S(2)}) %collective-permute-start.4) | collective-permute-done | bytes 131104 | tf_op jit(solution)/shard_map/ppermute | solution.py:101
  64.7 1.6 %collective-permute-start.5 = (f32[128,256]{1,0:T(8,128)S(1)}, f32[128,256]{1,0:T(8,128)S(1)}, u32[]{:S(2)}, u32[]{:S(2)}) collective-permute-start(f32[128,256]{1,0:T(8,128)S(1)} %add.102), channel_id=1, source_target_pairs={{0,4},{4,0},{8,12},{12,8},{16,20},{20,16},{24,28},{28,24},{1,5},{5... | collective-permute-start | bytes 393224 | tf_op jit(solution)/shard_map/ppermute | solution.py:101
  66.2 1.3 collective-permute-start.11
  68.1 4.7 %collective-permute-start.13 = (f32[2,4,64,256]{3,2,1,0:T(8,128)}, f32[2,4,64,256]{3,2,1,0:T(8,128)S(1)}, u32[]{:S(2)}, u32[]{:S(2)}) collective-permute-start(f32[2,4,64,256]{3,2,1,0:T(8,128)} %collective-permute-done.12), channel_id=1, source_target_pairs={{0,8},{4,12},{8,16},{12,20},{16,24},{20,28},{1,9},{5,13},{9,17},{1... | collective-permute-start | bytes 1572872 | tf_op jit(solution)/shard_map/ppermute | solution.py:106
  73.0 1.1 broadcast_select_fusion.1.refs_2_
  74.1 6.9 %collective-permute-done.6 = f32[256,256]{1,0:T(8,128)S(1)} collective-permute-done((f32[256,256]{1,0:T(8,128)S(1)}, f32[256,256]{1,0:T(8,128)S(1)}, u32[]{:S(2)}, u32[]{:S(2)}) %collective-permute-start.6) | collective-permute-done | bytes 262176 | tf_op jit(solution)/shard_map/ppermute | solution.py:101
  81.7 1.2 broadcast_select_fusion.2.refs_1_
  82.9 1.5 %collective-permute-done.13 = f32[2,4,64,256]{3,2,1,0:T(8,128)S(1)} collective-permute-done((f32[2,4,64,256]{3,2,1,0:T(8,128)}, f32[2,4,64,256]{3,2,1,0:T(8,128)S(1)}, u32[]{:S(2)}, u32[]{:S(2)}) %collective-permute-start.13) | collective-permute-done | bytes 524320 | tf_op jit(solution)/shard_map/ppermute | solution.py:106
  84.4 1.1 broadcast_select_fusion.refs_3_
  86.1 1.5 %collective-permute-start.17 = (f32[2,4,64,256]{3,2,1,0:T(8,128)S(1)}, f32[2,4,64,256]{3,2,1,0:T(8,128)}, u32[]{:S(2)}, u32[]{:S(2)}) collective-permute-start(f32[2,4,64,256]{3,2,1,0:T(8,128)S(1)} %broadcast_select_fusion.refs_3_), channel_id=1, source_target_pairs={{0,4},{4,0},{8,12},{12,8},{16,20},{20,16},{24,28},{28,24},{1,5},{5... | collective-permute-start | bytes 1572872 | tf_op jit(solution)/shard_map/ppermute | solution.py:101
  87.6 8.3 %collective-permute-done.16.refs_6_ = f32[2,4,64,256]{3,2,1,0:T(8,128)} collective-permute-done((f32[2,4,64,256]{3,2,1,0:T(8,128)S(1)}, f32[2,4,64,256]{3,2,1,0:T(8,128)}, u32[]{:S(2)}, u32[]{:S(2)}) %collective-permute-start.16) | collective-permute-done | bytes 524320 | tf_op jit(solution)/shard_map/ppermute | solution.py:101
  96.6 10.6 %collective-permute-done.15.refs_5_ = f32[2,4,64,256]{3,2,1,0:T(8,128)} collective-permute-done((f32[2,4,64,256]{3,2,1,0:T(8,128)S(1)}, f32[2,4,64,256]{3,2,1,0:T(8,128)}, u32[]{:S(2)}, u32[]{:S(2)}) %collective-permute-start.15) | collective-permute-done | bytes 524320 | tf_op jit(solution)/shard_map/ppermute | solution.py:101
  107.2 9.2 %collective-permute-done.17.refs_7_ = f32[2,4,64,256]{3,2,1,0:T(8,128)} collective-permute-done((f32[2,4,64,256]{3,2,1,0:T(8,128)S(1)}, f32[2,4,64,256]{3,2,1,0:T(8,128)}, u32[]{:S(2)}, u32[]{:S(2)}) %collective-permute-start.17) | collective-permute-done | bytes 524320 | tf_op jit(solution)/shard_map/ppermute | solution.py:101
  116.6 1.0 fusion.order
  117.6 1.7 %maximum_select_fusion = f32[1024,256]{1,0:T(8,128)S(1)} fusion(f32[512,256]{1,0:T(8,128)} %copy-done.5, f32[512,256]{1,0:T(8,128)} %copy-done.4, pred[]{:T(512)S(6)} %eq.25), kind=kLoop, calls=%fused_computation | loop fusion | flops 786432 | bytes 2097153 | tf_op jit(solution)/shard_map/jit(_where)/select_n | solution.py:123
  119.3 1.0 copy-done.3
  121.1 1.0 copy-done.1
  122.1 15.0 %pair_contraction.1 = f32[2,256,256]{2,1,0:T(8,128)} custom-call(s32[2]{0:T(128)S(1)} %fusion.14.blocks, f32[2,2,256,256]{3,2,1,0:T(8,128)} %bitcast.15, bf16[512,512]{1,0:T(8,128)(2,1)S(1)} %copy-done.1, f32[2,4,64,256]{3,2,1,0:T(8,128)S(1)} %bitcast.11, f32[2,4,64,256]{3,2,1,0:T(8,128)S(1)} %broadcast_select_fusion.2.refs_1_, ...), custom_call_target="tpu_custom_call" | custom-call | tf_op jit(solution)/shard_map/pair_contraction/pallas_call | solution.py:234
  (64 shorter events, 6.3 us)
Async XLA Ops:
  0.6 20.5 %copy-start = (f32[2,128,1024]{2,1,0:T(8,128)S(1)}, f32[2,128,1024]{2,1,0:T(8,128)}, u32[]{:S(2)}) copy-start(f32[2,128,1024]{2,1,0:T(8,128)} %param.5) | copy-start | bytes 3145732
  15.4 2.1 %collective-permute-start = (f32[512,256]{1,0:T(8,128)S(1)}, f32[512,256]{1,0:T(8,128)S(1)}, u32[]{:S(2)}, u32[]{:S(2)}) collective-permute-start(f32[512,256]{1,0:T(8,128)S(1)} %constant_dynamic-slice_fusion.5), channel_id=1, source_target_pairs={{0,1},{1,0},{2,3},{3,2},{4,5},{5,4},{6,7},{7,6},{8,9},{9,8},{10,11... | collective-permute-start | bytes 1572872 | tf_op jit(solution)/shard_map/ppermute | solution.py:101
  18.2 9.8 %collective-permute-start.1 = (f32[256,256]{1,0:T(8,128)}, f32[256,256]{1,0:T(8,128)}, u32[]{:S(2)}, u32[]{:S(2)}) collective-permute-start(f32[256,256]{1,0:T(8,128)} %constant_dynamic-slice_fusion.4), channel_id=1, source_target_pairs={{0,2},{1,3},{2,0},{3,1},{4,6},{5,7},{6,4},{7,5},{8,10},{9,11},{10,... | collective-permute-start | bytes 786440 | tf_op jit(solution)/shard_map/ppermute | solution.py:101
  21.1 95.3 %copy-start.9 = (s32[32,2]{0,1:T(2,128)S(1)}, s32[32,2]{0,1:T(2,128)}, u32[]{:S(2)}) copy-start(s32[32,2]{0,1:T(2,128)} %param.7) | copy-start | bytes 772
  21.8 15.6 %collective-permute-start.9 = (f32[2,4,64,256]{3,2,1,0:T(8,128)S(1)}, f32[2,4,64,256]{3,2,1,0:T(8,128)S(1)}, u32[]{:S(2)}, u32[]{:S(2)}) collective-permute-start(f32[2,4,64,256]{3,2,1,0:T(8,128)S(1)} %bitcast.7), channel_id=1, source_target_pairs={{8,0},{12,4},{16,8},{20,12},{24,16},{28,20},{9,1},{13,5},{17,9},{2... | collective-permute-start | bytes 1572872 | tf_op jit(solution)/shard_map/ppermute | solution.py:106
  23.1 15.6 %collective-permute-start.8 = (f32[2,4,64,256]{3,2,1,0:T(8,128)S(1)}, f32[2,4,64,256]{3,2,1,0:T(8,128)S(1)}, u32[]{:S(2)}, u32[]{:S(2)}) collective-permute-start(f32[2,4,64,256]{3,2,1,0:T(8,128)S(1)} %bitcast.8), channel_id=1, source_target_pairs={{0,8},{4,12},{8,16},{12,20},{16,24},{20,28},{1,9},{5,13},{9,17},{1... | collective-permute-start | bytes 1572872 | tf_op jit(solution)/shard_map/ppermute | solution.py:106
  29.0 15.1 %collective-permute-start.2 = (f32[128,256]{1,0:T(8,128)S(1)}, f32[128,256]{1,0:T(8,128)S(1)}, u32[]{:S(2)}, u32[]{:S(2)}) collective-permute-start(f32[128,256]{1,0:T(8,128)S(1)} %constant_dynamic-slice_fusion.3), channel_id=1, source_target_pairs={{0,4},{4,0},{8,12},{12,8},{16,20},{20,16},{24,28},{28,24},{1,5},{5... | collective-permute-start | bytes 393224 | tf_op jit(solution)/shard_map/ppermute | solution.py:101
  30.8 36.8 %collective-permute-start.14 = (f32[2,4,64,256]{3,2,1,0:T(8,128)S(1)}, f32[2,4,64,256]{3,2,1,0:T(8,128)}, u32[]{:S(2)}, u32[]{:S(2)}) collective-permute-start(f32[2,4,64,256]{3,2,1,0:T(8,128)S(1)} %bitcast.9), channel_id=1, source_target_pairs={{0,4},{4,0},{8,12},{12,8},{16,20},{20,16},{24,28},{28,24},{1,5},{5... | collective-permute-start | bytes 1572872 | tf_op jit(solution)/shard_map/ppermute | solution.py:101
  37.4 44.2 %copy-start.6 = (f32[2,4,64,256]{3,2,1,0:T(8,128)}, f32[2,4,64,256]{3,2,1,0:T(8,128)S(1)}, u32[]{:S(2)}) copy-start(f32[2,4,64,256]{3,2,1,0:T(8,128)S(1)} %collective-permute-done.9) | copy-start | bytes 1572868
  37.4 28.8 %collective-permute-start.10 = (f32[2,4,64,256]{3,2,1,0:T(8,128)S(1)}, f32[2,4,64,256]{3,2,1,0:T(8,128)}, u32[]{:S(2)}, u32[]{:S(2)}) collective-permute-start(f32[2,4,64,256]{3,2,1,0:T(8,128)S(1)} %collective-permute-done.9), channel_id=1, source_target_pairs={{8,0},{12,4},{16,8},{20,12},{24,16},{28,20},{9,1},{13,5},{17,9},{2... | collective-permute-start | bytes 1572872 | tf_op jit(solution)/shard_map/ppermute | solution.py:106
  38.7 29.4 %collective-permute-start.12 = (f32[2,4,64,256]{3,2,1,0:T(8,128)S(1)}, f32[2,4,64,256]{3,2,1,0:T(8,128)}, u32[]{:S(2)}, u32[]{:S(2)}) collective-permute-start(f32[2,4,64,256]{3,2,1,0:T(8,128)S(1)} %collective-permute-done.8), channel_id=1, source_target_pairs={{0,8},{4,12},{8,16},{12,20},{16,24},{20,28},{1,9},{5,13},{9,17},{1... | collective-permute-start | bytes 1572872 | tf_op jit(solution)/shard_map/ppermute | solution.py:106
  44.1 12.1 %collective-permute-start.3 = (f32[128,256]{1,0:T(8,128)S(1)}, f32[128,256]{1,0:T(8,128)S(1)}, u32[]{:S(2)}, u32[]{:S(2)}) collective-permute-start(f32[128,256]{1,0:T(8,128)S(1)} %dynamic-slice_add_fusion.2), channel_id=1, source_target_pairs={{0,8},{4,12},{8,0},{12,4},{16,24},{20,28},{24,16},{28,20},{1,9},{5... | collective-permute-start | bytes 393224 | tf_op jit(solution)/shard_map/ppermute | solution.py:101
  56.2 8.4 %collective-permute-start.4 = (f32[128,256]{1,0:T(8,128)S(1)}, f32[128,256]{1,0:T(8,128)S(1)}, u32[]{:S(2)}, u32[]{:S(2)}) collective-permute-start(f32[128,256]{1,0:T(8,128)S(1)} %add.101), channel_id=1, source_target_pairs={{0,16},{4,20},{8,24},{12,28},{16,0},{20,4},{24,8},{28,12},{1,17},{... | collective-permute-start | bytes 393224 | tf_op jit(solution)/shard_map/ppermute | solution.py:101
  64.7 8.2 %collective-permute-start.5 = (f32[128,256]{1,0:T(8,128)S(1)}, f32[128,256]{1,0:T(8,128)S(1)}, u32[]{:S(2)}, u32[]{:S(2)}) collective-permute-start(f32[128,256]{1,0:T(8,128)S(1)} %add.102), channel_id=1, source_target_pairs={{0,4},{4,0},{8,12},{12,8},{16,20},{20,16},{24,28},{28,24},{1,5},{5... | collective-permute-start | bytes 393224 | tf_op jit(solution)/shard_map/ppermute | solution.py:101
  66.2 15.4 %collective-permute-start.11 = (f32[2,4,64,256]{3,2,1,0:T(8,128)}, f32[2,4,64,256]{3,2,1,0:T(8,128)}, u32[]{:S(2)}, u32[]{:S(2)}) collective-permute-start(f32[2,4,64,256]{3,2,1,0:T(8,128)} %collective-permute-done.10), channel_id=1, source_target_pairs={{8,0},{12,4},{16,8},{20,12},{24,16},{28,20},{9,1},{13,5},{17,9},{2... | collective-permute-start | bytes 1572872 | tf_op jit(solution)/shard_map/ppermute | solution.py:106
  67.5 18.0 %collective-permute-start.18 = (f32[2,4,64,256]{3,2,1,0:T(8,128)S(1)}, f32[2,4,64,256]{3,2,1,0:T(8,128)}, u32[]{:S(2)}, u32[]{:S(2)}) collective-permute-start(f32[2,4,64,256]{3,2,1,0:T(8,128)S(1)} %bitcast.10), channel_id=1, source_target_pairs={{0,1},{1,0},{2,3},{3,2},{4,5},{5,4},{6,7},{7,6},{8,9},{9,8},{10,11... | collective-permute-start | bytes 1572872 | tf_op jit(solution)/shard_map/ppermute | solution.py:101
  67.6 18.5 %collective-permute-start.22 = (f32[2,4,64,256]{3,2,1,0:T(8,128)}, f32[2,4,64,256]{3,2,1,0:T(8,128)S(1)}, u32[]{:S(2)}, u32[]{:S(2)}) collective-permute-start(f32[2,4,64,256]{3,2,1,0:T(8,128)} %collective-permute-done.14.refs_4_), channel_id=1, source_target_pairs={{0,1},{1,0},{2,3},{3,2},{4,5},{5,4},{6,7},{7,6},{8,9},{9,8},{10,11... | collective-permute-start | bytes 1572872 | tf_op jit(solution)/shard_map/ppermute | solution.py:101
  68.1 16.3 %collective-permute-start.13 = (f32[2,4,64,256]{3,2,1,0:T(8,128)}, f32[2,4,64,256]{3,2,1,0:T(8,128)S(1)}, u32[]{:S(2)}, u32[]{:S(2)}) collective-permute-start(f32[2,4,64,256]{3,2,1,0:T(8,128)} %collective-permute-done.12), channel_id=1, source_target_pairs={{0,8},{4,12},{8,16},{12,20},{16,24},{20,28},{1,9},{5,13},{9,17},{1... | collective-permute-start | bytes 1572872 | tf_op jit(solution)/shard_map/ppermute | solution.py:106
  72.9 8.1 %collective-permute-start.6 = (f32[256,256]{1,0:T(8,128)S(1)}, f32[256,256]{1,0:T(8,128)S(1)}, u32[]{:S(2)}, u32[]{:S(2)}) collective-permute-start(f32[256,256]{1,0:T(8,128)S(1)} %maximum_select_fusion.2), channel_id=1, source_target_pairs={{0,2},{1,3},{2,0},{3,1},{4,6},{5,7},{6,4},{7,5},{8,10},{9,11},{10,... | collective-permute-start | bytes 786440 | tf_op jit(solution)/shard_map/ppermute | solution.py:101
  81.0 15.0 %collective-permute-start.16 = (f32[2,4,64,256]{3,2,1,0:T(8,128)S(1)}, f32[2,4,64,256]{3,2,1,0:T(8,128)}, u32[]{:S(2)}, u32[]{:S(2)}) collective-permute-start(f32[2,4,64,256]{3,2,1,0:T(8,128)S(1)} %broadcast_select_fusion.1.refs_2_), channel_id=1, source_target_pairs={{0,4},{4,0},{8,12},{12,8},{16,20},{20,16},{24,28},{28,24},{1,5},{5... | collective-permute-start | bytes 1572872 | tf_op jit(solution)/shard_map/ppermute | solution.py:101
  81.6 34.8 %copy-start.4 = (f32[512,256]{1,0:T(8,128)}, f32[512,256]{1,0:T(8,128)S(1)}, u32[]{:S(2)}) copy-start(f32[512,256]{1,0:T(8,128)S(1)} %maximum_select_fusion.1) | copy-start | bytes 1572868
  81.6 14.4 %collective-permute-start.20 = (f32[2,4,64,256]{3,2,1,0:T(8,128)S(1)}, f32[2,4,64,256]{3,2,1,0:T(8,128)S(1)}, u32[]{:S(2)}, u32[]{:S(2)}) collective-permute-start(f32[2,4,64,256]{3,2,1,0:T(8,128)S(1)} %broadcast_select_fusion.1.refs_2_), channel_id=1, source_target_pairs={{0,1},{1,0},{2,3},{3,2},{4,5},{5,4},{6,7},{7,6},{8,9},{9,8},{10,11... | collective-permute-start | bytes 1572872 | tf_op jit(solution)/shard_map/ppermute | solution.py:101
  84.4 12.1 %collective-permute-start.7 = (f32[512,256]{1,0:T(8,128)S(1)}, f32[512,256]{1,0:T(8,128)S(1)}, u32[]{:S(2)}, u32[]{:S(2)}) collective-permute-start(f32[512,256]{1,0:T(8,128)S(1)} %maximum_select_fusion.1), channel_id=1, source_target_pairs={{0,1},{1,0},{2,3},{3,2},{4,5},{5,4},{6,7},{7,6},{8,9},{9,8},{10,11... | collective-permute-start | bytes 1572872 | tf_op jit(solution)/shard_map/ppermute | solution.py:101
  85.5 21.7 %collective-permute-start.15 = (f32[2,4,64,256]{3,2,1,0:T(8,128)S(1)}, f32[2,4,64,256]{3,2,1,0:T(8,128)}, u32[]{:S(2)}, u32[]{:S(2)}) collective-permute-start(f32[2,4,64,256]{3,2,1,0:T(8,128)S(1)} %broadcast_select_fusion.2.refs_1_), channel_id=1, source_target_pairs={{0,4},{4,0},{8,12},{12,8},{16,20},{20,16},{24,28},{28,24},{1,5},{5... | collective-permute-start | bytes 1572872 | tf_op jit(solution)/shard_map/ppermute | solution.py:101
  86.1 30.2 %copy-start.7 = (f32[2,4,64,256]{3,2,1,0:T(8,128)}, f32[2,4,64,256]{3,2,1,0:T(8,128)S(1)}, u32[]{:S(2)}) copy-start(f32[2,4,64,256]{3,2,1,0:T(8,128)S(1)} %collective-permute-done.22.refs_12_) | copy-start | bytes 1572868
  86.1 30.2 %collective-permute-start.17 = (f32[2,4,64,256]{3,2,1,0:T(8,128)S(1)}, f32[2,4,64,256]{3,2,1,0:T(8,128)}, u32[]{:S(2)}, u32[]{:S(2)}) collective-permute-start(f32[2,4,64,256]{3,2,1,0:T(8,128)S(1)} %broadcast_select_fusion.refs_3_), channel_id=1, source_target_pairs={{0,4},{4,0},{8,12},{12,8},{16,20},{20,16},{24,28},{28,24},{1,5},{5... | collective-permute-start | bytes 1572872 | tf_op jit(solution)/shard_map/ppermute | solution.py:101
  96.0 25.1 %collective-permute-start.19 = (f32[2,4,64,256]{3,2,1,0:T(8,128)S(1)}, f32[2,4,64,256]{3,2,1,0:T(8,128)}, u32[]{:S(2)}, u32[]{:S(2)}) collective-permute-start(f32[2,4,64,256]{3,2,1,0:T(8,128)S(1)} %broadcast_select_fusion.2.refs_1_), channel_id=1, source_target_pairs={{0,1},{1,0},{2,3},{3,2},{4,5},{5,4},{6,7},{7,6},{8,9},{9,8},{10,11... | collective-permute-start | bytes 1572872 | tf_op jit(solution)/shard_map/ppermute | solution.py:101
  96.0 20.4 %copy-start.8 = (f32[2,4,64,256]{3,2,1,0:T(8,128)}, f32[2,4,64,256]{3,2,1,0:T(8,128)S(1)}, u32[]{:S(2)}) copy-start(f32[2,4,64,256]{3,2,1,0:T(8,128)S(1)} %collective-permute-done.20.refs_10_) | copy-start | bytes 1572868
  96.0 25.1 %collective-permute-start.21 = (f32[2,4,64,256]{3,2,1,0:T(8,128)S(1)}, f32[2,4,64,256]{3,2,1,0:T(8,128)}, u32[]{:S(2)}, u32[]{:S(2)}) collective-permute-start(f32[2,4,64,256]{3,2,1,0:T(8,128)S(1)} %broadcast_select_fusion.refs_3_), channel_id=1, source_target_pairs={{0,1},{1,0},{2,3},{3,2},{4,5},{5,4},{6,7},{7,6},{8,9},{9,8},{10,11... | collective-permute-start | bytes 1572872 | tf_op jit(solution)/shard_map/ppermute | solution.py:101
  96.5 24.6 %collective-permute-start.24 = (f32[2,4,64,256]{3,2,1,0:T(8,128)}, f32[2,4,64,256]{3,2,1,0:T(8,128)}, u32[]{:S(2)}, u32[]{:S(2)}) collective-permute-start(f32[2,4,64,256]{3,2,1,0:T(8,128)} %collective-permute-done.16.refs_6_), channel_id=1, source_target_pairs={{0,1},{1,0},{2,3},{3,2},{4,5},{5,4},{6,7},{7,6},{8,9},{9,8},{10,11... | collective-permute-start | bytes 1572872 | tf_op jit(solution)/shard_map/ppermute | solution.py:101
  107.2 13.9 %collective-permute-start.23 = (f32[2,4,64,256]{3,2,1,0:T(8,128)}, f32[2,4,64,256]{3,2,1,0:T(8,128)}, u32[]{:S(2)}, u32[]{:S(2)}) collective-permute-start(f32[2,4,64,256]{3,2,1,0:T(8,128)} %collective-permute-done.15.refs_5_), channel_id=1, source_target_pairs={{0,1},{1,0},{2,3},{3,2},{4,5},{5,4},{6,7},{7,6},{8,9},{9,8},{10,11... | collective-permute-start | bytes 1572872 | tf_op jit(solution)/shard_map/ppermute | solution.py:101
  116.4 4.7 %collective-permute-start.25 = (f32[2,4,64,256]{3,2,1,0:T(8,128)}, f32[2,4,64,256]{3,2,1,0:T(8,128)}, u32[]{:S(2)}, u32[]{:S(2)}) collective-permute-start(f32[2,4,64,256]{3,2,1,0:T(8,128)} %collective-permute-done.17.refs_7_), channel_id=1, source_target_pairs={{0,1},{1,0},{2,3},{3,2},{4,5},{5,4},{6,7},{7,6},{8,9},{9,8},{10,11... | collective-permute-start | bytes 1572872 | tf_op jit(solution)/shard_map/ppermute | solution.py:101
  (4 other events, 22.7 us)

commit v2 on v1

v2 whole, which is shorter than its diff:
```python
import functools
import math

import jax
import jax.numpy as jnp
from jax import lax
from jax.experimental import pallas as pl
from jax.experimental.pallas import tpu as pltpu
from jax.sharding import PartitionSpec as P

LATTICE_EDGE = 64
LANES = 128
F32 = jnp.float32
BF16 = jnp.bfloat16
GRAM_VMEM = 56 * 1024 * 1024
PAIR_VMEM = 60 * 1024 * 1024


def bits_of(count):
    return range(count.bit_length() - 1)


def split(value):
    high = value.astype(BF16)
    return high, (value - high.astype(F32)).astype(BF16)


def dot_nt(left, right):
    return lax.dot_general(left, right, (((1,), (1,)), ((), ())), preferred_element_type=F32)


def product(left, right):
    return dot_nt(left[0], right[0]) + dot_nt(left[0], right[1]) + dot_nt(left[1], right[0])


def dot_tn(left, right):
    return lax.dot_general(left, right, (((0,), (0,)), ((), ())), preferred_element_type=F32)


def gram_kernel(momenta, vectors, *refs, width, norm):
    away, kept, held, arrived = refs[-4:]
    _, colours, _, sites = vectors.shape
    core = lax.rem(lax.axis_index("tile"), 2)
    first_site = (lax.axis_index("space") * lax.axis_size("tile") + lax.axis_index("tile")) * sites
    chunks = sites // width
    copies = []
    for colour in range(colours):
        for chunk in range(chunks):
            lanes = pl.ds(chunk * width, width)
            copies.append(
                pltpu.make_async_copy(
                    vectors.at[:, colour, :, lanes], held.at[:, colour, :, lanes], arrived.at[len(copies)]
                )
            )
    for copy in copies:
        copy.start()
    half = kept.shape[0]
    sums = []
    for total, first in ((kept, core * half), (away, (1 - core) * half)):
        for p in range(half):
            phases = []
            for chunk in range(chunks):
                site = first_site + chunk * width + lax.broadcasted_iota(jnp.int32, (1, width), 1)
                wave = (
                    momenta[first + p, 0] * (site % LATTICE_EDGE)
                    + momenta[first + p, 1] * (site // LATTICE_EDGE % LATTICE_EDGE)
                    + momenta[first + p, 2] * (site // (LATTICE_EDGE * LATTICE_EDGE))
                ) % LATTICE_EDGE
                theta = wave.astype(F32) * (2.0 * math.pi / LATTICE_EDGE)
                phases.append((jnp.cos(theta), jnp.sin(theta)))
            sums.append((total, p, phases))
    held_sums = {}
    for n, copy in enumerate(copies):
        copy.wait()
        chunk = n % chunks
        real = held[0, n // chunks, :, chunk * width : (chunk + 1) * width]
        imag = held[1, n // chunks, :, chunk * width : (chunk + 1) * width]
        left = split(real), split(imag), split(real - imag)
        for number, (_, _, phases) in enumerate(sums):
            cosine, sine = phases[chunk]
            phased_real = cosine * real + sine * imag
            phased_imag = cosine * imag - sine * real
            by_real = product(left[2], split(phased_real))
            from_real = product(left[0], split(phased_imag - phased_real))
            from_imag = product(left[1], split(phased_real + phased_imag))
            parts = by_real, from_real, from_imag
            held_sums[number] = parts if n == 0 else [old + new for old, new in zip(held_sums[number], parts)]
    for number, (total, p, _) in enumerate(sums):
        by_real, from_real, from_imag = held_sums[number]
        total[p, 0] = (by_real + from_imag) * norm
        total[p, 1] = (by_real + from_real) * norm


def local_gram(planes, momenta, norm, started):
    _, colours, count, sites = planes.shape
    half = momenta.shape[0] // 2
    width = min(sites, 512)
    return pl.pallas_call(
        functools.partial(gram_kernel, width=width, norm=norm),
        in_specs=[pl.BlockSpec(memory_space=pltpu.SMEM), pl.BlockSpec(memory_space=pltpu.HBM)]
        + [pl.BlockSpec(memory_space=pl.ANY)] * len(started),
        out_specs=[pl.BlockSpec(memory_space=pltpu.VMEM)] * 2,
        out_shape=[jax.ShapeDtypeStruct((half, 2, count, count), F32)] * 2,
        scratch_shapes=[
            pltpu.VMEM(planes.shape, F32),
            pltpu.SemaphoreType.DMA((colours * sites // width,)),
        ],
        compiler_params=pltpu.CompilerParams(vmem_limit_bytes=GRAM_VMEM),
        cost_estimate=pl.CostEstimate(
            flops=48 * half * count * count * colours * sites,
            bytes_accessed=8 * count * colours * sites,
            transcendentals=0,
        ),
        name="local_gram",
    )(momenta, planes, *started)


def after(value, others):
    if not others:
        return value
    anywhere = pl.BlockSpec(memory_space=pl.ANY)
    return pl.pallas_call(
        lambda *refs: None,
        in_specs=[anywhere] * (1 + len(others)),
        out_specs=anywhere,
        out_shape=jax.ShapeDtypeStruct(value.shape, value.dtype),
        input_output_aliases={0: 0},
        compiler_params=pltpu.CompilerParams(vmem_limit_bytes=1024 * 1024),
        name="after",
    )(value, *others)


def swap(value, axis, bit):
    size = lax.axis_size(axis)
    return lax.ppermute(value, axis, [(i, i ^ (1 << bit)) for i in range(size)])


def shift(value, axis, by):
    size = lax.axis_size(axis)
    return lax.ppermute(value, axis, [(i, i + by) for i in range(size) if 0 <= i + by < size])


def own_bit(axis, bit):
    return (lax.axis_index(axis) >> bit) & 1


def halve(value, axis, bit):
    mine = own_bit(axis, bit)
    half = value.shape[0] // 2
    away = lax.dynamic_slice_in_dim(value, (1 - mine) * half, half, 0)
    kept = lax.dynamic_slice_in_dim(value, mine * half, half, 0)
    return kept + swap(away, axis, bit)


def both(value, axis, bit):
    return value + swap(value, axis, bit)


def double(value, axis, bit):
    other = swap(value, axis, bit)
    return jnp.where(
        own_bit(axis, bit) == 0,
        jnp.concatenate([value, other]),
        jnp.concatenate([other, value]),
    )


def deal_kernel(tau, travel, rest, *, by_core, by_tile, tiles):
    parts, spin, _, count = travel.shape
    tile = lax.axis_index("tile")
    core = lax.rem(tile, 2)
    groups = [(pl.multiple_of(core * by_core, 8), by_core, travel, 0, pl.ds(0, by_core))]
    shared = 2 * by_core
    if by_tile:
        for n in range(tiles // 2):
            first = pl.multiple_of(shared + (2 * n + core) * by_tile, 8)
            groups.append((first, by_tile, rest, n * by_tile, None))
        first = pl.multiple_of(shared + tile * by_tile, 8)
        groups.append((first, by_tile, travel, by_core, None))
    rows = jnp.concatenate(
        [tau[part, pl.ds(first, depth), :] for part in range(parts) for first, depth, *_ in groups], axis=0
    )
    width = min(count, LANES)
    line = lax.broadcasted_iota(jnp.int32, (spin * width, spin * width), 0)
    lane = lax.broadcasted_iota(jnp.int32, (spin * width, spin * width), 1)
    order = (line == lane % width * spin + lane // width).astype(BF16)
    for block in range(count // width):
        value = rows[:, block * spin * width : (block + 1) * spin * width]
        high = value.astype(BF16)
        left = value - high.astype(F32)
        middle, low = split(left)
        moved = (
            jnp.dot(high, order, preferred_element_type=F32)
            + jnp.dot(middle, order, preferred_element_type=F32)
        ) + jnp.dot(low, order, preferred_element_type=F32)
        top = 0
        for part in range(parts):
            for _, depth, target, at, _ in groups:
                for a in range(spin):
                    target[part, a, at : at + depth, block * width : (block + 1) * width] = moved[
                        top : top + depth, a * width : (a + 1) * width
                    ]
                top += depth


def deal(part, spin, by_core, by_tile):
    parts, _, order = part.shape
    tiles = lax.axis_size("tile")
    shape = (parts, spin, by_core + by_tile, order // spin)
    rest = (parts, spin, max(tiles // 2 * by_tile, 8), order // spin)
    return pl.pallas_call(
        functools.partial(deal_kernel, by_core=by_core, by_tile=by_tile, tiles=tiles),
        in_specs=[pl.BlockSpec(memory_space=pltpu.VMEM)],
        out_specs=[pl.BlockSpec(memory_space=pltpu.VMEM)] * 2,
        out_shape=[jax.ShapeDtypeStruct(shape, F32), jax.ShapeDtypeStruct(rest, F32)],
        compiler_params=pltpu.CompilerParams(vmem_limit_bytes=GRAM_VMEM),
        name="deal",
    )(part)


def exchange_everything(part, gram):
    space_bits, tile_bits = bits_of(lax.axis_size("space")), bits_of(lax.axis_size("tile"))
    tile_count = lax.axis_size("tile")
    sources = part.shape[1]
    shared = sources // 4
    if (sources - shared) // tile_count % 8:
        shared = sources
    by_core, by_tile = shared // 2, (sources - shared) // tile_count
    mixed, rest = deal(part, 4, by_core, by_tile)
    pieces = [(mixed, by_core)]
    if by_tile:
        pieces.append((rest, rest.shape[2]))

    slots, rounds, spread = {0: mixed}, [], None
    for r in range(1, len(space_bits) + 2):
        arrived = []
        masks = [mask for mask in range(1, lax.axis_size("space")) if mask.bit_count() == r]
        for mask in masks:
            low = mask & -mask
            slots[mask] = swap(slots[mask ^ low], "space", low.bit_length() - 1)
            arrived.append(slots[mask])
        if spread is not None:
            for bit in tile_bits[1:]:
                arrived.append(swap(spread, "tile", bit))
                spread = jnp.concatenate([spread, arrived[-1]], axis=2)
        spread = None
        if masks and by_tile:
            spread = jnp.concatenate([slots[mask][:, :, by_core:] for mask in masks], axis=2)
        rounds.append(arrived)
        pieces += [(piece, piece.shape[2]) for piece in arrived]

    away, kept = gram([mixed])
    away = after(away.reshape(-1, kept.shape[-1]), rounds[0])
    rows = kept.reshape(-1, kept.shape[-1]) + swap(away, "tile", 0)
    steps = [(halve, "tile", b) for b in tile_bits[1:]]
    steps += [(halve, "space", b) for b in space_bits[:1]]
    steps += [(both, "space", b) for b in space_bits[1:]]
    middle = len(steps) - 2
    steps += [(double, axis, b) for step, axis, b in steps[::-1] if step is halve]
    ends = {middle: 1, middle + 2: 2, len(steps) - 1: 3}
    for n, (step, axis, bit) in enumerate(steps):
        rows = step(rows, axis, bit)
        if n in ends:
            rows = after(rows, rounds[ends[n]] if ends[n] < len(rounds) else [])
    return rows, swap(rows, "tile", 0), pieces


def pair_kernel(blocks, own, other, order, *refs, depths, scale):
    sources = refs[: len(depths)]
    away, kept, left, right, woven, tau, held, placing, arrived = refs[len(depths) :]
    _, spin, total, count = tau.shape
    outs = (away, kept)
    rows = left.shape[3] // 2
    tiles = count // rows
    half = own.shape[0]
    core = lax.rem(lax.axis_index("tile"), 2)
    gathered = [
        pltpu.make_async_copy(own, held.at[pl.ds(core * half, half)], arrived.at[len(depths)]),
        pltpu.make_async_copy(other, held.at[pl.ds((1 - core) * half, half)], arrived.at[len(depths) + 1]),
    ]
    copies, first = [], 0
    for n, depth in enumerate(depths):
        target = tau.at[:, :, pl.ds(first, depth)]
        copies.append(pltpu.make_async_copy(sources[n].at[:, :, pl.ds(0, depth)], target, arrived.at[n]))
        first += depth
    last = pltpu.make_async_copy(order, placing, arrived.at[len(depths) + 2])
    for copy in [*gathered, *copies, last]:
        copy.start()
    for copy in gathered:
        copy.wait()
    real_rows, imag_rows = [], []
    for side in range(4):
        block = blocks[side // 2, side % 2]
        p = block // tiles
        start = pl.multiple_of(block % tiles * rows, rows)
        real = held[p, 0, pl.ds(start, rows), :]
        imag = held[p, 1, pl.ds(start, rows), :]
        real_rows += [real, imag]
        imag_rows += [-imag, real]
    weights = split(
        jnp.concatenate([jnp.concatenate(real_rows, axis=0), jnp.concatenate(imag_rows, axis=0)], axis=1)
    )
    depth = min(total, 256)
    for n in range(total // depth):
        while copies and sum(depths[: len(depths) - len(copies)]) < (n + 1) * depth:
            copies.pop(0).wait()
        here = pl.ds(n * depth, depth)

        def mix(a, carry):
            given = jnp.concatenate([tau[0, a, here, :], tau[1, a, here, :]], axis=1)
            mixed = product(split(given), weights)
            for g in range(2):
                left[g, a, here, :] = mixed[:, 4 * g * rows : (4 * g + 2) * rows]
                right[g, a, here, :] = mixed[:, (4 * g + 2) * rows : (4 * g + 4) * rows]
            return carry

        lax.fori_loop(0, spin, mix, 0)
    last.wait()
    width = rows * spin
    for g, out in enumerate(outs):
        left_hi, left_lo = split(jnp.concatenate([left[g, a] for a in range(spin)], axis=1))
        right_hi, right_lo = split(jnp.concatenate([right[g, a] for a in range(spin)], axis=1))
        pair = (dot_tn(left_hi, right_hi) + dot_tn(left_hi, right_lo) + dot_tn(left_lo, right_hi)) * scale
        pair_hi, pair_lo = split(pair)
        placed = jnp.dot(pair_hi, placing[...], preferred_element_type=F32) + jnp.dot(
            pair_lo, placing[...], preferred_element_type=F32
        )
        for a in range(spin):
            top = placed[2 * a * rows : (2 * a + 1) * rows]
            low = placed[(2 * a + 1) * rows : (2 * a + 2) * rows]
            parts = top[:, :width] - low[:, width:], top[:, width:] + low[:, :width]
            for n, value in enumerate(parts):
                for c in range(width // LANES):
                    woven[n, c, pl.ds(a, rows, stride=spin), :] = value[:, c * LANES : (c + 1) * LANES]
        for n in range(2):
            for c in range(width // LANES):
                out[n, :, c * LANES : (c + 1) * LANES] = woven[n, c]


def lane_order(rows, spin):
    size = 2 * rows * spin
    lane = lax.iota(jnp.int32, size)
    a, part, i = lane // (2 * rows), lane // rows % 2, lane % rows
    target = part * rows * spin + i * spin + a
    return (target[:, None] == lane[None, :]).astype(BF16)


def pair_contraction(blocks, own, other, pieces, scale):
    half, _, count, _ = own.shape
    spin = pieces[0][0].shape[1]
    depths = [depth for _, depth in pieces]
    total = sum(depths)
    rows = count // lax.axis_size("tile")
    order = lane_order(rows, spin)
    mixed = pltpu.VMEM((2, spin, total, 2 * rows), F32)
    return pl.pallas_call(
        functools.partial(pair_kernel, depths=depths, scale=scale),
        in_specs=[pl.BlockSpec(memory_space=pltpu.SMEM)]
        + [pl.BlockSpec(memory_space=pltpu.HBM)] * (3 + len(pieces)),
        out_specs=[pl.BlockSpec(memory_space=pltpu.VMEM)] * 2,
        out_shape=[jax.ShapeDtypeStruct((2, rows * spin, rows * spin), F32)] * 2,
        scratch_shapes=[
            mixed,
            mixed,
            pltpu.VMEM((2, rows * spin // LANES, rows * spin, LANES), F32),
            pltpu.VMEM((2, spin, total, count), F32),
            pltpu.VMEM((2 * half, 2, count, count), F32),
            pltpu.VMEM(order.shape, BF16),
            pltpu.SemaphoreType.DMA((len(pieces) + 3,)),
        ],
        compiler_params=pltpu.CompilerParams(vmem_limit_bytes=PAIR_VMEM),
        name="pair_contraction",
    )(blocks, own, other, order, *[piece for piece, _ in pieces])


def per_device(eigenvectors, perambulator, momenta, graph_blocks):
    space_count = lax.axis_size("space")
    tile_count = lax.axis_size("tile")
    space_index = lax.axis_index("space")
    tile_index = lax.axis_index("tile")
    device = space_index * tile_count + tile_index
    _, count, colours, sites = eigenvectors.shape
    order = perambulator.shape[2]
    norm = 1.0 / math.sqrt(colours * sites * space_count * tile_count)
    planes = eigenvectors.transpose(0, 2, 1, 3)

    def gram(started):
        return local_gram(planes, momenta, norm, started)

    own, other, pieces = exchange_everything(perambulator, gram)
    half = momenta.shape[0] // 2
    own = own.reshape(half, 2, count, count)
    other = other.reshape(half, 2, count, count)
    rows, columns = count // tile_count, count // space_count
    start = (0, 0, tile_index * rows, space_index * columns)
    own_part = lax.dynamic_slice(own, start, (half, 2, rows, columns))
    other_part = lax.dynamic_slice(other, start, (half, 2, rows, columns))
    elementals = jnp.where(
        tile_index % 2 == 0,
        jnp.concatenate([own_part, other_part]),
        jnp.concatenate([other_part, own_part]),
    )
    scale = 1.0 / (count * math.sqrt(order))
    blocks = jnp.stack([graph_blocks[device ^ 1], graph_blocks[device]])
    away, kept = pair_contraction(blocks, own, other, pieces, scale)
    return elementals, (kept + swap(away, "tile", 0))[None]


def solution(mesh):
    in_specs = (P(None, None, None, ("space", "tile")), P(None, "space", None), P(), P())
    out_specs = (P(None, None, "tile", "space"), P(("space", "tile"), None, None, None))
    return jax.shard_map(
        per_device, mesh=mesh, in_specs=in_specs, out_specs=out_specs, check_vma=False
    )
```

time: 138 us -> 101 us (0.73)
  waiting for transfers between devices: 60.9 us -> 30.1 us
  starting transfers between devices: 33.8 us -> 25.6 us
  local copies, waits for them, and re-layouts: 5.3 us -> 9.1 us
  Pallas kernels: 28.9 us -> 27.1 us
    ppermute x20 -> x19, waiting for transfers between devices: 53.1 us -> 30.1 us  [swap(): return lax.ppermute(value, axis, [(i, i ^ 1 << bit) for i in range(size)])]
    ppermute x6 -> x0, starting transfers between devices: 18.5 us -> none  [shift(): lax.ppermute(value, axis, [(i, i + by) for i in range(size) if 0 <= i + b...]
    ppermute x20 -> x19, starting transfers between devices: 15.2 us -> 25.6 us  [swap(): return lax.ppermute(value, axis, [(i, i ^ 1 << bit) for i in range(size)])]
    ppermute x6 -> x0, waiting for transfers between devices: 7.8 us -> none  [shift(): lax.ppermute(value, axis, [(i, i + by) for i in range(size) if 0 <= i + b...]
    select_n x3 -> x1, other arithmetic: 3.45 us -> 0.02 us  [per_device(): jnp.where(tile_index % 2 == 0, jnp.concatenate([own_part, other_part]), j...]
    unnamed x21 -> x33, local copies, waits for them, and re-layouts: 3.51 us -> 5.45 us
    broadcast_in_dim x0 -> x1, other arithmetic: none -> 1.9 us  [per_device(): return (elementals, (kept + swap(away, 'tile', 0))[None])]
    pallas_call x2 -> x7, Pallas kernels: 28.9 us -> 27.1 us  [the longest x1 12.3 us: pair_contraction(): pl.pallas_call(functools.partial(pair_kernel, depths=depths, scale=scale)...]
  transfers between devices with their start and end apart: 26 -> 19, of which waited for: 10 -> 11; matrix products, arithmetic and copies ran while one was open for 6% -> 9% of each run, Pallas kernels for 0% -> 12%
where the time goes in v2:
time: 101 us; the launch traced here: 100 us
  waiting for transfers between devices  30.1 us (30%)
  Pallas kernels  27.1 us (27%)
  starting transfers between devices  25.6 us (25%)
  local copies, waits for them, and re-layouts  9.1 us (9%)
  other arithmetic  7.43 us (7%)
    ppermute x19, waiting for transfers between devices, swap(): return lax.ppermute(value, axis, [(i, i ^ 1 << bit) for i in range(size)])  30.1 us
    ppermute x19, starting transfers between devices, swap(): return lax.ppermute(value, axis, [(i, i ^ 1 << bit) for i in range(size)])  25.6 us
    pallas_call x1, Pallas kernels, pair_contraction(): pl.pallas_call(functools.partial(pair_kernel, depths=depths, scale=scale)...  12.3 us
    pallas_call x1, Pallas kernels, local_gram(): pl.pallas_call(functools.partial(gram_kernel, width=width, norm=norm), in...  12 us
    unnamed x33, local copies, waits for them, and re-layouts  5.45 us
    pallas_call x1, Pallas kernels, deal(): pl.pallas_call(functools.partial(deal_kernel, by_core=by_core, by_tile=by...  2.83 us
  transfers between devices with their start and end apart: 19, of which 11 were waited for; matrix products, arithmetic and copies ran while one was open for 9% of the time, Pallas kernels for 12%

profile of v2, /device:TPU:0, one launch (start us, length us, event | category | flops | bytes accessed | tf_op | source)
XLA Modules:
  0.0 100.1 jit_solution(14844487600725025086)
XLA Ops:
  0.6 2.8 %deal.1 = (f32[2,4,40,256]{3,2,1,0:T(8,128)}, f32[2,4,48,256]{3,2,1,0:T(8,128)}) custom-call(f32[2,128,1024]{2,1,0:T(8,128)} %tau.1), custom_call_target="tpu_custom_call" | custom-call | tf_op jit(solution)/shard_map/deal/pallas_call | solution.py:211
  3.5 4.1 %collective-permute-start.2 = (f32[2,4,40,256]{3,2,1,0:T(8,128)}, f32[2,4,40,256]{3,2,1,0:T(8,128)S(1)}, u32[]{:S(2)}, u32[]{:S(2)}) collective-permute-start(f32[2,4,40,256]{3,2,1,0:T(8,128)} %get-tuple-element.8.refs_0_), channel_id=1, source_target_pairs={{0,16},{4,20},{8,24},{12,28},{16,0},{20,4},{24,8},{28,12},{1,17},{... | collective-permute-start | bytes 983048 | tf_op jit(solution)/shard_map/ppermute | solution.py:135
  7.5 1.6 %collective-permute-start.1 = (f32[2,4,40,256]{3,2,1,0:T(8,128)}, f32[2,4,40,256]{3,2,1,0:T(8,128)S(1)}, u32[]{:S(2)}, u32[]{:S(2)}) collective-permute-start(f32[2,4,40,256]{3,2,1,0:T(8,128)} %get-tuple-element.8.refs_0_), channel_id=1, source_target_pairs={{0,8},{4,12},{8,0},{12,4},{16,24},{20,28},{24,16},{28,20},{1,9},{5... | collective-permute-start | bytes 983048 | tf_op jit(solution)/shard_map/ppermute | solution.py:135
  9.1 1.5 %collective-permute-start = (f32[2,4,40,256]{3,2,1,0:T(8,128)}, f32[2,4,40,256]{3,2,1,0:T(8,128)S(1)}, u32[]{:S(2)}, u32[]{:S(2)}) collective-permute-start(f32[2,4,40,256]{3,2,1,0:T(8,128)} %get-tuple-element.8.refs_0_), channel_id=1, source_target_pairs={{0,4},{4,0},{8,12},{12,8},{16,20},{20,16},{24,28},{28,24},{1,5},{5... | collective-permute-start | bytes 983048 | tf_op jit(solution)/shard_map/ppermute | solution.py:135
  10.6 12.0 %local_gram.1 = (f32[1,2,256,256]{3,2,1,0:T(8,128)}, f32[1,2,256,256]{3,2,1,0:T(8,128)}) custom-call(s32[2,3]{1,0:T(2,128)} %momenta.1, f32[2,3,256,1024]{3,2,1,0:T(8,128)} %bitcast.13, f32[2,4,40,256]{3,2,1,0:T(8,128)} %get-tuple-element.8.refs_0_), custom_call_target="tpu_custom_call" | custom-call | flops 9663676416 | bytes 6291456 | tf_op jit(solution)/shard_map/local_gram/pallas_call | solution.py:98
  22.7 1.3 %copy-done.11 = f32[1,2,256,256]{3,2,1,0:T(8,128)S(1)} copy-done((f32[1,2,256,256]{3,2,1,0:T(8,128)S(1)}, f32[1,2,256,256]{3,2,1,0:T(8,128)}, u32[]{:S(2)}) %copy-start.11) | copy-done | bytes 524312
  24.8 2.1 %collective-permute-done.3 = f32[512,256]{1,0:T(8,128)S(1)} collective-permute-done((f32[512,256]{1,0:T(8,128)}, f32[512,256]{1,0:T(8,128)S(1)}, u32[]{:S(2)}, u32[]{:S(2)}) %collective-permute-start.3) | collective-permute-done | bytes 524320 | tf_op jit(solution)/shard_map/ppermute | solution.py:135
  26.9 1.1 %bitcast_add_fusion = f32[512,256]{1,0:T(8,128)S(1)} fusion(f32[512,256]{1,0:T(8,128)S(1)} %collective-permute-done.3, f32[1,2,256,256]{3,2,1,0:T(8,128)} %get-tuple-element.9), kind=kLoop, calls=%fused_computation.5 | loop fusion | flops 131072 | bytes 1572864 | tf_op jit(solution)/shard_map/add | solution.py:254
  28.1 1.6 %collective-permute-start.4 = (f32[256,256]{1,0:T(8,128)S(1)}, f32[256,256]{1,0:T(8,128)}, u32[]{:S(2)}, u32[]{:S(2)}) collective-permute-start(f32[256,256]{1,0:T(8,128)S(1)} %constant_dynamic-slice_fusion.5), channel_id=1, source_target_pairs={{0,2},{1,3},{2,0},{3,1},{4,6},{5,7},{6,4},{7,5},{8,10},{9,11},{10,... | collective-permute-start | bytes 786440 | tf_op jit(solution)/shard_map/ppermute | solution.py:135
  31.1 1.5 %collective-permute-start.9 = (f32[2,4,40,256]{3,2,1,0:T(8,128)S(1)}, f32[2,4,40,256]{3,2,1,0:T(8,128)S(1)}, u32[]{:S(2)}, u32[]{:S(2)}) collective-permute-start(f32[2,4,40,256]{3,2,1,0:T(8,128)S(1)} %collective-permute-done.2.refs_3_.refs_4_), channel_id=1, source_target_pairs={{0,8},{4,12},{8,0},{12,4},{16,24},{20,28},{24,16},{28,20},{1,9},{5... | collective-permute-start | bytes 983048 | tf_op jit(solution)/shard_map/ppermute | solution.py:135
  32.6 1.5 %collective-permute-start.8 = (f32[2,4,40,256]{3,2,1,0:T(8,128)S(1)}, f32[2,4,40,256]{3,2,1,0:T(8,128)S(1)}, u32[]{:S(2)}, u32[]{:S(2)}) collective-permute-start(f32[2,4,40,256]{3,2,1,0:T(8,128)S(1)} %collective-permute-done.2.refs_3_.refs_4_), channel_id=1, source_target_pairs={{0,4},{4,0},{8,12},{12,8},{16,20},{20,16},{24,28},{28,24},{1,5},{5... | collective-permute-start | bytes 983048 | tf_op jit(solution)/shard_map/ppermute | solution.py:135
  34.6 2.8 %collective-permute-done.4 = f32[256,256]{1,0:T(8,128)} collective-permute-done((f32[256,256]{1,0:T(8,128)S(1)}, f32[256,256]{1,0:T(8,128)}, u32[]{:S(2)}, u32[]{:S(2)}) %collective-permute-start.4) | collective-permute-done | bytes 262176 | tf_op jit(solution)/shard_map/ppermute | solution.py:135
  37.4 1.0 dynamic-slice_add_fusion
  39.1 1.5 %collective-permute-start.5 = (f32[128,256]{1,0:T(8,128)}, f32[128,256]{1,0:T(8,128)S(1)}, u32[]{:S(2)}, u32[]{:S(2)}) collective-permute-start(f32[128,256]{1,0:T(8,128)} %constant_dynamic-slice_fusion.4), channel_id=1, source_target_pairs={{0,4},{4,0},{8,12},{12,8},{16,20},{20,16},{24,28},{28,24},{1,5},{5... | collective-permute-start | bytes 393224 | tf_op jit(solution)/shard_map/ppermute | solution.py:135
  40.6 2.6 %collective-permute-done.8.refs_2_.refs_6_ = f32[2,4,40,256]{3,2,1,0:T(8,128)S(1)} collective-permute-done((f32[2,4,40,256]{3,2,1,0:T(8,128)S(1)}, f32[2,4,40,256]{3,2,1,0:T(8,128)S(1)}, u32[]{:S(2)}, u32[]{:S(2)}) %collective-permute-start.8) | collective-permute-done | bytes 327712 | tf_op jit(solution)/shard_map/ppermute | solution.py:135
  43.3 6.7 %collective-permute-done.7.refs_1_.refs_5_ = f32[2,4,40,256]{3,2,1,0:T(8,128)S(1)} collective-permute-done((f32[2,4,40,256]{3,2,1,0:T(8,128)S(1)}, f32[2,4,40,256]{3,2,1,0:T(8,128)S(1)}, u32[]{:S(2)}, u32[]{:S(2)}) %collective-permute-start.7) | collective-permute-done | bytes 327712 | tf_op jit(solution)/shard_map/ppermute | solution.py:135
  51.6 1.5 %collective-permute-start.14 = (f32[2,4,72,256]{3,2,1,0:T(8,128)}, f32[2,4,72,256]{3,2,1,0:T(8,128)S(1)}, u32[]{:S(2)}, u32[]{:S(2)}) collective-permute-start(f32[2,4,72,256]{3,2,1,0:T(8,128)} %pad_maximum_fusion.1), channel_id=1, source_target_pairs={{0,2},{1,3},{2,0},{3,1},{4,6},{5,7},{6,4},{7,5},{8,10},{9,11},{10,... | collective-permute-start | bytes 1769480 | tf_op jit(solution)/shard_map/ppermute | solution.py:135
  53.8 4.4 %collective-permute-done.6 = f32[128,256]{1,0:T(8,128)S(1)} collective-permute-done((f32[128,256]{1,0:T(8,128)S(1)}, f32[128,256]{1,0:T(8,128)S(1)}, u32[]{:S(2)}, u32[]{:S(2)}) %collective-permute-start.6) | collective-permute-done | bytes 131104 | tf_op jit(solution)/shard_map/ppermute | solution.py:135
  58.2 1.0 copy-done.9
  59.2 3.4 %collective-permute-start.11 = (f32[128,256]{1,0:T(8,128)S(1)}, f32[128,256]{1,0:T(8,128)S(1)}, u32[]{:S(2)}, u32[]{:S(2)}) collective-permute-start(f32[128,256]{1,0:T(8,128)S(1)} %after.5), channel_id=1, source_target_pairs={{0,16},{4,20},{8,24},{12,28},{16,0},{20,4},{24,8},{28,12},{1,17},{... | collective-permute-start | bytes 393224 | tf_op jit(solution)/shard_map/ppermute | solution.py:135
  62.6 1.5 %collective-permute-start.13 = (f32[2,4,40,256]{3,2,1,0:T(8,128)S(1)}, f32[2,4,40,256]{3,2,1,0:T(8,128)}, u32[]{:S(2)}, u32[]{:S(2)}) collective-permute-start(f32[2,4,40,256]{3,2,1,0:T(8,128)S(1)} %collective-permute-done.9.refs_3_.refs_7_), channel_id=1, source_target_pairs={{0,4},{4,0},{8,12},{12,8},{16,20},{20,16},{24,28},{28,24},{1,5},{5... | collective-permute-start | bytes 983048 | tf_op jit(solution)/shard_map/ppermute | solution.py:135
  64.1 2.4 %collective-permute-done.11 = f32[128,256]{1,0:T(8,128)S(1)} collective-permute-done((f32[128,256]{1,0:T(8,128)S(1)}, f32[128,256]{1,0:T(8,128)S(1)}, u32[]{:S(2)}, u32[]{:S(2)}) %collective-permute-start.11) | collective-permute-done | bytes 131104 | tf_op jit(solution)/shard_map/ppermute | solution.py:135
  66.5 1.6 %collective-permute-start.12 = (f32[128,256]{1,0:T(8,128)S(1)}, f32[128,256]{1,0:T(8,128)S(1)}, u32[]{:S(2)}, u32[]{:S(2)}) collective-permute-start(f32[128,256]{1,0:T(8,128)S(1)} %add.102), channel_id=1, source_target_pairs={{0,4},{4,0},{8,12},{12,8},{16,20},{20,16},{24,28},{28,24},{1,5},{5... | collective-permute-start | bytes 393224 | tf_op jit(solution)/shard_map/ppermute | solution.py:135
  68.0 3.5 %collective-permute-done.12 = f32[128,256]{1,0:T(8,128)S(1)} collective-permute-done((f32[128,256]{1,0:T(8,128)S(1)}, f32[128,256]{1,0:T(8,128)S(1)}, u32[]{:S(2)}, u32[]{:S(2)}) %collective-permute-start.12) | collective-permute-done | bytes 131104 | tf_op jit(solution)/shard_map/ppermute | solution.py:135
  72.1 0.9 slice.34
  73.0 1.6 %collective-permute-start.16 = (f32[2,4,24,256]{3,2,1,0:T(8,128)S(1)}, f32[2,4,24,256]{3,2,1,0:T(8,128)S(1)}, u32[]{:S(2)}, u32[]{:S(2)}) collective-permute-start(f32[2,4,24,256]{3,2,1,0:T(8,128)S(1)} %slice.34), channel_id=1, source_target_pairs={{0,2},{1,3},{2,0},{3,1},{4,6},{5,7},{6,4},{7,5},{8,10},{9,11},{10,... | collective-permute-start | bytes 589832 | tf_op jit(solution)/shard_map/ppermute | solution.py:135
  74.7 3.3 %collective-permute-done.15 = f32[256,256]{1,0:T(8,128)S(1)} collective-permute-done((f32[256,256]{1,0:T(8,128)S(1)}, f32[256,256]{1,0:T(8,128)S(1)}, u32[]{:S(2)}, u32[]{:S(2)}) %collective-permute-start.15) | collective-permute-done | bytes 262176 | tf_op jit(solution)/shard_map/ppermute | solution.py:135
  78.1 2.1 %collective-permute-done.16.refs_1_.refs_11_ = f32[2,4,24,256]{3,2,1,0:T(8,128)S(1)} collective-permute-done((f32[2,4,24,256]{3,2,1,0:T(8,128)S(1)}, f32[2,4,24,256]{3,2,1,0:T(8,128)S(1)}, u32[]{:S(2)}, u32[]{:S(2)}) %collective-permute-start.16) | collective-permute-done | bytes 196640 | tf_op jit(solution)/shard_map/ppermute | solution.py:135
  81.0 1.0 fusion.order
  82.8 12.3 %pair_contraction.1 = (f32[2,256,256]{2,1,0:T(8,128)}, f32[2,256,256]{2,1,0:T(8,128)}) custom-call(s32[2,2]{1,0:T(2,128)} %pad_add_fusion.blocks, f32[1,2,256,256]{3,2,1,0:T(8,128)} %bitcast.8, f32[1,2,256,256]{3,2,1,0:T(8,128)} %bitcast.11, bf16[512,512]{1,0:T(8,128)(2,1)} %fusion.order, f32[2,4,40,256]{3,2,1,0:T(8,128)} %get-tuple-element.8.refs_0_, ...), custom_call_target="tpu_custom_call" | custom-call | tf_op jit(solution)/shard_map/pair_contraction/pallas_call | solution.py:356
  96.6 0.9 constant_dynamic-slice_fusion.2
  98.2 1.9 %add_bitcast_fusion = f32[1,2,256,256]{3,2,1,0:T(8,128)} fusion(f32[2,256,256]{2,1,0:T(8,128)} %get-tuple-element.12, f32[2,256,256]{2,1,0:T(8,128)S(1)} %collective-permute-done.18), kind=kLoop, calls=%fused_computation.6 | loop fusion | flops 131072 | bytes 1572864 | tf_op jit(solution)/shard_map/broadcast_in_dim | solution.py:406
  (72 shorter events, 10.3 us)
Async XLA Ops:
  3.5 19.1 %collective-permute-start.2 = (f32[2,4,40,256]{3,2,1,0:T(8,128)}, f32[2,4,40,256]{3,2,1,0:T(8,128)S(1)}, u32[]{:S(2)}, u32[]{:S(2)}) collective-permute-start(f32[2,4,40,256]{3,2,1,0:T(8,128)} %get-tuple-element.8.refs_0_), channel_id=1, source_target_pairs={{0,16},{4,20},{8,24},{12,28},{16,0},{20,4},{24,8},{28,12},{1,17},{... | collective-permute-start | bytes 983048 | tf_op jit(solution)/shard_map/ppermute | solution.py:135
  7.5 15.2 %collective-permute-start.1 = (f32[2,4,40,256]{3,2,1,0:T(8,128)}, f32[2,4,40,256]{3,2,1,0:T(8,128)S(1)}, u32[]{:S(2)}, u32[]{:S(2)}) collective-permute-start(f32[2,4,40,256]{3,2,1,0:T(8,128)} %get-tuple-element.8.refs_0_), channel_id=1, source_target_pairs={{0,8},{4,12},{8,0},{12,4},{16,24},{20,28},{24,16},{28,20},{1,9},{5... | collective-permute-start | bytes 983048 | tf_op jit(solution)/shard_map/ppermute | solution.py:135
  9.1 13.7 %collective-permute-start = (f32[2,4,40,256]{3,2,1,0:T(8,128)}, f32[2,4,40,256]{3,2,1,0:T(8,128)S(1)}, u32[]{:S(2)}, u32[]{:S(2)}) collective-permute-start(f32[2,4,40,256]{3,2,1,0:T(8,128)} %get-tuple-element.8.refs_0_), channel_id=1, source_target_pairs={{0,4},{4,0},{8,12},{12,8},{16,20},{20,16},{24,28},{28,24},{1,5},{5... | collective-permute-start | bytes 983048 | tf_op jit(solution)/shard_map/ppermute | solution.py:135
  22.6 43.9 %copy-start.3 = (f32[2,4,40,256]{3,2,1,0:T(8,128)}, f32[2,4,40,256]{3,2,1,0:T(8,128)S(1)}, u32[]{:S(2)}) copy-start(f32[2,4,40,256]{3,2,1,0:T(8,128)S(1)} %collective-permute-done.2.refs_3_.refs_4_) | copy-start | bytes 983044
  22.7 43.7 %copy-start.4 = (f32[2,4,40,256]{3,2,1,0:T(8,128)}, f32[2,4,40,256]{3,2,1,0:T(8,128)S(1)}, u32[]{:S(2)}) copy-start(f32[2,4,40,256]{3,2,1,0:T(8,128)S(1)} %collective-permute-done.1.refs_2_.refs_3_) | copy-start | bytes 983044
  22.7 43.8 %copy-start.5 = (f32[2,4,40,256]{3,2,1,0:T(8,128)}, f32[2,4,40,256]{3,2,1,0:T(8,128)S(1)}, u32[]{:S(2)}) copy-start(f32[2,4,40,256]{3,2,1,0:T(8,128)S(1)} %collective-permute-done.refs_1_.refs_2_) | copy-start | bytes 983044
  22.7 1.3 %copy-start.11 = (f32[1,2,256,256]{3,2,1,0:T(8,128)S(1)}, f32[1,2,256,256]{3,2,1,0:T(8,128)}, u32[]{:S(2)}) copy-start(f32[1,2,256,256]{3,2,1,0:T(8,128)} %get-tuple-element.10) | copy-start | bytes 1572868
  24.8 2.1 %collective-permute-start.3 = (f32[512,256]{1,0:T(8,128)}, f32[512,256]{1,0:T(8,128)S(1)}, u32[]{:S(2)}, u32[]{:S(2)}) collective-permute-start(f32[512,256]{1,0:T(8,128)} %copy-done.12), channel_id=1, source_target_pairs={{0,1},{1,0},{2,3},{3,2},{4,5},{5,4},{6,7},{7,6},{8,9},{9,8},{10,11... | collective-permute-start | bytes 1572872 | tf_op jit(solution)/shard_map/ppermute | solution.py:135
  28.1 9.3 %collective-permute-start.4 = (f32[256,256]{1,0:T(8,128)S(1)}, f32[256,256]{1,0:T(8,128)}, u32[]{:S(2)}, u32[]{:S(2)}) collective-permute-start(f32[256,256]{1,0:T(8,128)S(1)} %constant_dynamic-slice_fusion.5), channel_id=1, source_target_pairs={{0,2},{1,3},{2,0},{3,1},{4,6},{5,7},{6,4},{7,5},{8,10},{9,11},{10,... | collective-permute-start | bytes 786440 | tf_op jit(solution)/shard_map/ppermute | solution.py:135
  29.8 50.4 %copy-start.14 = (s32[32,2]{0,1:T(2,128)S(1)}, s32[32,2]{0,1:T(2,128)}, u32[]{:S(2)}) copy-start(s32[32,2]{0,1:T(2,128)} %param.7) | copy-start | bytes 772
  30.7 27.5 %collective-permute-start.10 = (f32[2,4,72,256]{3,2,1,0:T(8,128)}, f32[2,4,72,256]{3,2,1,0:T(8,128)S(1)}, u32[]{:S(2)}, u32[]{:S(2)}) collective-permute-start(f32[2,4,72,256]{3,2,1,0:T(8,128)} %pad_maximum_fusion), channel_id=1, source_target_pairs={{0,2},{1,3},{2,0},{3,1},{4,6},{5,7},{6,4},{7,5},{8,10},{9,11},{10,... | collective-permute-start | bytes 1769480 | tf_op jit(solution)/shard_map/ppermute | solution.py:135
  31.1 9.5 %collective-permute-start.9 = (f32[2,4,40,256]{3,2,1,0:T(8,128)S(1)}, f32[2,4,40,256]{3,2,1,0:T(8,128)S(1)}, u32[]{:S(2)}, u32[]{:S(2)}) collective-permute-start(f32[2,4,40,256]{3,2,1,0:T(8,128)S(1)} %collective-permute-done.2.refs_3_.refs_4_), channel_id=1, source_target_pairs={{0,8},{4,12},{8,0},{12,4},{16,24},{20,28},{24,16},{28,20},{1,9},{5... | collective-permute-start | bytes 983048 | tf_op jit(solution)/shard_map/ppermute | solution.py:135
  32.6 10.7 %collective-permute-start.8 = (f32[2,4,40,256]{3,2,1,0:T(8,128)S(1)}, f32[2,4,40,256]{3,2,1,0:T(8,128)S(1)}, u32[]{:S(2)}, u32[]{:S(2)}) collective-permute-start(f32[2,4,40,256]{3,2,1,0:T(8,128)S(1)} %collective-permute-done.2.refs_3_.refs_4_), channel_id=1, source_target_pairs={{0,4},{4,0},{8,12},{12,8},{16,20},{20,16},{24,28},{28,24},{1,5},{5... | collective-permute-start | bytes 983048 | tf_op jit(solution)/shard_map/ppermute | solution.py:135
  34.1 15.8 %collective-permute-start.7 = (f32[2,4,40,256]{3,2,1,0:T(8,128)S(1)}, f32[2,4,40,256]{3,2,1,0:T(8,128)S(1)}, u32[]{:S(2)}, u32[]{:S(2)}) collective-permute-start(f32[2,4,40,256]{3,2,1,0:T(8,128)S(1)} %collective-permute-done.1.refs_2_.refs_3_), channel_id=1, source_target_pairs={{0,4},{4,0},{8,12},{12,8},{16,20},{20,16},{24,28},{28,24},{1,5},{5... | collective-permute-start | bytes 983048 | tf_op jit(solution)/shard_map/ppermute | solution.py:135
  39.1 14.0 %collective-permute-start.5 = (f32[128,256]{1,0:T(8,128)}, f32[128,256]{1,0:T(8,128)S(1)}, u32[]{:S(2)}, u32[]{:S(2)}) collective-permute-start(f32[128,256]{1,0:T(8,128)} %constant_dynamic-slice_fusion.4), channel_id=1, source_target_pairs={{0,4},{4,0},{8,12},{12,8},{16,20},{20,16},{24,28},{28,24},{1,5},{5... | collective-permute-start | bytes 393224 | tf_op jit(solution)/shard_map/ppermute | solution.py:135
  40.6 41.5 %copy-start.6 = (f32[2,4,40,256]{3,2,1,0:T(8,128)}, f32[2,4,40,256]{3,2,1,0:T(8,128)S(1)}, u32[]{:S(2)}) copy-start(f32[2,4,40,256]{3,2,1,0:T(8,128)S(1)} %collective-permute-done.9.refs_3_.refs_7_) | copy-start | bytes 983044
  43.2 31.4 %copy-start.7 = (f32[2,4,40,256]{3,2,1,0:T(8,128)}, f32[2,4,40,256]{3,2,1,0:T(8,128)S(1)}, u32[]{:S(2)}) copy-start(f32[2,4,40,256]{3,2,1,0:T(8,128)S(1)} %collective-permute-done.8.refs_2_.refs_6_) | copy-start | bytes 983044
  51.6 20.0 %collective-permute-start.14 = (f32[2,4,72,256]{3,2,1,0:T(8,128)}, f32[2,4,72,256]{3,2,1,0:T(8,128)S(1)}, u32[]{:S(2)}, u32[]{:S(2)}) collective-permute-start(f32[2,4,72,256]{3,2,1,0:T(8,128)} %pad_maximum_fusion.1), channel_id=1, source_target_pairs={{0,2},{1,3},{2,0},{3,1},{4,6},{5,7},{6,4},{7,5},{8,10},{9,11},{10,... | collective-permute-start | bytes 1769480 | tf_op jit(solution)/shard_map/ppermute | solution.py:135
  53.1 5.0 %collective-permute-start.6 = (f32[128,256]{1,0:T(8,128)S(1)}, f32[128,256]{1,0:T(8,128)S(1)}, u32[]{:S(2)}, u32[]{:S(2)}) collective-permute-start(f32[128,256]{1,0:T(8,128)S(1)} %dynamic-slice_add_fusion.1), channel_id=1, source_target_pairs={{0,8},{4,12},{8,0},{12,4},{16,24},{20,28},{24,16},{28,20},{1,9},{5... | collective-permute-start | bytes 393224 | tf_op jit(solution)/shard_map/ppermute | solution.py:135
  58.2 1.0 copy-start.9
  59.2 22.9 %copy-start.1 = (f32[2,4,72,256]{3,2,1,0:T(8,128)}, f32[2,4,72,256]{3,2,1,0:T(8,128)S(1)}, u32[]{:S(2)}) copy-start(f32[2,4,72,256]{3,2,1,0:T(8,128)S(1)} %collective-permute-done.10.refs_4_.refs_8_) | copy-start | bytes 1769476
  59.2 7.3 %collective-permute-start.11 = (f32[128,256]{1,0:T(8,128)S(1)}, f32[128,256]{1,0:T(8,128)S(1)}, u32[]{:S(2)}, u32[]{:S(2)}) collective-permute-start(f32[128,256]{1,0:T(8,128)S(1)} %after.5), channel_id=1, source_target_pairs={{0,16},{4,20},{8,24},{12,28},{16,0},{20,4},{24,8},{28,12},{1,17},{... | collective-permute-start | bytes 393224 | tf_op jit(solution)/shard_map/ppermute | solution.py:135
  62.6 9.0 %collective-permute-start.13 = (f32[2,4,40,256]{3,2,1,0:T(8,128)S(1)}, f32[2,4,40,256]{3,2,1,0:T(8,128)}, u32[]{:S(2)}, u32[]{:S(2)}) collective-permute-start(f32[2,4,40,256]{3,2,1,0:T(8,128)S(1)} %collective-permute-done.9.refs_3_.refs_7_), channel_id=1, source_target_pairs={{0,4},{4,0},{8,12},{12,8},{16,20},{20,16},{24,28},{28,24},{1,5},{5... | collective-permute-start | bytes 983048 | tf_op jit(solution)/shard_map/ppermute | solution.py:135
  66.5 5.0 %collective-permute-start.12 = (f32[128,256]{1,0:T(8,128)S(1)}, f32[128,256]{1,0:T(8,128)S(1)}, u32[]{:S(2)}, u32[]{:S(2)}) collective-permute-start(f32[128,256]{1,0:T(8,128)S(1)} %add.102), channel_id=1, source_target_pairs={{0,4},{4,0},{8,12},{12,8},{16,20},{20,16},{24,28},{28,24},{1,5},{5... | collective-permute-start | bytes 393224 | tf_op jit(solution)/shard_map/ppermute | solution.py:135
  71.6 10.5 %copy-start.2 = (f32[2,4,72,256]{3,2,1,0:T(8,128)}, f32[2,4,72,256]{3,2,1,0:T(8,128)S(1)}, u32[]{:S(2)}) copy-start(f32[2,4,72,256]{3,2,1,0:T(8,128)S(1)} %collective-permute-done.14.refs_2_.refs_10_) | copy-start | bytes 1769476
  71.6 6.4 %collective-permute-start.15 = (f32[256,256]{1,0:T(8,128)S(1)}, f32[256,256]{1,0:T(8,128)S(1)}, u32[]{:S(2)}, u32[]{:S(2)}) collective-permute-start(f32[256,256]{1,0:T(8,128)S(1)} %after.6), channel_id=1, source_target_pairs={{0,2},{1,3},{2,0},{3,1},{4,6},{5,7},{6,4},{7,5},{8,10},{9,11},{10,... | collective-permute-start | bytes 786440 | tf_op jit(solution)/shard_map/ppermute | solution.py:135
  73.0 7.1 %collective-permute-start.16 = (f32[2,4,24,256]{3,2,1,0:T(8,128)S(1)}, f32[2,4,24,256]{3,2,1,0:T(8,128)S(1)}, u32[]{:S(2)}, u32[]{:S(2)}) collective-permute-start(f32[2,4,24,256]{3,2,1,0:T(8,128)S(1)} %slice.34), channel_id=1, source_target_pairs={{0,2},{1,3},{2,0},{3,1},{4,6},{5,7},{6,4},{7,5},{8,10},{9,11},{10,... | collective-permute-start | bytes 589832 | tf_op jit(solution)/shard_map/ppermute | solution.py:135
  80.1 1.9 %copy-start.10 = (f32[2,4,24,256]{3,2,1,0:T(8,128)}, f32[2,4,24,256]{3,2,1,0:T(8,128)S(1)}, u32[]{:S(2)}) copy-start(f32[2,4,24,256]{3,2,1,0:T(8,128)S(1)} %collective-permute-done.16.refs_1_.refs_11_) | copy-start | bytes 589828
  80.1 1.9 %copy-start = (f32[512,256]{1,0:T(8,128)}, f32[512,256]{1,0:T(8,128)S(1)}, u32[]{:S(2)}) copy-start(f32[512,256]{1,0:T(8,128)S(1)} %after.7) | copy-start | bytes 1572868
  80.1 1.9 %collective-permute-start.17 = (f32[512,256]{1,0:T(8,128)S(1)}, f32[512,256]{1,0:T(8,128)S(1)}, u32[]{:S(2)}, u32[]{:S(2)}) collective-permute-start(f32[512,256]{1,0:T(8,128)S(1)} %after.7), channel_id=1, source_target_pairs={{0,1},{1,0},{2,3},{3,2},{4,5},{5,4},{6,7},{7,6},{8,9},{9,8},{10,11... | collective-permute-start | bytes 1572872 | tf_op jit(solution)/shard_map/ppermute | solution.py:135
  82.1 0.8 copy-start.13
  95.1 3.1 %collective-permute-start.18 = (f32[2,256,256]{2,1,0:T(8,128)}, f32[2,256,256]{2,1,0:T(8,128)S(1)}, u32[]{:S(2)}, u32[]{:S(2)}) collective-permute-start(f32[2,256,256]{2,1,0:T(8,128)} %get-tuple-element.13), channel_id=1, source_target_pairs={{0,1},{1,0},{2,3},{3,2},{4,5},{5,4},{6,7},{7,6},{8,9},{9,8},{10,11... | collective-permute-start | bytes 1572872 | tf_op jit(solution)/shard_map/ppermute | solution.py:135
  (2 other events, 1.5 us)

commit v3 on v2

--- a/solution.py
+++ b/solution.py
@@ -12,8 +12,10 @@
 LANES = 128
 F32 = jnp.float32
 BF16 = jnp.bfloat16
-GRAM_VMEM = 56 * 1024 * 1024
-PAIR_VMEM = 60 * 1024 * 1024
+WAVE_ENDS = (-2, 0)
+PASS_ENDS = (-1, 1, 2)
+GRAM_VMEM = 55 * 1024 * 1024
+PAIR_VMEM = 58 * 1024 * 1024
 
 
 def bits_of(count):
@@ -115,19 +117,17 @@
     )(momenta, planes, *started)
 
 
-def after(value, others):
-    if not others:
-        return value
+def together(*values):
     anywhere = pl.BlockSpec(memory_space=pl.ANY)
     return pl.pallas_call(
         lambda *refs: None,
-        in_specs=[anywhere] * (1 + len(others)),
-        out_specs=anywhere,
-        out_shape=jax.ShapeDtypeStruct(value.shape, value.dtype),
-        input_output_aliases={0: 0},
+        in_specs=[anywhere] * len(values),
+        out_specs=[anywhere] * len(values),
+        out_shape=[jax.ShapeDtypeStruct(value.shape, value.dtype) for value in values],
+        input_output_aliases={n: n for n in range(len(values))},
         compiler_params=pltpu.CompilerParams(vmem_limit_bytes=1024 * 1024),
-        name="after",
-    )(value, *others)
+        name="together",
+    )(*values)
 
 
 def swap(value, axis, bit):
@@ -165,42 +165,57 @@
     )
 
 
-def deal_kernel(tau, travel, rest, *, by_core, by_tile, tiles):
+def deal_kernel(tau, travel, rest, fetched, arrived, *, by_core, by_tile, tiles):
     parts, spin, _, count = travel.shape
     tile = lax.axis_index("tile")
     core = lax.rem(tile, 2)
-    groups = [(pl.multiple_of(core * by_core, 8), by_core, travel, 0, pl.ds(0, by_core))]
+    groups = [(pl.multiple_of(core * by_core, 8), by_core, travel, 0)]
     shared = 2 * by_core
     if by_tile:
         for n in range(tiles // 2):
             first = pl.multiple_of(shared + (2 * n + core) * by_tile, 8)
-            groups.append((first, by_tile, rest, n * by_tile, None))
-        first = pl.multiple_of(shared + tile * by_tile, 8)
-        groups.append((first, by_tile, travel, by_core, None))
-    rows = jnp.concatenate(
-        [tau[part, pl.ds(first, depth), :] for part in range(parts) for first, depth, *_ in groups], axis=0
-    )
+            groups.append((first, by_tile, rest, n * by_tile))
+    copies, top = [], 0
+    for part in range(parts):
+        for first, depth, *_ in groups:
+            copies.append(
+                pltpu.make_async_copy(
+                    tau.at[part, pl.ds(first, depth)], fetched.at[pl.ds(top, depth)], arrived.at[len(copies)]
+                )
+            )
+            top += depth
+    for copy in copies:
+        copy.start()
+    for copy in copies:
+        copy.wait()
+    rows = fetched[...]
     width = min(count, LANES)
     line = lax.broadcasted_iota(jnp.int32, (spin * width, spin * width), 0)
     lane = lax.broadcasted_iota(jnp.int32, (spin * width, spin * width), 1)
     order = (line == lane % width * spin + lane // width).astype(BF16)
-    for block in range(count // width):
-        value = rows[:, block * spin * width : (block + 1) * spin * width]
-        high = value.astype(BF16)
-        left = value - high.astype(F32)
-        middle, low = split(left)
-        moved = (
-            jnp.dot(high, order, preferred_element_type=F32)
-            + jnp.dot(middle, order, preferred_element_type=F32)
-        ) + jnp.dot(low, order, preferred_element_type=F32)
-        top = 0
+    blocks = count // width
+    value = jnp.concatenate(
+        [rows[:, block * spin * width : (block + 1) * spin * width] for block in range(blocks)], axis=0
+    )
+    high = value.astype(BF16)
+    middle, low = split(value - high.astype(F32))
+    moved = jnp.dot(jnp.concatenate([high, middle, low], axis=0), order, preferred_element_type=F32)
+    size = value.shape[0]
+    moved = moved[:size] + moved[size : 2 * size] + moved[2 * size :]
+    top = 0
+    for block in range(blocks):
         for part in range(parts):
-            for _, depth, target, at, _ in groups:
+            for _, depth, target, at in groups:
                 for a in range(spin):
                     target[part, a, at : at + depth, block * width : (block + 1) * width] = moved[
                         top : top + depth, a * width : (a + 1) * width
                     ]
                 top += depth
+    if by_tile:
+        mine = pl.ds(pl.multiple_of(tile // 2 * by_tile, 8), by_tile)
+        for part in range(parts):
+            for a in range(spin):
+                travel[part, a, by_core : by_core + by_tile, :] = rest[part, a, mine, :]
 
 
 def deal(part, spin, by_core, by_tile):
@@ -210,15 +225,19 @@
     rest = (parts, spin, max(tiles // 2 * by_tile, 8), order // spin)
     return pl.pallas_call(
         functools.partial(deal_kernel, by_core=by_core, by_tile=by_tile, tiles=tiles),
-        in_specs=[pl.BlockSpec(memory_space=pltpu.VMEM)],
+        in_specs=[pl.BlockSpec(memory_space=pltpu.HBM)],
         out_specs=[pl.BlockSpec(memory_space=pltpu.VMEM)] * 2,
         out_shape=[jax.ShapeDtypeStruct(shape, F32), jax.ShapeDtypeStruct(rest, F32)],
-        compiler_params=pltpu.CompilerParams(vmem_limit_bytes=GRAM_VMEM),
+        scratch_shapes=[
+            pltpu.VMEM((parts * (by_core + tiles // 2 * by_tile), order), F32),
+            pltpu.SemaphoreType.DMA((parts * (1 + tiles // 2),)),
+        ],
+        compiler_params=pltpu.CompilerParams(vmem_limit_bytes=PAIR_VMEM),
         name="deal",
     )(part)
 
 
-def exchange_everything(part, gram):
+def exchange_everything(part, gram, extra):
     space_bits, tile_bits = bits_of(lax.axis_size("space")), bits_of(lax.axis_size("tile"))
     tile_count = lax.axis_size("tile")
     sources = part.shape[1]
@@ -231,43 +250,76 @@
     if by_tile:
         pieces.append((rest, rest.shape[2]))
 
-    slots, rounds, spread = {0: mixed}, [], None
-    for r in range(1, len(space_bits) + 2):
+    slots = {0: mixed}
+    places = lax.axis_size("space")
+
+    def wave_of(mask):
+        return 2 if mask == 3 else mask.bit_count() - 1
+
+    waves = max(wave_of(mask) for mask in range(1, places)) + 1
+    masks_of = [[mask for mask in range(1, places) if wave_of(mask) == w] for w in range(waves)]
+
+    def wave(w):
+        bits = [1 if mask == 3 else (mask & -mask).bit_length() - 1 for mask in masks_of[w]]
+        return [swap(slots[mask ^ (1 << bit)], "space", bit) for mask, bit in zip(masks_of[w], bits)]
+
+    def passing(w):
         arrived = []
-        masks = [mask for mask in range(1, lax.axis_size("space")) if mask.bit_count() == r]
-        for mask in masks:
-            low = mask & -mask
-            slots[mask] = swap(slots[mask ^ low], "space", low.bit_length() - 1)
-            arrived.append(slots[mask])
-        if spread is not None:
+        if by_tile:
+            held = jnp.concatenate([slots[mask][:, :, by_core:] for mask in masks_of[w]], axis=2)
             for bit in tile_bits[1:]:
-                arrived.append(swap(spread, "tile", bit))
-                spread = jnp.concatenate([spread, arrived[-1]], axis=2)
-        spread = None
-        if masks and by_tile:
-            spread = jnp.concatenate([slots[mask][:, :, by_core:] for mask in masks], axis=2)
-        rounds.append(arrived)
-        pieces += [(piece, piece.shape[2]) for piece in arrived]
-
-    away, kept = gram([mixed])
-    away = after(away.reshape(-1, kept.shape[-1]), rounds[0])
-    rows = kept.reshape(-1, kept.shape[-1]) + swap(away, "tile", 0)
+                arrived.append(swap(held, "tile", bit))
+                held = jnp.concatenate([held, arrived[-1]], axis=2)
+        return arrived
+
+    coming = {}
+
+    def land(rows, step):
+        landing = [w for w in range(waves) if wave_end(w) == step]
+        values = [coming.pop(("wave", w)) for w in landing]
+        passed = [coming.pop(("pass", w)) for w in range(waves) if pass_end(w) == step]
+        flat = [piece for group in values + passed for piece in group]
+        if flat:
+            rows, *flat = together(rows, *flat)
+            pieces.extend((piece, piece.shape[2]) for piece in flat)
+            for w in landing:
+                slots.update(zip(masks_of[w], flat))
+                flat = flat[len(masks_of[w]) :]
+        for w in landing:
+            if w + 1 < waves:
+                coming["wave", w + 1] = wave(w + 1)
+            coming["pass", w] = passing(w)
+        return rows
+
     steps = [(halve, "tile", b) for b in tile_bits[1:]]
     steps += [(halve, "space", b) for b in space_bits[:1]]
     steps += [(both, "space", b) for b in space_bits[1:]]
     middle = len(steps) - 2
     steps += [(double, axis, b) for step, axis, b in steps[::-1] if step is halve]
-    ends = {middle: 1, middle + 2: 2, len(steps) - 1: 3}
+
+    def wave_end(w):
+        return -1 if w == 0 else middle + WAVE_ENDS[w - 1] if w <= len(WAVE_ENDS) else len(steps) + w
+
+    def pass_end(w):
+        return middle + PASS_ENDS[w] if w < len(PASS_ENDS) else len(steps) + waves + w
+
+    coming["wave", 0] = wave(0)
+    away, kept = gram([mixed])
+    away = land(away.reshape(-1, kept.shape[-1]), -1)
+    rows = kept.reshape(-1, kept.shape[-1]) + swap(away, "tile", 0)
     for n, (step, axis, bit) in enumerate(steps):
         rows = step(rows, axis, bit)
-        if n in ends:
-            rows = after(rows, rounds[ends[n]] if ends[n] < len(rounds) else [])
-    return rows, swap(rows, "tile", 0), pieces
+        if n == middle - 1:
+            rows, *extra = together(rows, *extra)
+        rows = land(rows, n)
+    for n in range(len(steps), len(steps) + 2 * waves):
+        rows = land(rows, n)
+    return rows, swap(rows, "tile", 0), pieces, extra
 
 
 def pair_kernel(blocks, own, other, order, *refs, depths, scale):
     sources = refs[: len(depths)]
-    away, kept, left, right, woven, tau, held, placing, arrived = refs[len(depths) :]
+    away, kept, part_out, left, right, woven, tau, held, placing, arrived = refs[len(depths) :]
     _, spin, total, count = tau.shape
     outs = (away, kept)
     rows = left.shape[3] // 2
@@ -300,6 +352,20 @@
     weights = split(
         jnp.concatenate([jnp.concatenate(real_rows, axis=0), jnp.concatenate(imag_rows, axis=0)], axis=1)
     )
+    columns = part_out.shape[3]
+    line = lax.broadcasted_iota(jnp.int32, (count, columns), 0)
+    lane = lax.broadcasted_iota(jnp.int32, (count, columns), 1)
+    chosen = (line == lane + lax.axis_index("space") * columns).astype(BF16)
+    mine = pl.ds(pl.multiple_of(lax.axis_index("tile") * rows, rows), rows)
+    for p in range(2 * half):
+        for part in range(2):
+            value = held[p, part, mine, :]
+            high = value.astype(BF16)
+            middle, low = split(value - high.astype(F32))
+            part_out[p, part] = (
+                jnp.dot(high, chosen, preferred_element_type=F32)
+                + jnp.dot(middle, chosen, preferred_element_type=F32)
+            ) + jnp.dot(low, chosen, preferred_element_type=F32)
     depth = min(total, 256)
     for n in range(total // depth):
         while copies and sum(depths[: len(depths) - len(copies)]) < (n + 1) * depth:
@@ -314,22 +380,28 @@
                 right[g, a, here, :] = mixed[:, (4 * g + 2) * rows : (4 * g + 4) * rows]
             return carry
 
-        lax.fori_loop(0, spin, mix, 0)
+        for a in range(spin):
+            mix(a, 0)
     last.wait()
     width = rows * spin
     for g, out in enumerate(outs):
         left_hi, left_lo = split(jnp.concatenate([left[g, a] for a in range(spin)], axis=1))
         right_hi, right_lo = split(jnp.concatenate([right[g, a] for a in range(spin)], axis=1))
         pair = (dot_tn(left_hi, right_hi) + dot_tn(left_hi, right_lo) + dot_tn(left_lo, right_hi)) * scale
+        top = jnp.concatenate([pair[2 * a * rows : (2 * a + 1) * rows] for a in range(spin)], axis=0)
+        low = jnp.concatenate([pair[(2 * a + 1) * rows : (2 * a + 2) * rows] for a in range(spin)], axis=0)
+        lane = lax.broadcasted_iota(jnp.int32, top.shape, 1)
+        swapped = jnp.concatenate(
+            [pltpu.roll(low[:, 2 * a * rows : 2 * (a + 1) * rows], rows, 1) for a in range(spin)], axis=1
+        )
+        pair = top + jnp.where(lane % (2 * rows) < rows, -swapped, swapped)
         pair_hi, pair_lo = split(pair)
         placed = jnp.dot(pair_hi, placing[...], preferred_element_type=F32) + jnp.dot(
             pair_lo, placing[...], preferred_element_type=F32
         )
         for a in range(spin):
-            top = placed[2 * a * rows : (2 * a + 1) * rows]
-            low = placed[(2 * a + 1) * rows : (2 * a + 2) * rows]
-            parts = top[:, :width] - low[:, width:], top[:, width:] + low[:, :width]
-            for n, value in enumerate(parts):
+            for n in range(2):
+                value = placed[a * rows : (a + 1) * rows, n * width : (n + 1) * width]
                 for c in range(width // LANES):
                     woven[n, c, pl.ds(a, rows, stride=spin), :] = value[:, c * LANES : (c + 1) * LANES]
         for n in range(2):
@@ -345,20 +417,20 @@
     return (target[:, None] == lane[None, :]).astype(BF16)
 
 
-def pair_contraction(blocks, own, other, pieces, scale):
+def pair_contraction(blocks, order, own, other, pieces, scale):
     half, _, count, _ = own.shape
     spin = pieces[0][0].shape[1]
     depths = [depth for _, depth in pieces]
     total = sum(depths)
     rows = count // lax.axis_size("tile")
-    order = lane_order(rows, spin)
     mixed = pltpu.VMEM((2, spin, total, 2 * rows), F32)
     return pl.pallas_call(
         functools.partial(pair_kernel, depths=depths, scale=scale),
         in_specs=[pl.BlockSpec(memory_space=pltpu.SMEM)]
         + [pl.BlockSpec(memory_space=pltpu.HBM)] * (3 + len(pieces)),
-        out_specs=[pl.BlockSpec(memory_space=pltpu.VMEM)] * 2,
-        out_shape=[jax.ShapeDtypeStruct((2, rows * spin, rows * spin), F32)] * 2,
+        out_specs=[pl.BlockSpec(memory_space=pltpu.VMEM)] * 3,
+        out_shape=[jax.ShapeDtypeStruct((2, rows * spin, rows * spin), F32)] * 2
+        + [jax.ShapeDtypeStruct((2 * half, 2, rows, count // lax.axis_size("space")), F32)],
         scratch_shapes=[
             mixed,
             mixed,
@@ -387,22 +459,15 @@
     def gram(started):
         return local_gram(planes, momenta, norm, started)
 
-    own, other, pieces = exchange_everything(perambulator, gram)
+    spin = order // count
+    blocks = jnp.stack([graph_blocks[device ^ 1], graph_blocks[device]])
+    extra = [blocks, lane_order(count // tile_count, spin)]
+    own, other, pieces, extra = exchange_everything(perambulator, gram, extra)
     half = momenta.shape[0] // 2
     own = own.reshape(half, 2, count, count)
     other = other.reshape(half, 2, count, count)
-    rows, columns = count // tile_count, count // space_count
-    start = (0, 0, tile_index * rows, space_index * columns)
-    own_part = lax.dynamic_slice(own, start, (half, 2, rows, columns))
-    other_part = lax.dynamic_slice(other, start, (half, 2, rows, columns))
-    elementals = jnp.where(
-        tile_index % 2 == 0,
-        jnp.concatenate([own_part, other_part]),
-        jnp.concatenate([other_part, own_part]),
-    )
     scale = 1.0 / (count * math.sqrt(order))
-    blocks = jnp.stack([graph_blocks[device ^ 1], graph_blocks[device]])
-    away, kept = pair_contraction(blocks, own, other, pieces, scale)
+    away, kept, elementals = pair_contraction(*extra, own, other, pieces, scale)
     return elementals, (kept + swap(away, "tile", 0))[None]
 
 

time: 101 us -> 92.3 us (0.914)
  local copies, waits for them, and re-layouts: 9.1 us -> 6.25 us
  other arithmetic: 7.43 us -> 5.12 us
  Pallas kernels: 27.1 us -> 24.8 us
  starting transfers between devices: 25.6 us -> 23.6 us
  waiting for transfers between devices: 30.1 us -> 31.3 us
    pallas_call x1, Pallas kernels: 12.3 us -> 10.2 us  [pair_contraction(): pl.pallas_call(functools.partial(pair_kernel, depths=depths, scale=scale)...]
    ppermute x19, starting transfers between devices: 25.6 us -> 23.6 us  [swap(): return lax.ppermute(value, axis, [(i, i ^ 1 << bit) for i in range(size)])]
    dynamic_slice x2 -> x0, local copies, waits for them, and re-layouts: 1.85 us -> none  [the longest x1 0.93 us: per_device(): other_part = lax.dynamic_slice(other, start, (half, 2, rows, columns))]
    ppermute x19, waiting for transfers between devices: 30.1 us -> 31.3 us  [swap(): return lax.ppermute(value, axis, [(i, i ^ 1 << bit) for i in range(size)])]
    unnamed x33 -> x31, local copies, waits for them, and re-layouts: 5.45 us -> 4.41 us
  transfers between devices with their start and end apart: 19 -> 19, of which waited for: 11 -> 13; matrix products, arithmetic and copies ran while one was open for 9% -> 6% of each run, Pallas kernels for 12% -> 13%
where the time goes in v3:
time: 92.3 us; the launch traced here: 92 us
  waiting for transfers between devices  31.3 us (34%)
  Pallas kernels  24.8 us (27%)
  starting transfers between devices  23.6 us (26%)
  local copies, waits for them, and re-layouts  6.25 us (7%)
  other arithmetic  5.12 us (6%)
  between operations  0.97 us (1%)
    ppermute x19, waiting for transfers between devices, swap(): return lax.ppermute(value, axis, [(i, i ^ 1 << bit) for i in range(size)])  31.3 us
    ppermute x19, starting transfers between devices, swap(): return lax.ppermute(value, axis, [(i, i ^ 1 << bit) for i in range(size)])  23.6 us
    pallas_call x1, Pallas kernels, local_gram(): pl.pallas_call(functools.partial(gram_kernel, width=width, norm=norm), in...  12 us
    pallas_call x1, Pallas kernels, pair_contraction(): pl.pallas_call(functools.partial(pair_kernel, depths=depths, scale=scale)...  10.2 us
    unnamed x31, local copies, waits for them, and re-layouts  4.41 us
    pallas_call x1, Pallas kernels, deal(): pl.pallas_call(functools.partial(deal_kernel, by_core=by_core, by_tile=by...  2.6 us
    broadcast_in_dim x1, other arithmetic, per_device(): return (elementals, (kept + swap(away, 'tile', 0))[None])  1.9 us
  transfers between devices with their start and end apart: 19, of which 13 were waited for; matrix products, arithmetic and copies ran while one was open for 6% of the time, Pallas kernels for 13%

profile of v3, /device:TPU:0, one launch (start us, length us, event | category | flops | bytes accessed | tf_op | source)
XLA Modules:
  0.0 92.0 jit_solution(14688531769511993868)
XLA Ops:
  0.6 2.6 %deal.1 = (f32[2,4,40,256]{3,2,1,0:T(8,128)}, f32[2,4,48,256]{3,2,1,0:T(8,128)}) custom-call(f32[2,128,1024]{2,1,0:T(8,128)} %tau.1), custom_call_target="tpu_custom_call" | custom-call | tf_op jit(solution)/shard_map/deal/pallas_call | solution.py:226
  3.2 4.1 %collective-permute-start.2 = (f32[2,4,40,256]{3,2,1,0:T(8,128)}, f32[2,4,40,256]{3,2,1,0:T(8,128)S(1)}, u32[]{:S(2)}, u32[]{:S(2)}) collective-permute-start(f32[2,4,40,256]{3,2,1,0:T(8,128)} %get-tuple-element.28.refs_0_), channel_id=1, source_target_pairs={{0,16},{4,20},{8,24},{12,28},{16,0},{20,4},{24,8},{28,12},{1,17},{... | collective-permute-start | bytes 983048 | tf_op jit(solution)/shard_map/ppermute | solution.py:135
  7.3 1.6 %collective-permute-start.1 = (f32[2,4,40,256]{3,2,1,0:T(8,128)}, f32[2,4,40,256]{3,2,1,0:T(8,128)S(1)}, u32[]{:S(2)}, u32[]{:S(2)}) collective-permute-start(f32[2,4,40,256]{3,2,1,0:T(8,128)} %get-tuple-element.28.refs_0_), channel_id=1, source_target_pairs={{0,8},{4,12},{8,0},{12,4},{16,24},{20,28},{24,16},{28,20},{1,9},{5... | collective-permute-start | bytes 983048 | tf_op jit(solution)/shard_map/ppermute | solution.py:135
  8.9 1.5 %collective-permute-start = (f32[2,4,40,256]{3,2,1,0:T(8,128)}, f32[2,4,40,256]{3,2,1,0:T(8,128)}, u32[]{:S(2)}, u32[]{:S(2)}) collective-permute-start(f32[2,4,40,256]{3,2,1,0:T(8,128)} %get-tuple-element.28.refs_0_), channel_id=1, source_target_pairs={{0,4},{4,0},{8,12},{12,8},{16,20},{20,16},{24,28},{28,24},{1,5},{5... | collective-permute-start | bytes 983048 | tf_op jit(solution)/shard_map/ppermute | solution.py:135
  10.4 12.0 %local_gram.1 = (f32[1,2,256,256]{3,2,1,0:T(8,128)}, f32[1,2,256,256]{3,2,1,0:T(8,128)}) custom-call(s32[2,3]{1,0:T(2,128)} %momenta.1, f32[2,3,256,1024]{3,2,1,0:T(8,128)} %bitcast.11, f32[2,4,40,256]{3,2,1,0:T(8,128)} %get-tuple-element.28.refs_0_), custom_call_target="tpu_custom_call" | custom-call | flops 9663676416 | bytes 6291456 | tf_op jit(solution)/shard_map/local_gram/pallas_call | solution.py:100
  22.6 1.0 %copy-done.9 = f32[1,2,256,256]{3,2,1,0:T(8,128)S(1)} copy-done((f32[1,2,256,256]{3,2,1,0:T(8,128)S(1)}, f32[1,2,256,256]{3,2,1,0:T(8,128)}, u32[]{:S(2)}) %copy-start.9) | copy-done | bytes 524312
  23.7 1.9 %collective-permute-done.3 = f32[512,256]{1,0:T(8,128)S(1)} collective-permute-done((f32[512,256]{1,0:T(8,128)S(1)}, f32[512,256]{1,0:T(8,128)S(1)}, u32[]{:S(2)}, u32[]{:S(2)}) %collective-permute-start.3) | collective-permute-done | bytes 524320 | tf_op jit(solution)/shard_map/ppermute | solution.py:135
  25.5 1.1 %bitcast_add_fusion = f32[512,256]{1,0:T(8,128)S(1)} fusion(f32[512,256]{1,0:T(8,128)S(1)} %collective-permute-done.3, f32[1,2,256,256]{3,2,1,0:T(8,128)} %get-tuple-element.29), kind=kLoop, calls=%fused_computation.4 | loop fusion | flops 131072 | bytes 1572864 | tf_op jit(solution)/shard_map/add | solution.py:309
  26.7 1.6 %collective-permute-start.4 = (f32[256,256]{1,0:T(8,128)S(1)}, f32[256,256]{1,0:T(8,128)S(1)}, u32[]{:S(2)}, u32[]{:S(2)}) collective-permute-start(f32[256,256]{1,0:T(8,128)S(1)} %constant_dynamic-slice_fusion.3), channel_id=1, source_target_pairs={{0,2},{1,3},{2,0},{3,1},{4,6},{5,7},{6,4},{7,5},{8,10},{9,11},{10,... | collective-permute-start | bytes 786440 | tf_op jit(solution)/shard_map/ppermute | solution.py:135
  28.5 1.5 %collective-permute-start.6 = (f32[2,4,40,256]{3,2,1,0:T(8,128)S(1)}, f32[2,4,40,256]{3,2,1,0:T(8,128)S(1)}, u32[]{:S(2)}, u32[]{:S(2)}) collective-permute-start(f32[2,4,40,256]{3,2,1,0:T(8,128)S(1)} %get-tuple-element.32.refs_4_), channel_id=1, source_target_pairs={{0,8},{4,12},{8,0},{12,4},{16,24},{20,28},{24,16},{28,20},{1,9},{5... | collective-permute-start | bytes 983048 | tf_op jit(solution)/shard_map/ppermute | solution.py:135
  30.0 1.5 %collective-permute-start.5 = (f32[2,4,40,256]{3,2,1,0:T(8,128)S(1)}, f32[2,4,40,256]{3,2,1,0:T(8,128)S(1)}, u32[]{:S(2)}, u32[]{:S(2)}) collective-permute-start(f32[2,4,40,256]{3,2,1,0:T(8,128)S(1)} %get-tuple-element.32.refs_4_), channel_id=1, source_target_pairs={{0,4},{4,0},{8,12},{12,8},{16,20},{20,16},{24,28},{28,24},{1,5},{5... | collective-permute-start | bytes 983048 | tf_op jit(solution)/shard_map/ppermute | solution.py:135
  31.5 0.9 %slice.21 = f32[2,4,24,256]{3,2,1,0:T(8,128)S(1)} slice(f32[2,4,40,256]{3,2,1,0:T(8,128)} %get-tuple-element.36.refs_2_), slice={[0:2], [0:4], [16:40], [0:256]} | slice | bytes 393216 | tf_op jit(solution)/shard_map/slice | solution.py:269
  33.8 1.3 %collective-permute-done.4 = f32[256,256]{1,0:T(8,128)S(1)} collective-permute-done((f32[256,256]{1,0:T(8,128)S(1)}, f32[256,256]{1,0:T(8,128)S(1)}, u32[]{:S(2)}, u32[]{:S(2)}) %collective-permute-start.4) | collective-permute-done | bytes 262176 | tf_op jit(solution)/shard_map/ppermute | solution.py:135
  35.1 2.9 %collective-permute-done.6.refs_2_ = f32[2,4,40,256]{3,2,1,0:T(8,128)S(1)} collective-permute-done((f32[2,4,40,256]{3,2,1,0:T(8,128)S(1)}, f32[2,4,40,256]{3,2,1,0:T(8,128)S(1)}, u32[]{:S(2)}, u32[]{:S(2)}) %collective-permute-start.6) | collective-permute-done | bytes 327712 | tf_op jit(solution)/shard_map/ppermute | solution.py:135
  38.0 1.2 %collective-permute-done.5.refs_1_ = f32[2,4,40,256]{3,2,1,0:T(8,128)S(1)} collective-permute-done((f32[2,4,40,256]{3,2,1,0:T(8,128)S(1)}, f32[2,4,40,256]{3,2,1,0:T(8,128)S(1)}, u32[]{:S(2)}, u32[]{:S(2)}) %collective-permute-start.5) | collective-permute-done | bytes 327712 | tf_op jit(solution)/shard_map/ppermute | solution.py:135
  39.9 1.5 %collective-permute-start.7 = (f32[128,256]{1,0:T(8,128)}, f32[128,256]{1,0:T(8,128)S(1)}, u32[]{:S(2)}, u32[]{:S(2)}) collective-permute-start(f32[128,256]{1,0:T(8,128)} %constant_dynamic-slice_fusion.2), channel_id=1, source_target_pairs={{0,4},{4,0},{8,12},{12,8},{16,20},{20,16},{24,28},{28,24},{1,5},{5... | collective-permute-start | bytes 393224 | tf_op jit(solution)/shard_map/ppermute | solution.py:135
  43.0 3.5 %collective-permute-done.7 = f32[128,256]{1,0:T(8,128)S(1)} collective-permute-done((f32[128,256]{1,0:T(8,128)}, f32[128,256]{1,0:T(8,128)S(1)}, u32[]{:S(2)}, u32[]{:S(2)}) %collective-permute-start.7) | collective-permute-done | bytes 131104 | tf_op jit(solution)/shard_map/ppermute | solution.py:135
  46.5 1.6 %collective-permute-done.8.refs_1_ = f32[2,4,72,256]{3,2,1,0:T(8,128)S(1)} collective-permute-done((f32[2,4,72,256]{3,2,1,0:T(8,128)}, f32[2,4,72,256]{3,2,1,0:T(8,128)S(1)}, u32[]{:S(2)}, u32[]{:S(2)}) %collective-permute-start.8) | collective-permute-done | bytes 589856 | tf_op jit(solution)/shard_map/ppermute | solution.py:135
  48.1 1.2 %collective-permute-start.9 = (f32[128,256]{1,0:T(8,128)S(1)}, f32[128,256]{1,0:T(8,128)S(1)}, u32[]{:S(2)}, u32[]{:S(2)}) collective-permute-start(f32[128,256]{1,0:T(8,128)S(1)} %get-tuple-element.38), channel_id=1, source_target_pairs={{0,8},{4,12},{8,0},{12,4},{16,24},{20,28},{24,16},{28,20},{1,9},{5... | collective-permute-start | bytes 393224 | tf_op jit(solution)/shard_map/ppermute | solution.py:135
  49.3 1.6 %collective-permute-start.13 = (f32[2,4,48,256]{3,2,1,0:T(8,128)S(1)}, f32[2,4,48,256]{3,2,1,0:T(8,128)S(1)}, u32[]{:S(2)}, u32[]{:S(2)}) collective-permute-start(f32[2,4,48,256]{3,2,1,0:T(8,128)S(1)} %pad_maximum_fusion.1), channel_id=1, source_target_pairs={{0,2},{1,3},{2,0},{3,1},{4,6},{5,7},{6,4},{7,5},{8,10},{9,11},{10,... | collective-permute-start | bytes 1179656 | tf_op jit(solution)/shard_map/ppermute | solution.py:135
  50.9 2.2 %collective-permute-done.9 = f32[128,256]{1,0:T(8,128)S(1)} collective-permute-done((f32[128,256]{1,0:T(8,128)S(1)}, f32[128,256]{1,0:T(8,128)S(1)}, u32[]{:S(2)}, u32[]{:S(2)}) %collective-permute-start.9) | collective-permute-done | bytes 131104 | tf_op jit(solution)/shard_map/ppermute | solution.py:135
  54.1 1.2 %collective-permute-start.15 = (f32[2,4,48,256]{3,2,1,0:T(8,128)}, f32[2,4,48,256]{3,2,1,0:T(8,128)}, u32[]{:S(2)}, u32[]{:S(2)}) collective-permute-start(f32[2,4,48,256]{3,2,1,0:T(8,128)} %pad_maximum_fusion.2), channel_id=1, source_target_pairs={{0,2},{1,3},{2,0},{3,1},{4,6},{5,7},{6,4},{7,5},{8,10},{9,11},{10,... | collective-permute-start | bytes 1179656 | tf_op jit(solution)/shard_map/ppermute | solution.py:135
  55.3 1.8 %collective-permute-start.12 = (f32[128,256]{1,0:T(8,128)S(1)}, f32[128,256]{1,0:T(8,128)S(1)}, u32[]{:S(2)}, u32[]{:S(2)}) collective-permute-start(f32[128,256]{1,0:T(8,128)S(1)} %get-tuple-element.40), channel_id=1, source_target_pairs={{0,16},{4,20},{8,24},{12,28},{16,0},{20,4},{24,8},{28,12},{1,17},{... | collective-permute-start | bytes 393224 | tf_op jit(solution)/shard_map/ppermute | solution.py:135
  57.1 5.5 %collective-permute-done.12 = f32[128,256]{1,0:T(8,128)S(1)} collective-permute-done((f32[128,256]{1,0:T(8,128)S(1)}, f32[128,256]{1,0:T(8,128)S(1)}, u32[]{:S(2)}, u32[]{:S(2)}) %collective-permute-start.12) | collective-permute-done | bytes 131104 | tf_op jit(solution)/shard_map/ppermute | solution.py:135
  63.4 1.5 %collective-permute-start.14 = (f32[128,256]{1,0:T(8,128)S(1)}, f32[128,256]{1,0:T(8,128)S(1)}, u32[]{:S(2)}, u32[]{:S(2)}) collective-permute-start(f32[128,256]{1,0:T(8,128)S(1)} %get-tuple-element.42), channel_id=1, source_target_pairs={{0,4},{4,0},{8,12},{12,8},{16,20},{20,16},{24,28},{28,24},{1,5},{5... | collective-permute-start | bytes 393224 | tf_op jit(solution)/shard_map/ppermute | solution.py:135
  64.9 3.5 %collective-permute-done.14 = f32[128,256]{1,0:T(8,128)S(1)} collective-permute-done((f32[128,256]{1,0:T(8,128)S(1)}, f32[128,256]{1,0:T(8,128)S(1)}, u32[]{:S(2)}, u32[]{:S(2)}) %collective-permute-start.14) | collective-permute-done | bytes 131104 | tf_op jit(solution)/shard_map/ppermute | solution.py:135
  68.4 1.0 %collective-permute-start.16 = (f32[256,256]{1,0:T(8,128)S(1)}, f32[256,256]{1,0:T(8,128)S(1)}, u32[]{:S(2)}, u32[]{:S(2)}) collective-permute-start(f32[256,256]{1,0:T(8,128)S(1)} %get-tuple-element.45), channel_id=1, source_target_pairs={{0,2},{1,3},{2,0},{3,1},{4,6},{5,7},{6,4},{7,5},{8,10},{9,11},{10,... | collective-permute-start | bytes 786440 | tf_op jit(solution)/shard_map/ppermute | solution.py:135
  69.4 5.4 %collective-permute-done.16 = f32[256,256]{1,0:T(8,128)S(1)} collective-permute-done((f32[256,256]{1,0:T(8,128)S(1)}, f32[256,256]{1,0:T(8,128)S(1)}, u32[]{:S(2)}, u32[]{:S(2)}) %collective-permute-start.16) | collective-permute-done | bytes 262176 | tf_op jit(solution)/shard_map/ppermute | solution.py:135
  75.0 1.9 %collective-permute-done.17 = f32[512,256]{1,0:T(8,128)S(1)} collective-permute-done((f32[512,256]{1,0:T(8,128)S(1)}, f32[512,256]{1,0:T(8,128)S(1)}, u32[]{:S(2)}, u32[]{:S(2)}) %collective-permute-start.17) | collective-permute-done | bytes 524320 | tf_op jit(solution)/shard_map/ppermute | solution.py:135
  77.7 10.2 %pair_contraction.1 = (f32[2,256,256]{2,1,0:T(8,128)}, f32[2,256,256]{2,1,0:T(8,128)}, f32[2,2,64,32]{3,2,1,0:T(8,128)}) custom-call(s32[2,2]{1,0:T(2,128)} %copy-done.10, f32[1,2,256,256]{3,2,1,0:T(8,128)} %bitcast.9, f32[1,2,256,256]{3,2,1,0:T(8,128)} %bitcast.10, bf16[512,512]{1,0:T(8,128)(2,1)} %copy-done, f32[2,4,40,256]{3,2,1,0:T(8,128)} %get-tuple-element.28.refs_0_, ...), custom_call_target="tpu_custom_call" | custom-call | tf_op jit(solution)/shard_map/pair_contraction/pallas_call | solution.py:427
  88.1 1.6 %copy.27 = f32[2,2,64,32]{2,3,1,0:T(8,128)} copy(f32[2,2,64,32]{3,2,1,0:T(8,128)} %get-tuple-element.54) | data formatting | bytes 65536
  90.1 1.9 %add_bitcast_fusion = f32[1,2,256,256]{3,2,1,0:T(8,128)} fusion(f32[2,256,256]{2,1,0:T(8,128)} %get-tuple-element.52, f32[2,256,256]{2,1,0:T(8,128)S(1)} %collective-permute-done.18), kind=kLoop, calls=%fused_computation.5 | loop fusion | flops 131072 | bytes 1572864 | tf_op jit(solution)/shard_map/broadcast_in_dim | solution.py:471
  (71 shorter events, 7.3 us)
Async XLA Ops:
  3.2 19.2 %collective-permute-start.2 = (f32[2,4,40,256]{3,2,1,0:T(8,128)}, f32[2,4,40,256]{3,2,1,0:T(8,128)S(1)}, u32[]{:S(2)}, u32[]{:S(2)}) collective-permute-start(f32[2,4,40,256]{3,2,1,0:T(8,128)} %get-tuple-element.28.refs_0_), channel_id=1, source_target_pairs={{0,16},{4,20},{8,24},{12,28},{16,0},{20,4},{24,8},{28,12},{1,17},{... | collective-permute-start | bytes 983048 | tf_op jit(solution)/shard_map/ppermute | solution.py:135
  7.3 15.2 %collective-permute-start.1 = (f32[2,4,40,256]{3,2,1,0:T(8,128)}, f32[2,4,40,256]{3,2,1,0:T(8,128)S(1)}, u32[]{:S(2)}, u32[]{:S(2)}) collective-permute-start(f32[2,4,40,256]{3,2,1,0:T(8,128)} %get-tuple-element.28.refs_0_), channel_id=1, source_target_pairs={{0,8},{4,12},{8,0},{12,4},{16,24},{20,28},{24,16},{28,20},{1,9},{5... | collective-permute-start | bytes 983048 | tf_op jit(solution)/shard_map/ppermute | solution.py:135
  8.9 13.7 %collective-permute-start = (f32[2,4,40,256]{3,2,1,0:T(8,128)}, f32[2,4,40,256]{3,2,1,0:T(8,128)}, u32[]{:S(2)}, u32[]{:S(2)}) collective-permute-start(f32[2,4,40,256]{3,2,1,0:T(8,128)} %get-tuple-element.28.refs_0_), channel_id=1, source_target_pairs={{0,4},{4,0},{8,12},{12,8},{16,20},{20,16},{24,28},{28,24},{1,5},{5... | collective-permute-start | bytes 983048 | tf_op jit(solution)/shard_map/ppermute | solution.py:135
  22.4 19.0 %copy-start.13 = (s32[32,2]{0,1:T(2,128)S(1)}, s32[32,2]{0,1:T(2,128)}, u32[]{:S(2)}) copy-start(s32[32,2]{0,1:T(2,128)} %param.7) | copy-start | bytes 772
  22.6 1.0 %copy-start.9 = (f32[1,2,256,256]{3,2,1,0:T(8,128)S(1)}, f32[1,2,256,256]{3,2,1,0:T(8,128)}, u32[]{:S(2)}) copy-start(f32[1,2,256,256]{3,2,1,0:T(8,128)} %get-tuple-element.30) | copy-start | bytes 1572868
  23.6 30.4 %copy-start.6 = (f32[2,4,40,256]{3,2,1,0:T(8,128)}, f32[2,4,40,256]{3,2,1,0:T(8,128)S(1)}, u32[]{:S(2)}) copy-start(f32[2,4,40,256]{3,2,1,0:T(8,128)S(1)} %get-tuple-element.32.refs_4_) | copy-start | bytes 983044
  23.6 30.4 %copy-start.7 = (f32[2,4,40,256]{3,2,1,0:T(8,128)}, f32[2,4,40,256]{3,2,1,0:T(8,128)S(1)}, u32[]{:S(2)}) copy-start(f32[2,4,40,256]{3,2,1,0:T(8,128)S(1)} %get-tuple-element.37.refs_3_) | copy-start | bytes 983044
  23.6 1.9 %collective-permute-start.3 = (f32[512,256]{1,0:T(8,128)S(1)}, f32[512,256]{1,0:T(8,128)S(1)}, u32[]{:S(2)}, u32[]{:S(2)}) collective-permute-start(f32[512,256]{1,0:T(8,128)S(1)} %get-tuple-element.31), channel_id=1, source_target_pairs={{0,1},{1,0},{2,3},{3,2},{4,5},{5,4},{6,7},{7,6},{8,9},{9,8},{10,11... | collective-permute-start | bytes 1572872 | tf_op jit(solution)/shard_map/ppermute | solution.py:135
  26.7 8.4 %collective-permute-start.4 = (f32[256,256]{1,0:T(8,128)S(1)}, f32[256,256]{1,0:T(8,128)S(1)}, u32[]{:S(2)}, u32[]{:S(2)}) collective-permute-start(f32[256,256]{1,0:T(8,128)S(1)} %constant_dynamic-slice_fusion.3), channel_id=1, source_target_pairs={{0,2},{1,3},{2,0},{3,1},{4,6},{5,7},{6,4},{7,5},{8,10},{9,11},{10,... | collective-permute-start | bytes 786440 | tf_op jit(solution)/shard_map/ppermute | solution.py:135
  28.5 9.5 %collective-permute-start.6 = (f32[2,4,40,256]{3,2,1,0:T(8,128)S(1)}, f32[2,4,40,256]{3,2,1,0:T(8,128)S(1)}, u32[]{:S(2)}, u32[]{:S(2)}) collective-permute-start(f32[2,4,40,256]{3,2,1,0:T(8,128)S(1)} %get-tuple-element.32.refs_4_), channel_id=1, source_target_pairs={{0,8},{4,12},{8,0},{12,4},{16,24},{20,28},{24,16},{28,20},{1,9},{5... | collective-permute-start | bytes 983048 | tf_op jit(solution)/shard_map/ppermute | solution.py:135
  30.0 9.2 %collective-permute-start.5 = (f32[2,4,40,256]{3,2,1,0:T(8,128)S(1)}, f32[2,4,40,256]{3,2,1,0:T(8,128)S(1)}, u32[]{:S(2)}, u32[]{:S(2)}) collective-permute-start(f32[2,4,40,256]{3,2,1,0:T(8,128)S(1)} %get-tuple-element.32.refs_4_), channel_id=1, source_target_pairs={{0,4},{4,0},{8,12},{12,8},{16,20},{20,16},{24,28},{28,24},{1,5},{5... | collective-permute-start | bytes 983048 | tf_op jit(solution)/shard_map/ppermute | solution.py:135
  33.3 14.7 %collective-permute-start.8 = (f32[2,4,72,256]{3,2,1,0:T(8,128)}, f32[2,4,72,256]{3,2,1,0:T(8,128)S(1)}, u32[]{:S(2)}, u32[]{:S(2)}) collective-permute-start(f32[2,4,72,256]{3,2,1,0:T(8,128)} %pad_maximum_fusion), channel_id=1, source_target_pairs={{0,2},{1,3},{2,0},{3,1},{4,6},{5,7},{6,4},{7,5},{8,10},{9,11},{10,... | collective-permute-start | bytes 1769480 | tf_op jit(solution)/shard_map/ppermute | solution.py:135
  39.2 37.7 %copy-start.2 = (f32[2,4,40,256]{3,2,1,0:T(8,128)}, f32[2,4,40,256]{3,2,1,0:T(8,128)S(1)}, u32[]{:S(2)}) copy-start(f32[2,4,40,256]{3,2,1,0:T(8,128)S(1)} %get-tuple-element.39.refs_6_) | copy-start | bytes 983044
  39.2 37.7 %copy-start.3 = (f32[2,4,40,256]{3,2,1,0:T(8,128)}, f32[2,4,40,256]{3,2,1,0:T(8,128)S(1)}, u32[]{:S(2)}) copy-start(f32[2,4,40,256]{3,2,1,0:T(8,128)S(1)} %get-tuple-element.41.refs_5_) | copy-start | bytes 983044
  39.9 6.5 %collective-permute-start.7 = (f32[128,256]{1,0:T(8,128)}, f32[128,256]{1,0:T(8,128)S(1)}, u32[]{:S(2)}, u32[]{:S(2)}) collective-permute-start(f32[128,256]{1,0:T(8,128)} %constant_dynamic-slice_fusion.2), channel_id=1, source_target_pairs={{0,4},{4,0},{8,12},{12,8},{16,20},{20,16},{24,28},{28,24},{1,5},{5... | collective-permute-start | bytes 393224 | tf_op jit(solution)/shard_map/ppermute | solution.py:135
  41.7 11.4 %collective-permute-start.10 = (f32[2,4,40,256]{3,2,1,0:T(8,128)}, f32[2,4,40,256]{3,2,1,0:T(8,128)S(1)}, u32[]{:S(2)}, u32[]{:S(2)}) collective-permute-start(f32[2,4,40,256]{3,2,1,0:T(8,128)} %get-tuple-element.36.refs_2_), channel_id=1, source_target_pairs={{0,8},{4,12},{8,0},{12,4},{16,24},{20,28},{24,16},{28,20},{1,9},{5... | collective-permute-start | bytes 983048 | tf_op jit(solution)/shard_map/ppermute | solution.py:135
  42.3 10.7 %collective-permute-start.11 = (f32[2,4,40,256]{3,2,1,0:T(8,128)S(1)}, f32[2,4,40,256]{3,2,1,0:T(8,128)S(1)}, u32[]{:S(2)}, u32[]{:S(2)}) collective-permute-start(f32[2,4,40,256]{3,2,1,0:T(8,128)S(1)} %get-tuple-element.39.refs_6_), channel_id=1, source_target_pairs={{0,4},{4,0},{8,12},{12,8},{16,20},{20,16},{24,28},{28,24},{1,5},{5... | collective-permute-start | bytes 983048 | tf_op jit(solution)/shard_map/ppermute | solution.py:135
  46.5 30.4 %copy-start = (bf16[512,512]{1,0:T(8,128)(2,1)}, bf16[512,512]{1,0:T(8,128)(2,1)S(1)}, u32[]{:S(2)}) copy-start(bf16[512,512]{1,0:T(8,128)(2,1)S(1)} %get-tuple-element.46.order) | copy-start | bytes 1572868
  46.5 30.4 %copy-start.10 = (s32[2,2]{1,0:T(2,128)}, s32[2,2]{1,0:T(2,128)S(1)}, u32[]{:S(2)}) copy-start(s32[2,2]{1,0:T(2,128)S(1)} %get-tuple-element.34.blocks) | copy-start | bytes 52
  48.1 28.8 %copy-start.1 = (f32[2,4,72,256]{3,2,1,0:T(8,128)}, f32[2,4,72,256]{3,2,1,0:T(8,128)S(1)}, u32[]{:S(2)}) copy-start(f32[2,4,72,256]{3,2,1,0:T(8,128)S(1)} %get-tuple-element.48.refs_7_) | copy-start | bytes 1769476
  48.1 5.0 %collective-permute-start.9 = (f32[128,256]{1,0:T(8,128)S(1)}, f32[128,256]{1,0:T(8,128)S(1)}, u32[]{:S(2)}, u32[]{:S(2)}) collective-permute-start(f32[128,256]{1,0:T(8,128)S(1)} %get-tuple-element.38), channel_id=1, source_target_pairs={{0,8},{4,12},{8,0},{12,4},{16,24},{20,28},{24,16},{28,20},{1,9},{5... | collective-permute-start | bytes 393224 | tf_op jit(solution)/shard_map/ppermute | solution.py:135
  49.3 13.3 %collective-permute-start.13 = (f32[2,4,48,256]{3,2,1,0:T(8,128)S(1)}, f32[2,4,48,256]{3,2,1,0:T(8,128)S(1)}, u32[]{:S(2)}, u32[]{:S(2)}) collective-permute-start(f32[2,4,48,256]{3,2,1,0:T(8,128)S(1)} %pad_maximum_fusion.1), channel_id=1, source_target_pairs={{0,2},{1,3},{2,0},{3,1},{4,6},{5,7},{6,4},{7,5},{8,10},{9,11},{10,... | collective-permute-start | bytes 1179656 | tf_op jit(solution)/shard_map/ppermute | solution.py:135
  53.1 23.8 %copy-start.4 = (f32[2,4,40,256]{3,2,1,0:T(8,128)}, f32[2,4,40,256]{3,2,1,0:T(8,128)S(1)}, u32[]{:S(2)}) copy-start(f32[2,4,40,256]{3,2,1,0:T(8,128)S(1)} %get-tuple-element.43.refs_8_) | copy-start | bytes 983044
  53.1 23.8 %copy-start.5 = (f32[2,4,40,256]{3,2,1,0:T(8,128)}, f32[2,4,40,256]{3,2,1,0:T(8,128)S(1)}, u32[]{:S(2)}) copy-start(f32[2,4,40,256]{3,2,1,0:T(8,128)S(1)} %get-tuple-element.44.refs_9_) | copy-start | bytes 983044
  54.1 14.3 %collective-permute-start.15 = (f32[2,4,48,256]{3,2,1,0:T(8,128)}, f32[2,4,48,256]{3,2,1,0:T(8,128)}, u32[]{:S(2)}, u32[]{:S(2)}) collective-permute-start(f32[2,4,48,256]{3,2,1,0:T(8,128)} %pad_maximum_fusion.2), channel_id=1, source_target_pairs={{0,2},{1,3},{2,0},{3,1},{4,6},{5,7},{6,4},{7,5},{8,10},{9,11},{10,... | collective-permute-start | bytes 1179656 | tf_op jit(solution)/shard_map/ppermute | solution.py:135
  55.3 7.3 %collective-permute-start.12 = (f32[128,256]{1,0:T(8,128)S(1)}, f32[128,256]{1,0:T(8,128)S(1)}, u32[]{:S(2)}, u32[]{:S(2)}) collective-permute-start(f32[128,256]{1,0:T(8,128)S(1)} %get-tuple-element.40), channel_id=1, source_target_pairs={{0,16},{4,20},{8,24},{12,28},{16,0},{20,4},{24,8},{28,12},{1,17},{... | collective-permute-start | bytes 393224 | tf_op jit(solution)/shard_map/ppermute | solution.py:135
  63.4 5.0 %collective-permute-start.14 = (f32[128,256]{1,0:T(8,128)S(1)}, f32[128,256]{1,0:T(8,128)S(1)}, u32[]{:S(2)}, u32[]{:S(2)}) collective-permute-start(f32[128,256]{1,0:T(8,128)S(1)} %get-tuple-element.42), channel_id=1, source_target_pairs={{0,4},{4,0},{8,12},{12,8},{16,20},{20,16},{24,28},{28,24},{1,5},{5... | collective-permute-start | bytes 393224 | tf_op jit(solution)/shard_map/ppermute | solution.py:135
  68.4 6.4 %collective-permute-start.16 = (f32[256,256]{1,0:T(8,128)S(1)}, f32[256,256]{1,0:T(8,128)S(1)}, u32[]{:S(2)}, u32[]{:S(2)}) collective-permute-start(f32[256,256]{1,0:T(8,128)S(1)} %get-tuple-element.45), channel_id=1, source_target_pairs={{0,2},{1,3},{2,0},{3,1},{4,6},{5,7},{6,4},{7,5},{8,10},{9,11},{10,... | collective-permute-start | bytes 786440 | tf_op jit(solution)/shard_map/ppermute | solution.py:135
  74.9 2.0 %copy-start.11 = (f32[512,256]{1,0:T(8,128)}, f32[512,256]{1,0:T(8,128)S(1)}, u32[]{:S(2)}) copy-start(f32[512,256]{1,0:T(8,128)S(1)} %maximum_select_fusion) | copy-start | bytes 1572868
  74.9 2.0 %collective-permute-start.17 = (f32[512,256]{1,0:T(8,128)S(1)}, f32[512,256]{1,0:T(8,128)S(1)}, u32[]{:S(2)}, u32[]{:S(2)}) collective-permute-start(f32[512,256]{1,0:T(8,128)S(1)} %maximum_select_fusion), channel_id=1, source_target_pairs={{0,1},{1,0},{2,3},{3,2},{4,5},{5,4},{6,7},{7,6},{8,9},{9,8},{10,11... | collective-permute-start | bytes 1572872 | tf_op jit(solution)/shard_map/ppermute | solution.py:135
  76.9 0.8 copy-start.12
  87.9 2.2 %collective-permute-start.18 = (f32[2,256,256]{2,1,0:T(8,128)}, f32[2,256,256]{2,1,0:T(8,128)S(1)}, u32[]{:S(2)}, u32[]{:S(2)}) collective-permute-start(f32[2,256,256]{2,1,0:T(8,128)} %get-tuple-element.53), channel_id=1, source_target_pairs={{0,1},{1,0},{2,3},{3,2},{4,5},{5,4},{6,7},{7,6},{8,9},{9,8},{10,11... | collective-permute-start | bytes 1572872 | tf_op jit(solution)/shard_map/ppermute | solution.py:135
  (1 other events, 0.8 us)

commit v4 on v3

--- a/solution.py
+++ b/solution.py
@@ -165,16 +165,16 @@
     )
 
 
-def deal_kernel(tau, travel, rest, fetched, arrived, *, by_core, by_tile, tiles):
+def deal_kernel(tau, travel, whole, fetched, arrived, *, by_core, by_tile, tiles):
     parts, spin, _, count = travel.shape
     tile = lax.axis_index("tile")
     core = lax.rem(tile, 2)
-    groups = [(pl.multiple_of(core * by_core, 8), by_core, travel, 0)]
+    groups = [(pl.multiple_of(core * by_core, 8), by_core, whole, 0)]
     shared = 2 * by_core
     if by_tile:
         for n in range(tiles // 2):
             first = pl.multiple_of(shared + (2 * n + core) * by_tile, 8)
-            groups.append((first, by_tile, rest, n * by_tile))
+            groups.append((first, by_tile, whole, by_core + n * by_tile))
     copies, top = [], 0
     for part in range(parts):
         for first, depth, *_ in groups:
@@ -211,23 +211,24 @@
                         top : top + depth, a * width : (a + 1) * width
                     ]
                 top += depth
-    if by_tile:
-        mine = pl.ds(pl.multiple_of(tile // 2 * by_tile, 8), by_tile)
-        for part in range(parts):
-            for a in range(spin):
-                travel[part, a, by_core : by_core + by_tile, :] = rest[part, a, mine, :]
+    for part in range(parts):
+        for a in range(spin):
+            travel[part, a, :by_core, :] = whole[part, a, :by_core, :]
+            if by_tile:
+                mine = pl.ds(pl.multiple_of(by_core + tile // 2 * by_tile, 8), by_tile)
+                travel[part, a, by_core : by_core + by_tile, :] = whole[part, a, mine, :]
 
 
 def deal(part, spin, by_core, by_tile):
     parts, _, order = part.shape
     tiles = lax.axis_size("tile")
     shape = (parts, spin, by_core + by_tile, order // spin)
-    rest = (parts, spin, max(tiles // 2 * by_tile, 8), order // spin)
+    whole = (parts, spin, by_core + tiles // 2 * by_tile, order // spin)
     return pl.pallas_call(
         functools.partial(deal_kernel, by_core=by_core, by_tile=by_tile, tiles=tiles),
         in_specs=[pl.BlockSpec(memory_space=pltpu.HBM)],
         out_specs=[pl.BlockSpec(memory_space=pltpu.VMEM)] * 2,
-        out_shape=[jax.ShapeDtypeStruct(shape, F32), jax.ShapeDtypeStruct(rest, F32)],
+        out_shape=[jax.ShapeDtypeStruct(shape, F32), jax.ShapeDtypeStruct(whole, F32)],
         scratch_shapes=[
             pltpu.VMEM((parts * (by_core + tiles // 2 * by_tile), order), F32),
             pltpu.SemaphoreType.DMA((parts * (1 + tiles // 2),)),
@@ -245,10 +246,8 @@
     if (sources - shared) // tile_count % 8:
         shared = sources
     by_core, by_tile = shared // 2, (sources - shared) // tile_count
-    mixed, rest = deal(part, 4, by_core, by_tile)
-    pieces = [(mixed, by_core)]
-    if by_tile:
-        pieces.append((rest, rest.shape[2]))
+    mixed, whole = deal(part, 4, by_core, by_tile)
+    pieces = [(whole, whole.shape[2])]
 
     slots = {0: mixed}
     places = lax.axis_size("space")
@@ -261,12 +260,13 @@
 
     def wave(w):
         bits = [1 if mask == 3 else (mask & -mask).bit_length() - 1 for mask in masks_of[w]]
-        return [swap(slots[mask ^ (1 << bit)], "space", bit) for mask, bit in zip(masks_of[w], bits)]
+        given = [whole if mask == 1 else slots[mask ^ (1 << bit)] for mask, bit in zip(masks_of[w], bits)]
+        return [swap(value, "space", bit) for value, bit in zip(given, bits)]
 
     def passing(w):
         arrived = []
         if by_tile:
-            held = jnp.concatenate([slots[mask][:, :, by_core:] for mask in masks_of[w]], axis=2)
+            held = jnp.concatenate([slots[mask][:, :, by_core:] for mask in masks_of[w] if mask > 1], axis=2)
             for bit in tile_bits[1:]:
                 arrived.append(swap(held, "tile", bit))
                 held = jnp.concatenate([held, arrived[-1]], axis=2)
@@ -285,6 +285,10 @@
             for w in landing:
                 slots.update(zip(masks_of[w], flat))
                 flat = flat[len(masks_of[w]) :]
+            if 0 in landing and by_tile:
+                first = by_core + lax.axis_index("tile") // 2 * by_tile
+                mine = lax.dynamic_slice_in_dim(slots[1], first, by_tile, 2)
+                slots[1] = jnp.concatenate([slots[1][:, :, :by_core], mine], axis=2)
         for w in landing:
             if w + 1 < waves:
                 coming["wave", w + 1] = wave(w + 1)

time: 92.3 us -> 91.2 us (0.988)
  starting transfers between devices: 23.6 us -> 21.6 us
  waiting for transfers between devices: 31.3 us -> 32.5 us
  local copies, waits for them, and re-layouts: 6.25 us -> 5.3 us
    ppermute x19, starting transfers between devices: 23.6 us -> 21.6 us  [swap(): return lax.ppermute(value, axis, [(i, i ^ 1 << bit) for i in range(size)])]
    ppermute x19, waiting for transfers between devices: 31.3 us -> 32.5 us  [swap(): return lax.ppermute(value, axis, [(i, i ^ 1 << bit) for i in range(size)])]
    add x2, other arithmetic: 0.05 us -> 1 us  [halve(): return kept + swap(away, axis, bit)]
    slice x7 -> x6, local copies, waits for them, and re-layouts: 1.03 us -> 0.08 us  [passing(): slots[mask][:, :, by_core:]]
    unnamed x31 -> x35, local copies, waits for them, and re-layouts: 4.41 us -> 4.37 us
  transfers between devices with their start and end apart: 19 -> 19, of which waited for: 13 -> 11; matrix products, arithmetic and copies ran while one was open for 6% -> 5% of each run, Pallas kernels for 13% -> 13%
where the time goes in v4:
time: 91.2 us; the launch traced here: 90.8 us
  waiting for transfers between devices  32.5 us (36%)
  Pallas kernels  25 us (27%)
  starting transfers between devices  21.6 us (24%)
  local copies, waits for them, and re-layouts  5.3 us (6%)
  other arithmetic  5.24 us (6%)
  between operations  1.05 us (1%)
    ppermute x19, waiting for transfers between devices, swap(): return lax.ppermute(value, axis, [(i, i ^ 1 << bit) for i in range(size)])  32.5 us
    ppermute x19, starting transfers between devices, swap(): return lax.ppermute(value, axis, [(i, i ^ 1 << bit) for i in range(size)])  21.6 us
    pallas_call x1, Pallas kernels, local_gram(): pl.pallas_call(functools.partial(gram_kernel, width=width, norm=norm), in...  12.1 us
    pallas_call x1, Pallas kernels, pair_contraction(): pl.pallas_call(functools.partial(pair_kernel, depths=depths, scale=scale)...  10.3 us
    unnamed x35, local copies, waits for them, and re-layouts  4.37 us
    pallas_call x1, Pallas kernels, deal(): pl.pallas_call(functools.partial(deal_kernel, by_core=by_core, by_tile=by...  2.64 us
    broadcast_in_dim x1, other arithmetic, per_device(): return (elementals, (kept + swap(away, 'tile', 0))[None])  1.9 us
  transfers between devices with their start and end apart: 19, of which 11 were waited for; matrix products, arithmetic and copies ran while one was open for 5% of the time, Pallas kernels for 13%

profile of v4, /device:TPU:0, one launch (start us, length us, event | category | flops | bytes accessed | tf_op | source)
XLA Modules:
  0.0 90.8 jit_solution(6808868905499329854)
XLA Ops:
  0.6 2.6 %deal.1 = (f32[2,4,40,256]{3,2,1,0:T(8,128)}, f32[2,4,64,256]{3,2,1,0:T(8,128)}) custom-call(f32[2,128,1024]{2,1,0:T(8,128)} %tau.1), custom_call_target="tpu_custom_call" | custom-call | tf_op jit(solution)/shard_map/deal/pallas_call | solution.py:227
  3.3 4.1 %collective-permute-start.2 = (f32[2,4,40,256]{3,2,1,0:T(8,128)}, f32[2,4,40,256]{3,2,1,0:T(8,128)S(1)}, u32[]{:S(2)}, u32[]{:S(2)}) collective-permute-start(f32[2,4,40,256]{3,2,1,0:T(8,128)} %get-tuple-element.28.refs_0_), channel_id=1, source_target_pairs={{0,16},{4,20},{8,24},{12,28},{16,0},{20,4},{24,8},{28,12},{1,17},{... | collective-permute-start | bytes 983048 | tf_op jit(solution)/shard_map/ppermute | solution.py:135
  7.4 1.6 %collective-permute-start.1 = (f32[2,4,40,256]{3,2,1,0:T(8,128)}, f32[2,4,40,256]{3,2,1,0:T(8,128)S(1)}, u32[]{:S(2)}, u32[]{:S(2)}) collective-permute-start(f32[2,4,40,256]{3,2,1,0:T(8,128)} %get-tuple-element.28.refs_0_), channel_id=1, source_target_pairs={{0,8},{4,12},{8,0},{12,4},{16,24},{20,28},{24,16},{28,20},{1,9},{5... | collective-permute-start | bytes 983048 | tf_op jit(solution)/shard_map/ppermute | solution.py:135
  9.0 1.5 %collective-permute-start = (f32[2,4,64,256]{3,2,1,0:T(8,128)}, f32[2,4,64,256]{3,2,1,0:T(8,128)S(1)}, u32[]{:S(2)}, u32[]{:S(2)}) collective-permute-start(f32[2,4,64,256]{3,2,1,0:T(8,128)} %get-tuple-element.31.refs_0_), channel_id=1, source_target_pairs={{0,4},{4,0},{8,12},{12,8},{16,20},{20,16},{24,28},{28,24},{1,5},{5... | collective-permute-start | bytes 1572872 | tf_op jit(solution)/shard_map/ppermute | solution.py:135
  10.4 12.1 %local_gram.1 = (f32[1,2,256,256]{3,2,1,0:T(8,128)}, f32[1,2,256,256]{3,2,1,0:T(8,128)}) custom-call(s32[2,3]{1,0:T(2,128)} %momenta.1, f32[2,3,256,1024]{3,2,1,0:T(8,128)} %bitcast.11, f32[2,4,40,256]{3,2,1,0:T(8,128)} %get-tuple-element.28.refs_0_), custom_call_target="tpu_custom_call" | custom-call | flops 9663676416 | bytes 6291456 | tf_op jit(solution)/shard_map/local_gram/pallas_call | solution.py:100
  22.6 1.0 %copy-done.11 = f32[1,2,256,256]{3,2,1,0:T(8,128)S(1)} copy-done((f32[1,2,256,256]{3,2,1,0:T(8,128)S(1)}, f32[1,2,256,256]{3,2,1,0:T(8,128)}, u32[]{:S(2)}) %copy-start.11) | copy-done | bytes 524312
  23.9 1.7 %collective-permute-done.3 = f32[512,256]{1,0:T(8,128)S(1)} collective-permute-done((f32[512,256]{1,0:T(8,128)S(1)}, f32[512,256]{1,0:T(8,128)S(1)}, u32[]{:S(2)}, u32[]{:S(2)}) %collective-permute-start.3) | collective-permute-done | bytes 524320 | tf_op jit(solution)/shard_map/ppermute | solution.py:135
  25.6 1.1 %bitcast_add_fusion = f32[512,256]{1,0:T(8,128)S(1)} fusion(f32[512,256]{1,0:T(8,128)S(1)} %collective-permute-done.3, f32[1,2,256,256]{3,2,1,0:T(8,128)} %get-tuple-element.29), kind=kLoop, calls=%fused_computation.3 | loop fusion | flops 131072 | bytes 1572864 | tf_op jit(solution)/shard_map/add | solution.py:313
  26.7 0.7 constant_dynamic-slice_fusion.4
  27.4 1.6 %collective-permute-start.4 = (f32[256,256]{1,0:T(8,128)}, f32[256,256]{1,0:T(8,128)}, u32[]{:S(2)}, u32[]{:S(2)}) collective-permute-start(f32[256,256]{1,0:T(8,128)} %constant_dynamic-slice_fusion.4), channel_id=1, source_target_pairs={{0,2},{1,3},{2,0},{3,1},{4,6},{5,7},{6,4},{7,5},{8,10},{9,11},{10,... | collective-permute-start | bytes 786440 | tf_op jit(solution)/shard_map/ppermute | solution.py:135
  29.3 1.5 %collective-permute-start.6 = (f32[2,4,40,256]{3,2,1,0:T(8,128)S(1)}, f32[2,4,40,256]{3,2,1,0:T(8,128)S(1)}, u32[]{:S(2)}, u32[]{:S(2)}) collective-permute-start(f32[2,4,40,256]{3,2,1,0:T(8,128)S(1)} %get-tuple-element.33.refs_3_), channel_id=1, source_target_pairs={{0,8},{4,12},{8,0},{12,4},{16,24},{20,28},{24,16},{28,20},{1,9},{5... | collective-permute-start | bytes 983048 | tf_op jit(solution)/shard_map/ppermute | solution.py:135
  30.8 1.5 %collective-permute-start.5 = (f32[2,4,40,256]{3,2,1,0:T(8,128)S(1)}, f32[2,4,40,256]{3,2,1,0:T(8,128)S(1)}, u32[]{:S(2)}, u32[]{:S(2)}) collective-permute-start(f32[2,4,40,256]{3,2,1,0:T(8,128)S(1)} %get-tuple-element.33.refs_3_), channel_id=1, source_target_pairs={{0,4},{4,0},{8,12},{12,8},{16,20},{20,16},{24,28},{28,24},{1,5},{5... | collective-permute-start | bytes 983048 | tf_op jit(solution)/shard_map/ppermute | solution.py:135
  32.9 4.0 %collective-permute-done.4 = f32[256,256]{1,0:T(8,128)} collective-permute-done((f32[256,256]{1,0:T(8,128)}, f32[256,256]{1,0:T(8,128)}, u32[]{:S(2)}, u32[]{:S(2)}) %collective-permute-start.4) | collective-permute-done | bytes 262176 | tf_op jit(solution)/shard_map/ppermute | solution.py:135
  36.9 1.0 %dynamic-slice_add_fusion.refs_0_ = f32[256,256]{1,0:T(8,128)S(1)} fusion(f32[256,256]{1,0:T(8,128)} %collective-permute-done.4, f32[512,256]{1,0:T(8,128)S(1)} %bitcast_add_fusion, s32[]{:T(128)S(6)} %select_n.86), kind=kLoop, calls=%fused_computation.10 | loop fusion | flops 65536 | bytes 786436 | tf_op jit(solution)/shard_map/add | solution.py:152
  37.9 0.9 %collective-permute-done.6.refs_2_ = f32[2,4,40,256]{3,2,1,0:T(8,128)S(1)} collective-permute-done((f32[2,4,40,256]{3,2,1,0:T(8,128)S(1)}, f32[2,4,40,256]{3,2,1,0:T(8,128)S(1)}, u32[]{:S(2)}, u32[]{:S(2)}) %collective-permute-start.6) | collective-permute-done | bytes 327712 | tf_op jit(solution)/shard_map/ppermute | solution.py:135
  38.8 1.2 %collective-permute-done.5.refs_1_ = f32[2,4,40,256]{3,2,1,0:T(8,128)S(1)} collective-permute-done((f32[2,4,40,256]{3,2,1,0:T(8,128)S(1)}, f32[2,4,40,256]{3,2,1,0:T(8,128)S(1)}, u32[]{:S(2)}, u32[]{:S(2)}) %collective-permute-start.5) | collective-permute-done | bytes 327712 | tf_op jit(solution)/shard_map/ppermute | solution.py:135
  40.0 1.6 %collective-permute-start.7 = (f32[128,256]{1,0:T(8,128)S(1)}, f32[128,256]{1,0:T(8,128)S(1)}, u32[]{:S(2)}, u32[]{:S(2)}) collective-permute-start(f32[128,256]{1,0:T(8,128)S(1)} %constant_dynamic-slice_fusion.3), channel_id=1, source_target_pairs={{0,4},{4,0},{8,12},{12,8},{16,20},{20,16},{24,28},{28,24},{1,5},{5... | collective-permute-start | bytes 393224 | tf_op jit(solution)/shard_map/ppermute | solution.py:135
  42.9 3.4 %collective-permute-done.7 = f32[128,256]{1,0:T(8,128)S(1)} collective-permute-done((f32[128,256]{1,0:T(8,128)S(1)}, f32[128,256]{1,0:T(8,128)S(1)}, u32[]{:S(2)}, u32[]{:S(2)}) %collective-permute-start.7) | collective-permute-done | bytes 131104 | tf_op jit(solution)/shard_map/ppermute | solution.py:135
  47.5 5.0 %collective-permute-done.9 = f32[128,256]{1,0:T(8,128)S(1)} collective-permute-done((f32[128,256]{1,0:T(8,128)S(1)}, f32[128,256]{1,0:T(8,128)S(1)}, u32[]{:S(2)}, u32[]{:S(2)}) %collective-permute-start.9) | collective-permute-done | bytes 131104 | tf_op jit(solution)/shard_map/ppermute | solution.py:135
  52.7 0.9 pad_maximum_fusion.2
  54.1 2.3 %collective-permute-start.12 = (f32[128,256]{1,0:T(8,128)S(1)}, f32[128,256]{1,0:T(8,128)S(1)}, u32[]{:S(2)}, u32[]{:S(2)}) collective-permute-start(f32[128,256]{1,0:T(8,128)S(1)} %get-tuple-element.41), channel_id=1, source_target_pairs={{0,16},{4,20},{8,24},{12,28},{16,0},{20,4},{24,8},{28,12},{1,17},{... | collective-permute-start | bytes 393224 | tf_op jit(solution)/shard_map/ppermute | solution.py:135
  56.4 4.9 %collective-permute-done.12 = f32[128,256]{1,0:T(8,128)S(1)} collective-permute-done((f32[128,256]{1,0:T(8,128)S(1)}, f32[128,256]{1,0:T(8,128)S(1)}, u32[]{:S(2)}, u32[]{:S(2)}) %collective-permute-start.12) | collective-permute-done | bytes 131104 | tf_op jit(solution)/shard_map/ppermute | solution.py:135
  61.4 0.7 copy-done.9
  62.1 0.8 collective-permute-start.14
  62.9 4.2 %collective-permute-done.14 = f32[128,256]{1,0:T(8,128)S(1)} collective-permute-done((f32[128,256]{1,0:T(8,128)S(1)}, f32[128,256]{1,0:T(8,128)S(1)}, u32[]{:S(2)}, u32[]{:S(2)}) %collective-permute-start.14) | collective-permute-done | bytes 131104 | tf_op jit(solution)/shard_map/ppermute | solution.py:135
  67.1 1.6 %collective-permute-start.16 = (f32[256,256]{1,0:T(8,128)S(1)}, f32[256,256]{1,0:T(8,128)S(1)}, u32[]{:S(2)}, u32[]{:S(2)}) collective-permute-start(f32[256,256]{1,0:T(8,128)S(1)} %get-tuple-element.46), channel_id=1, source_target_pairs={{0,2},{1,3},{2,0},{3,1},{4,6},{5,7},{6,4},{7,5},{8,10},{9,11},{10,... | collective-permute-start | bytes 786440 | tf_op jit(solution)/shard_map/ppermute | solution.py:135
  68.7 4.9 %collective-permute-done.16 = f32[256,256]{1,0:T(8,128)S(1)} collective-permute-done((f32[256,256]{1,0:T(8,128)S(1)}, f32[256,256]{1,0:T(8,128)S(1)}, u32[]{:S(2)}, u32[]{:S(2)}) %collective-permute-start.16) | collective-permute-done | bytes 262176 | tf_op jit(solution)/shard_map/ppermute | solution.py:135
  73.7 1.9 %collective-permute-done.17 = f32[512,256]{1,0:T(8,128)S(1)} collective-permute-done((f32[512,256]{1,0:T(8,128)S(1)}, f32[512,256]{1,0:T(8,128)S(1)}, u32[]{:S(2)}, u32[]{:S(2)}) %collective-permute-start.17) | collective-permute-done | bytes 524320 | tf_op jit(solution)/shard_map/ppermute | solution.py:135
  75.7 0.7 copy-done.14
  76.4 10.3 %pair_contraction.1 = (f32[2,256,256]{2,1,0:T(8,128)}, f32[2,256,256]{2,1,0:T(8,128)}, f32[2,2,64,32]{3,2,1,0:T(8,128)}) custom-call(s32[2,2]{1,0:T(2,128)} %copy-done.12, f32[1,2,256,256]{3,2,1,0:T(8,128)} %bitcast.9, f32[1,2,256,256]{3,2,1,0:T(8,128)} %bitcast.10, bf16[512,512]{1,0:T(8,128)(2,1)} %copy-done, f32[2,4,64,256]{3,2,1,0:T(8,128)} %get-tuple-element.31.refs_0_, ...), custom_call_target="tpu_custom_call" | custom-call | tf_op jit(solution)/shard_map/pair_contraction/pallas_call | solution.py:431
  86.9 1.6 %copy.27 = f32[2,2,64,32]{2,3,1,0:T(8,128)} copy(f32[2,2,64,32]{3,2,1,0:T(8,128)} %get-tuple-element.54) | data formatting | bytes 65536
  88.9 1.9 %add_bitcast_fusion = f32[1,2,256,256]{3,2,1,0:T(8,128)} fusion(f32[2,256,256]{2,1,0:T(8,128)} %get-tuple-element.52, f32[2,256,256]{2,1,0:T(8,128)S(1)} %collective-permute-done.18), kind=kLoop, calls=%fused_computation.4 | loop fusion | flops 131072 | bytes 1572864 | tf_op jit(solution)/shard_map/broadcast_in_dim | solution.py:475
  (77 shorter events, 4.9 us)
Async XLA Ops:
  3.3 19.3 %collective-permute-start.2 = (f32[2,4,40,256]{3,2,1,0:T(8,128)}, f32[2,4,40,256]{3,2,1,0:T(8,128)S(1)}, u32[]{:S(2)}, u32[]{:S(2)}) collective-permute-start(f32[2,4,40,256]{3,2,1,0:T(8,128)} %get-tuple-element.28.refs_0_), channel_id=1, source_target_pairs={{0,16},{4,20},{8,24},{12,28},{16,0},{20,4},{24,8},{28,12},{1,17},{... | collective-permute-start | bytes 983048 | tf_op jit(solution)/shard_map/ppermute | solution.py:135
  7.4 15.2 %collective-permute-start.1 = (f32[2,4,40,256]{3,2,1,0:T(8,128)}, f32[2,4,40,256]{3,2,1,0:T(8,128)S(1)}, u32[]{:S(2)}, u32[]{:S(2)}) collective-permute-start(f32[2,4,40,256]{3,2,1,0:T(8,128)} %get-tuple-element.28.refs_0_), channel_id=1, source_target_pairs={{0,8},{4,12},{8,0},{12,4},{16,24},{20,28},{24,16},{28,20},{1,9},{5... | collective-permute-start | bytes 983048 | tf_op jit(solution)/shard_map/ppermute | solution.py:135
  9.0 13.7 %collective-permute-start = (f32[2,4,64,256]{3,2,1,0:T(8,128)}, f32[2,4,64,256]{3,2,1,0:T(8,128)S(1)}, u32[]{:S(2)}, u32[]{:S(2)}) collective-permute-start(f32[2,4,64,256]{3,2,1,0:T(8,128)} %get-tuple-element.31.refs_0_), channel_id=1, source_target_pairs={{0,4},{4,0},{8,12},{12,8},{16,20},{20,16},{24,28},{28,24},{1,5},{5... | collective-permute-start | bytes 1572872 | tf_op jit(solution)/shard_map/ppermute | solution.py:135
  10.4 18.6 %copy-start.15 = (s32[32,2]{0,1:T(2,128)S(1)}, s32[32,2]{0,1:T(2,128)}, u32[]{:S(2)}) copy-start(s32[32,2]{0,1:T(2,128)} %param.7) | copy-start | bytes 772
  23.7 29.0 %copy-start.1 = (f32[2,4,64,256]{3,2,1,0:T(8,128)}, f32[2,4,64,256]{3,2,1,0:T(8,128)S(1)}, u32[]{:S(2)}) copy-start(f32[2,4,64,256]{3,2,1,0:T(8,128)S(1)} %get-tuple-element.39.refs_1_) | copy-start | bytes 1572868
  23.7 29.0 %copy-start.6 = (f32[2,4,40,256]{3,2,1,0:T(8,128)}, f32[2,4,40,256]{3,2,1,0:T(8,128)S(1)}, u32[]{:S(2)}) copy-start(f32[2,4,40,256]{3,2,1,0:T(8,128)S(1)} %get-tuple-element.33.refs_3_) | copy-start | bytes 983044
  23.7 29.0 %copy-start.7 = (f32[2,4,40,256]{3,2,1,0:T(8,128)}, f32[2,4,40,256]{3,2,1,0:T(8,128)S(1)}, u32[]{:S(2)}) copy-start(f32[2,4,40,256]{3,2,1,0:T(8,128)S(1)} %get-tuple-element.37.refs_2_) | copy-start | bytes 983044
  23.7 1.9 %collective-permute-start.3 = (f32[512,256]{1,0:T(8,128)S(1)}, f32[512,256]{1,0:T(8,128)S(1)}, u32[]{:S(2)}, u32[]{:S(2)}) collective-permute-start(f32[512,256]{1,0:T(8,128)S(1)} %get-tuple-element.32), channel_id=1, source_target_pairs={{0,1},{1,0},{2,3},{3,2},{4,5},{5,4},{6,7},{7,6},{8,9},{9,8},{10,11... | collective-permute-start | bytes 1572872 | tf_op jit(solution)/shard_map/ppermute | solution.py:135
  27.4 9.5 %collective-permute-start.4 = (f32[256,256]{1,0:T(8,128)}, f32[256,256]{1,0:T(8,128)}, u32[]{:S(2)}, u32[]{:S(2)}) collective-permute-start(f32[256,256]{1,0:T(8,128)} %constant_dynamic-slice_fusion.4), channel_id=1, source_target_pairs={{0,2},{1,3},{2,0},{3,1},{4,6},{5,7},{6,4},{7,5},{8,10},{9,11},{10,... | collective-permute-start | bytes 786440 | tf_op jit(solution)/shard_map/ppermute | solution.py:135
  29.3 9.5 %collective-permute-start.6 = (f32[2,4,40,256]{3,2,1,0:T(8,128)S(1)}, f32[2,4,40,256]{3,2,1,0:T(8,128)S(1)}, u32[]{:S(2)}, u32[]{:S(2)}) collective-permute-start(f32[2,4,40,256]{3,2,1,0:T(8,128)S(1)} %get-tuple-element.33.refs_3_), channel_id=1, source_target_pairs={{0,8},{4,12},{8,0},{12,4},{16,24},{20,28},{24,16},{28,20},{1,9},{5... | collective-permute-start | bytes 983048 | tf_op jit(solution)/shard_map/ppermute | solution.py:135
  30.8 9.2 %collective-permute-start.5 = (f32[2,4,40,256]{3,2,1,0:T(8,128)S(1)}, f32[2,4,40,256]{3,2,1,0:T(8,128)S(1)}, u32[]{:S(2)}, u32[]{:S(2)}) collective-permute-start(f32[2,4,40,256]{3,2,1,0:T(8,128)S(1)} %get-tuple-element.33.refs_3_), channel_id=1, source_target_pairs={{0,4},{4,0},{8,12},{12,8},{16,20},{20,16},{24,28},{28,24},{1,5},{5... | collective-permute-start | bytes 983048 | tf_op jit(solution)/shard_map/ppermute | solution.py:135
  32.3 14.1 %collective-permute-start.8 = (f32[2,4,48,256]{3,2,1,0:T(8,128)S(1)}, f32[2,4,48,256]{3,2,1,0:T(8,128)S(1)}, u32[]{:S(2)}, u32[]{:S(2)}) collective-permute-start(f32[2,4,48,256]{3,2,1,0:T(8,128)S(1)} %pad_maximum_fusion), channel_id=1, source_target_pairs={{0,2},{1,3},{2,0},{3,1},{4,6},{5,7},{6,4},{7,5},{8,10},{9,11},{10,... | collective-permute-start | bytes 1179656 | tf_op jit(solution)/shard_map/ppermute | solution.py:135
  40.0 35.6 %copy-start.2 = (f32[2,4,40,256]{3,2,1,0:T(8,128)}, f32[2,4,40,256]{3,2,1,0:T(8,128)S(1)}, u32[]{:S(2)}) copy-start(f32[2,4,40,256]{3,2,1,0:T(8,128)S(1)} %get-tuple-element.40.refs_5_) | copy-start | bytes 983044
  40.0 35.6 %copy-start.3 = (f32[2,4,40,256]{3,2,1,0:T(8,128)}, f32[2,4,40,256]{3,2,1,0:T(8,128)S(1)}, u32[]{:S(2)}) copy-start(f32[2,4,40,256]{3,2,1,0:T(8,128)S(1)} %get-tuple-element.42.refs_4_) | copy-start | bytes 983044
  40.0 6.4 %collective-permute-start.7 = (f32[128,256]{1,0:T(8,128)S(1)}, f32[128,256]{1,0:T(8,128)S(1)}, u32[]{:S(2)}, u32[]{:S(2)}) collective-permute-start(f32[128,256]{1,0:T(8,128)S(1)} %constant_dynamic-slice_fusion.3), channel_id=1, source_target_pairs={{0,4},{4,0},{8,12},{12,8},{16,20},{20,16},{24,28},{28,24},{1,5},{5... | collective-permute-start | bytes 393224 | tf_op jit(solution)/shard_map/ppermute | solution.py:135
  41.6 10.9 %collective-permute-start.10 = (f32[2,4,40,256]{3,2,1,0:T(8,128)S(1)}, f32[2,4,40,256]{3,2,1,0:T(8,128)S(1)}, u32[]{:S(2)}, u32[]{:S(2)}) collective-permute-start(f32[2,4,40,256]{3,2,1,0:T(8,128)S(1)} %pad_maximum_fusion.3), channel_id=1, source_target_pairs={{0,8},{4,12},{8,0},{12,4},{16,24},{20,28},{24,16},{28,20},{1,9},{5... | collective-permute-start | bytes 983048 | tf_op jit(solution)/shard_map/ppermute | solution.py:135
  42.3 10.2 %collective-permute-start.11 = (f32[2,4,40,256]{3,2,1,0:T(8,128)S(1)}, f32[2,4,40,256]{3,2,1,0:T(8,128)S(1)}, u32[]{:S(2)}, u32[]{:S(2)}) collective-permute-start(f32[2,4,40,256]{3,2,1,0:T(8,128)S(1)} %get-tuple-element.40.refs_5_), channel_id=1, source_target_pairs={{0,4},{4,0},{8,12},{12,8},{16,20},{20,16},{24,28},{28,24},{1,5},{5... | collective-permute-start | bytes 983048 | tf_op jit(solution)/shard_map/ppermute | solution.py:135
  46.4 29.2 %copy-start = (bf16[512,512]{1,0:T(8,128)(2,1)}, bf16[512,512]{1,0:T(8,128)(2,1)S(1)}, u32[]{:S(2)}) copy-start(bf16[512,512]{1,0:T(8,128)(2,1)S(1)} %get-tuple-element.47.order) | copy-start | bytes 1572868
  46.4 29.2 %copy-start.12 = (s32[2,2]{1,0:T(2,128)}, s32[2,2]{1,0:T(2,128)S(1)}, u32[]{:S(2)}) copy-start(s32[2,2]{1,0:T(2,128)S(1)} %get-tuple-element.35.blocks) | copy-start | bytes 52
  46.4 29.2 %copy-start.8 = (f32[2,4,48,256]{3,2,1,0:T(8,128)}, f32[2,4,48,256]{3,2,1,0:T(8,128)S(1)}, u32[]{:S(2)}) copy-start(f32[2,4,48,256]{3,2,1,0:T(8,128)S(1)} %get-tuple-element.48.refs_6_) | copy-start | bytes 1179652
  46.5 6.0 %collective-permute-start.9 = (f32[128,256]{1,0:T(8,128)S(1)}, f32[128,256]{1,0:T(8,128)S(1)}, u32[]{:S(2)}, u32[]{:S(2)}) collective-permute-start(f32[128,256]{1,0:T(8,128)S(1)} %get-tuple-element.38), channel_id=1, source_target_pairs={{0,8},{4,12},{8,0},{12,4},{16,24},{20,28},{24,16},{28,20},{1,9},{5... | collective-permute-start | bytes 393224 | tf_op jit(solution)/shard_map/ppermute | solution.py:135
  47.0 14.4 %collective-permute-start.13 = (f32[2,4,48,256]{3,2,1,0:T(8,128)S(1)}, f32[2,4,48,256]{3,2,1,0:T(8,128)S(1)}, u32[]{:S(2)}, u32[]{:S(2)}) collective-permute-start(f32[2,4,48,256]{3,2,1,0:T(8,128)S(1)} %pad_maximum_fusion.1), channel_id=1, source_target_pairs={{0,2},{1,3},{2,0},{3,1},{4,6},{5,7},{6,4},{7,5},{8,10},{9,11},{10,... | collective-permute-start | bytes 1179656 | tf_op jit(solution)/shard_map/ppermute | solution.py:135
  52.6 23.1 %copy-start.4 = (f32[2,4,40,256]{3,2,1,0:T(8,128)}, f32[2,4,40,256]{3,2,1,0:T(8,128)S(1)}, u32[]{:S(2)}) copy-start(f32[2,4,40,256]{3,2,1,0:T(8,128)S(1)} %get-tuple-element.44.refs_7_) | copy-start | bytes 983044
  52.6 23.1 %copy-start.5 = (f32[2,4,40,256]{3,2,1,0:T(8,128)}, f32[2,4,40,256]{3,2,1,0:T(8,128)S(1)}, u32[]{:S(2)}) copy-start(f32[2,4,40,256]{3,2,1,0:T(8,128)S(1)} %get-tuple-element.45.refs_8_) | copy-start | bytes 983044
  53.5 13.6 %collective-permute-start.15 = (f32[2,4,48,256]{3,2,1,0:T(8,128)}, f32[2,4,48,256]{3,2,1,0:T(8,128)S(1)}, u32[]{:S(2)}, u32[]{:S(2)}) collective-permute-start(f32[2,4,48,256]{3,2,1,0:T(8,128)} %pad_maximum_fusion.2), channel_id=1, source_target_pairs={{0,2},{1,3},{2,0},{3,1},{4,6},{5,7},{6,4},{7,5},{8,10},{9,11},{10,... | collective-permute-start | bytes 1179656 | tf_op jit(solution)/shard_map/ppermute | solution.py:135
  54.1 7.3 %collective-permute-start.12 = (f32[128,256]{1,0:T(8,128)S(1)}, f32[128,256]{1,0:T(8,128)S(1)}, u32[]{:S(2)}, u32[]{:S(2)}) collective-permute-start(f32[128,256]{1,0:T(8,128)S(1)} %get-tuple-element.41), channel_id=1, source_target_pairs={{0,16},{4,20},{8,24},{12,28},{16,0},{20,4},{24,8},{28,12},{1,17},{... | collective-permute-start | bytes 393224 | tf_op jit(solution)/shard_map/ppermute | solution.py:135
  62.1 5.0 %collective-permute-start.14 = (f32[128,256]{1,0:T(8,128)S(1)}, f32[128,256]{1,0:T(8,128)S(1)}, u32[]{:S(2)}, u32[]{:S(2)}) collective-permute-start(f32[128,256]{1,0:T(8,128)S(1)} %get-tuple-element.43), channel_id=1, source_target_pairs={{0,4},{4,0},{8,12},{12,8},{16,20},{20,16},{24,28},{28,24},{1,5},{5... | collective-permute-start | bytes 393224 | tf_op jit(solution)/shard_map/ppermute | solution.py:135
  67.1 8.5 %copy-start.10 = (f32[2,4,48,256]{3,2,1,0:T(8,128)}, f32[2,4,48,256]{3,2,1,0:T(8,128)S(1)}, u32[]{:S(2)}) copy-start(f32[2,4,48,256]{3,2,1,0:T(8,128)S(1)} %get-tuple-element.50.refs_10_) | copy-start | bytes 1179652
  67.1 6.4 %collective-permute-start.16 = (f32[256,256]{1,0:T(8,128)S(1)}, f32[256,256]{1,0:T(8,128)S(1)}, u32[]{:S(2)}, u32[]{:S(2)}) collective-permute-start(f32[256,256]{1,0:T(8,128)S(1)} %get-tuple-element.46), channel_id=1, source_target_pairs={{0,2},{1,3},{2,0},{3,1},{4,6},{5,7},{6,4},{7,5},{8,10},{9,11},{10,... | collective-permute-start | bytes 786440 | tf_op jit(solution)/shard_map/ppermute | solution.py:135
  73.6 2.1 %copy-start.13 = (f32[512,256]{1,0:T(8,128)}, f32[512,256]{1,0:T(8,128)S(1)}, u32[]{:S(2)}) copy-start(f32[512,256]{1,0:T(8,128)S(1)} %maximum_select_fusion) | copy-start | bytes 1572868
  73.6 2.0 %collective-permute-start.17 = (f32[512,256]{1,0:T(8,128)S(1)}, f32[512,256]{1,0:T(8,128)S(1)}, u32[]{:S(2)}, u32[]{:S(2)}) collective-permute-start(f32[512,256]{1,0:T(8,128)S(1)} %maximum_select_fusion), channel_id=1, source_target_pairs={{0,1},{1,0},{2,3},{3,2},{4,5},{5,4},{6,7},{7,6},{8,9},{9,8},{10,11... | collective-permute-start | bytes 1572872 | tf_op jit(solution)/shard_map/ppermute | solution.py:135
  86.7 2.2 %collective-permute-start.18 = (f32[2,256,256]{2,1,0:T(8,128)}, f32[2,256,256]{2,1,0:T(8,128)S(1)}, u32[]{:S(2)}, u32[]{:S(2)}) collective-permute-start(f32[2,256,256]{2,1,0:T(8,128)} %get-tuple-element.53), channel_id=1, source_target_pairs={{0,1},{1,0},{2,3},{3,2},{4,5},{5,4},{6,7},{7,6},{8,9},{9,8},{10,11... | collective-permute-start | bytes 1572872 | tf_op jit(solution)/shard_map/ppermute | solution.py:135
  (3 other events, 2.6 us)

commit v5 on v4

--- a/solution.py
+++ b/solution.py
@@ -14,8 +14,8 @@
 BF16 = jnp.bfloat16
 WAVE_ENDS = (-2, 0)
 PASS_ENDS = (-1, 1, 2)
-GRAM_VMEM = 55 * 1024 * 1024
-PAIR_VMEM = 58 * 1024 * 1024
+GRAM_VMEM = 53 * 1024 * 1024
+PAIR_VMEM = 48 * 1024 * 1024
 
 
 def bits_of(count):

time: 91.2 us -> 86.9 us (0.953)
  Pallas kernels: 25 us -> 21.2 us
  other arithmetic: 5.24 us -> 4.09 us
    pallas_call x1, Pallas kernels: 10.3 us -> 8.46 us  [pair_contraction(): pl.pallas_call(functools.partial(pair_kernel, depths=depths, scale=scale)...]
    pallas_call x1, Pallas kernels: 2.64 us -> 1.3 us  [deal(): pl.pallas_call(functools.partial(deal_kernel, by_core=by_core, by_tile=by...]
    broadcast_in_dim x1, other arithmetic: 1.9 us -> 0.86 us  [per_device(): return (elementals, (kept + swap(away, 'tile', 0))[None])]
    unnamed x35 -> x17, local copies, waits for them, and re-layouts: 4.37 us -> 4.59 us
  transfers between devices with their start and end apart: 19 -> 19, of which waited for: 11 -> 11; matrix products, arithmetic and copies ran while one was open for 5% -> 4% of each run, Pallas kernels for 13% -> 13%
where the time goes in v5:
time: 86.9 us; the launch traced here: 86.6 us
  waiting for transfers between devices  32.7 us (38%)
  starting transfers between devices  22.1 us (25%)
  Pallas kernels  21.2 us (24%)
  local copies, waits for them, and re-layouts  5.51 us (6%)
  other arithmetic  4.09 us (5%)
  between operations  0.98 us (1%)
    ppermute x19, waiting for transfers between devices, swap(): return lax.ppermute(value, axis, [(i, i ^ 1 << bit) for i in range(size)])  32.7 us
    ppermute x19, starting transfers between devices, swap(): return lax.ppermute(value, axis, [(i, i ^ 1 << bit) for i in range(size)])  22.1 us
    pallas_call x1, Pallas kernels, local_gram(): pl.pallas_call(functools.partial(gram_kernel, width=width, norm=norm), in...  11.4 us
    pallas_call x1, Pallas kernels, pair_contraction(): pl.pallas_call(functools.partial(pair_kernel, depths=depths, scale=scale)...  8.46 us
    unnamed x17, local copies, waits for them, and re-layouts  4.59 us
  transfers between devices with their start and end apart: 19, of which 11 were waited for; matrix products, arithmetic and copies ran while one was open for 4% of the time, Pallas kernels for 13%

profile of v5, /device:TPU:0, one launch (start us, length us, event | category | flops | bytes accessed | tf_op | source)
XLA Modules:
  0.0 86.6 jit_solution(5848097054878809428)
XLA Ops:
  0.6 1.2 %copy-done.3 = f32[2,128,1024]{2,1,0:T(8,128)S(1)} copy-done((f32[2,128,1024]{2,1,0:T(8,128)S(1)}, f32[2,128,1024]{2,1,0:T(8,128)}, u32[]{:S(2)}) %copy-start.3) | copy-done | bytes 1048600
  1.9 1.3 %deal.1 = (f32[2,4,40,256]{3,2,1,0:T(8,128)S(1)}, f32[2,4,64,256]{3,2,1,0:T(8,128)S(1)}) custom-call(f32[2,128,1024]{2,1,0:T(8,128)S(1)} %copy-done.3), custom_call_target="tpu_custom_call" | custom-call | tf_op jit(solution)/shard_map/deal/pallas_call | solution.py:227
  3.2 4.1 %collective-permute-start.2 = (f32[2,4,40,256]{3,2,1,0:T(8,128)S(1)}, f32[2,4,40,256]{3,2,1,0:T(8,128)S(1)}, u32[]{:S(2)}, u32[]{:S(2)}) collective-permute-start(f32[2,4,40,256]{3,2,1,0:T(8,128)S(1)} %get-tuple-element.28.refs_0_), channel_id=1, source_target_pairs={{0,16},{4,20},{8,24},{12,28},{16,0},{20,4},{24,8},{28,12},{1,17},{... | collective-permute-start | bytes 983048 | tf_op jit(solution)/shard_map/ppermute | solution.py:135
  7.3 1.6 %collective-permute-start.1 = (f32[2,4,40,256]{3,2,1,0:T(8,128)S(1)}, f32[2,4,40,256]{3,2,1,0:T(8,128)S(1)}, u32[]{:S(2)}, u32[]{:S(2)}) collective-permute-start(f32[2,4,40,256]{3,2,1,0:T(8,128)S(1)} %get-tuple-element.28.refs_0_), channel_id=1, source_target_pairs={{0,8},{4,12},{8,0},{12,4},{16,24},{20,28},{24,16},{28,20},{1,9},{5... | collective-permute-start | bytes 983048 | tf_op jit(solution)/shard_map/ppermute | solution.py:135
  8.8 1.5 %collective-permute-start = (f32[2,4,64,256]{3,2,1,0:T(8,128)S(1)}, f32[2,4,64,256]{3,2,1,0:T(8,128)S(1)}, u32[]{:S(2)}, u32[]{:S(2)}) collective-permute-start(f32[2,4,64,256]{3,2,1,0:T(8,128)S(1)} %get-tuple-element.31.refs_0_), channel_id=1, source_target_pairs={{0,4},{4,0},{8,12},{12,8},{16,20},{20,16},{24,28},{28,24},{1,5},{5... | collective-permute-start | bytes 1572872 | tf_op jit(solution)/shard_map/ppermute | solution.py:135
  11.0 11.4 %local_gram.1 = (f32[1,2,256,256]{3,2,1,0:T(8,128)S(1)}, f32[1,2,256,256]{3,2,1,0:T(8,128)}) custom-call(s32[2,3]{1,0:T(2,128)S(1)} %copy-done.5, f32[2,3,256,1024]{3,2,1,0:T(8,128)} %bitcast.11, f32[2,4,40,256]{3,2,1,0:T(8,128)S(1)} %get-tuple-element.28.refs_0_), custom_call_target="tpu_custom_call" | custom-call | flops 9663676416 | bytes 6291456 | tf_op jit(solution)/shard_map/local_gram/pallas_call | solution.py:100
  22.8 1.7 %collective-permute-done.3 = f32[512,256]{1,0:T(8,128)S(1)} collective-permute-done((f32[512,256]{1,0:T(8,128)S(1)}, f32[512,256]{1,0:T(8,128)S(1)}, u32[]{:S(2)}, u32[]{:S(2)}) %collective-permute-start.3) | collective-permute-done | bytes 524320 | tf_op jit(solution)/shard_map/ppermute | solution.py:135
  24.5 1.1 %bitcast_add_fusion = f32[512,256]{1,0:T(8,128)S(1)} fusion(f32[512,256]{1,0:T(8,128)S(1)} %collective-permute-done.3, f32[1,2,256,256]{3,2,1,0:T(8,128)} %get-tuple-element.29), kind=kLoop, calls=%fused_computation.3 | loop fusion | flops 131072 | bytes 1572864 | tf_op jit(solution)/shard_map/add | solution.py:313
  26.3 1.5 %collective-permute-start.4 = (f32[256,256]{1,0:T(8,128)}, f32[256,256]{1,0:T(8,128)}, u32[]{:S(2)}, u32[]{:S(2)}) collective-permute-start(f32[256,256]{1,0:T(8,128)} %constant_dynamic-slice_fusion.4), channel_id=1, source_target_pairs={{0,2},{1,3},{2,0},{3,1},{4,6},{5,7},{6,4},{7,5},{8,10},{9,11},{10,... | collective-permute-start | bytes 786440 | tf_op jit(solution)/shard_map/ppermute | solution.py:135
  28.1 1.3 %collective-permute-start.6 = (f32[2,4,40,256]{3,2,1,0:T(8,128)S(1)}, f32[2,4,40,256]{3,2,1,0:T(8,128)S(1)}, u32[]{:S(2)}, u32[]{:S(2)}) collective-permute-start(f32[2,4,40,256]{3,2,1,0:T(8,128)S(1)} %get-tuple-element.33.refs_3_), channel_id=1, source_target_pairs={{0,8},{4,12},{8,0},{12,4},{16,24},{20,28},{24,16},{28,20},{1,9},{5... | collective-permute-start | bytes 983048 | tf_op jit(solution)/shard_map/ppermute | solution.py:135
  29.4 1.5 %collective-permute-start.5 = (f32[2,4,40,256]{3,2,1,0:T(8,128)S(1)}, f32[2,4,40,256]{3,2,1,0:T(8,128)S(1)}, u32[]{:S(2)}, u32[]{:S(2)}) collective-permute-start(f32[2,4,40,256]{3,2,1,0:T(8,128)S(1)} %get-tuple-element.33.refs_3_), channel_id=1, source_target_pairs={{0,4},{4,0},{8,12},{12,8},{16,20},{20,16},{24,28},{28,24},{1,5},{5... | collective-permute-start | bytes 983048 | tf_op jit(solution)/shard_map/ppermute | solution.py:135
  31.5 4.2 %collective-permute-done.4 = f32[256,256]{1,0:T(8,128)} collective-permute-done((f32[256,256]{1,0:T(8,128)}, f32[256,256]{1,0:T(8,128)}, u32[]{:S(2)}, u32[]{:S(2)}) %collective-permute-start.4) | collective-permute-done | bytes 262176 | tf_op jit(solution)/shard_map/ppermute | solution.py:135
  35.8 1.0 %dynamic-slice_add_fusion.refs_0_ = f32[256,256]{1,0:T(8,128)S(1)} fusion(f32[256,256]{1,0:T(8,128)} %collective-permute-done.4, f32[512,256]{1,0:T(8,128)S(1)} %bitcast_add_fusion, s32[]{:T(128)S(6)} %select_n.86), kind=kLoop, calls=%fused_computation.10 | loop fusion | flops 65536 | bytes 786436 | tf_op jit(solution)/shard_map/add | solution.py:152
  36.8 0.9 %collective-permute-done.6.refs_2_ = f32[2,4,40,256]{3,2,1,0:T(8,128)S(1)} collective-permute-done((f32[2,4,40,256]{3,2,1,0:T(8,128)S(1)}, f32[2,4,40,256]{3,2,1,0:T(8,128)S(1)}, u32[]{:S(2)}, u32[]{:S(2)}) %collective-permute-start.6) | collective-permute-done | bytes 327712 | tf_op jit(solution)/shard_map/ppermute | solution.py:135
  37.7 1.0 %collective-permute-done.5.refs_1_ = f32[2,4,40,256]{3,2,1,0:T(8,128)S(1)} collective-permute-done((f32[2,4,40,256]{3,2,1,0:T(8,128)S(1)}, f32[2,4,40,256]{3,2,1,0:T(8,128)S(1)}, u32[]{:S(2)}, u32[]{:S(2)}) %collective-permute-start.5) | collective-permute-done | bytes 327712 | tf_op jit(solution)/shard_map/ppermute | solution.py:135
  38.6 1.6 %collective-permute-start.7 = (f32[128,256]{1,0:T(8,128)S(1)}, f32[128,256]{1,0:T(8,128)S(1)}, u32[]{:S(2)}, u32[]{:S(2)}) collective-permute-start(f32[128,256]{1,0:T(8,128)S(1)} %constant_dynamic-slice_fusion.3), channel_id=1, source_target_pairs={{0,4},{4,0},{8,12},{12,8},{16,20},{20,16},{24,28},{28,24},{1,5},{5... | collective-permute-start | bytes 393224 | tf_op jit(solution)/shard_map/ppermute | solution.py:135
  40.9 0.8 collective-permute-start.11
  41.7 3.3 %collective-permute-done.7 = f32[128,256]{1,0:T(8,128)S(1)} collective-permute-done((f32[128,256]{1,0:T(8,128)S(1)}, f32[128,256]{1,0:T(8,128)S(1)}, u32[]{:S(2)}, u32[]{:S(2)}) %collective-permute-start.7) | collective-permute-done | bytes 131104 | tf_op jit(solution)/shard_map/ppermute | solution.py:135
  45.1 0.8 collective-permute-start.9
  46.5 4.6 %collective-permute-done.9 = f32[128,256]{1,0:T(8,128)S(1)} collective-permute-done((f32[128,256]{1,0:T(8,128)S(1)}, f32[128,256]{1,0:T(8,128)S(1)}, u32[]{:S(2)}, u32[]{:S(2)}) %collective-permute-start.9) | collective-permute-done | bytes 131104 | tf_op jit(solution)/shard_map/ppermute | solution.py:135
  51.2 0.8 pad_maximum_fusion.2
  52.5 2.4 %collective-permute-start.12 = (f32[128,256]{1,0:T(8,128)S(1)}, f32[128,256]{1,0:T(8,128)S(1)}, u32[]{:S(2)}, u32[]{:S(2)}) collective-permute-start(f32[128,256]{1,0:T(8,128)S(1)} %get-tuple-element.41), channel_id=1, source_target_pairs={{0,16},{4,20},{8,24},{12,28},{16,0},{20,4},{24,8},{28,12},{1,17},{... | collective-permute-start | bytes 393224 | tf_op jit(solution)/shard_map/ppermute | solution.py:135
  54.9 4.9 %collective-permute-done.12 = f32[128,256]{1,0:T(8,128)S(1)} collective-permute-done((f32[128,256]{1,0:T(8,128)S(1)}, f32[128,256]{1,0:T(8,128)S(1)}, u32[]{:S(2)}, u32[]{:S(2)}) %collective-permute-start.12) | collective-permute-done | bytes 131104 | tf_op jit(solution)/shard_map/ppermute | solution.py:135
  60.6 0.8 collective-permute-start.14
  61.4 4.2 %collective-permute-done.14 = f32[128,256]{1,0:T(8,128)S(1)} collective-permute-done((f32[128,256]{1,0:T(8,128)S(1)}, f32[128,256]{1,0:T(8,128)S(1)}, u32[]{:S(2)}, u32[]{:S(2)}) %collective-permute-start.14) | collective-permute-done | bytes 131104 | tf_op jit(solution)/shard_map/ppermute | solution.py:135
  65.6 1.6 %collective-permute-start.16 = (f32[256,256]{1,0:T(8,128)S(1)}, f32[256,256]{1,0:T(8,128)S(1)}, u32[]{:S(2)}, u32[]{:S(2)}) collective-permute-start(f32[256,256]{1,0:T(8,128)S(1)} %get-tuple-element.46), channel_id=1, source_target_pairs={{0,2},{1,3},{2,0},{3,1},{4,6},{5,7},{6,4},{7,5},{8,10},{9,11},{10,... | collective-permute-start | bytes 786440 | tf_op jit(solution)/shard_map/ppermute | solution.py:135
  67.2 4.9 %collective-permute-done.16 = f32[256,256]{1,0:T(8,128)S(1)} collective-permute-done((f32[256,256]{1,0:T(8,128)S(1)}, f32[256,256]{1,0:T(8,128)S(1)}, u32[]{:S(2)}, u32[]{:S(2)}) %collective-permute-start.16) | collective-permute-done | bytes 262176 | tf_op jit(solution)/shard_map/ppermute | solution.py:135
  72.2 1.9 %collective-permute-done.17 = f32[512,256]{1,0:T(8,128)S(1)} collective-permute-done((f32[512,256]{1,0:T(8,128)S(1)}, f32[512,256]{1,0:T(8,128)S(1)}, u32[]{:S(2)}, u32[]{:S(2)}) %collective-permute-start.17) | collective-permute-done | bytes 524320 | tf_op jit(solution)/shard_map/ppermute | solution.py:135
  74.1 1.0 %copy-done.2 = f32[2,4,48,256]{3,2,1,0:T(8,128)S(1)} copy-done((f32[2,4,48,256]{3,2,1,0:T(8,128)S(1)}, f32[2,4,48,256]{3,2,1,0:T(8,128)}, u32[]{:S(2)}) %copy-start.2) | copy-done | bytes 393240
  75.1 8.5 %pair_contraction.1 = (f32[2,256,256]{2,1,0:T(8,128)}, f32[2,256,256]{2,1,0:T(8,128)S(1)}, f32[2,2,64,32]{3,2,1,0:T(8,128)S(1)}) custom-call(s32[2,2]{1,0:T(2,128)S(1)} %get-tuple-element.35.blocks, f32[1,2,256,256]{3,2,1,0:T(8,128)S(1)} %bitcast.8, f32[1,2,256,256]{3,2,1,0:T(8,128)S(1)} %bitcast.9, bf16[512,512]{1,0:T(8,128)(2,1)S(1)} %get-tuple-element.47.order, ...), custom_call_target="tpu_custom_call" | custom-call | tf_op jit(solution)/shard_map/pair_contraction/pallas_call | solution.py:431
  84.5 1.3 %collective-permute-done.18 = f32[2,256,256]{2,1,0:T(8,128)S(1)} collective-permute-done((f32[2,256,256]{2,1,0:T(8,128)}, f32[2,256,256]{2,1,0:T(8,128)S(1)}, u32[]{:S(2)}, u32[]{:S(2)}) %collective-permute-start.18) | collective-permute-done | bytes 524320 | tf_op jit(solution)/shard_map/ppermute | solution.py:135
  85.7 0.9 add_bitcast_fusion
  (59 shorter events, 6.4 us)
Async XLA Ops:
  0.6 1.2 %copy-start.3 = (f32[2,128,1024]{2,1,0:T(8,128)S(1)}, f32[2,128,1024]{2,1,0:T(8,128)}, u32[]{:S(2)}) copy-start(f32[2,128,1024]{2,1,0:T(8,128)} %tau.1) | copy-start | bytes 3145732
  3.2 19.3 %copy-start.4 = (f32[2,4,64,256]{3,2,1,0:T(8,128)}, f32[2,4,64,256]{3,2,1,0:T(8,128)S(1)}, u32[]{:S(2)}) copy-start(f32[2,4,64,256]{3,2,1,0:T(8,128)S(1)} %get-tuple-element.31.refs_0_) | copy-start | bytes 1572868
  3.2 19.3 %collective-permute-start.2 = (f32[2,4,40,256]{3,2,1,0:T(8,128)S(1)}, f32[2,4,40,256]{3,2,1,0:T(8,128)S(1)}, u32[]{:S(2)}, u32[]{:S(2)}) collective-permute-start(f32[2,4,40,256]{3,2,1,0:T(8,128)S(1)} %get-tuple-element.28.refs_0_), channel_id=1, source_target_pairs={{0,16},{4,20},{8,24},{12,28},{16,0},{20,4},{24,8},{28,12},{1,17},{... | collective-permute-start | bytes 983048 | tf_op jit(solution)/shard_map/ppermute | solution.py:135
  7.3 15.2 %collective-permute-start.1 = (f32[2,4,40,256]{3,2,1,0:T(8,128)S(1)}, f32[2,4,40,256]{3,2,1,0:T(8,128)S(1)}, u32[]{:S(2)}, u32[]{:S(2)}) collective-permute-start(f32[2,4,40,256]{3,2,1,0:T(8,128)S(1)} %get-tuple-element.28.refs_0_), channel_id=1, source_target_pairs={{0,8},{4,12},{8,0},{12,4},{16,24},{20,28},{24,16},{28,20},{1,9},{5... | collective-permute-start | bytes 983048 | tf_op jit(solution)/shard_map/ppermute | solution.py:135
  8.8 13.6 %collective-permute-start = (f32[2,4,64,256]{3,2,1,0:T(8,128)S(1)}, f32[2,4,64,256]{3,2,1,0:T(8,128)S(1)}, u32[]{:S(2)}, u32[]{:S(2)}) collective-permute-start(f32[2,4,64,256]{3,2,1,0:T(8,128)S(1)} %get-tuple-element.31.refs_0_), channel_id=1, source_target_pairs={{0,4},{4,0},{8,12},{12,8},{16,20},{20,16},{24,28},{28,24},{1,5},{5... | collective-permute-start | bytes 1572872 | tf_op jit(solution)/shard_map/ppermute | solution.py:135
  10.3 0.7 copy-start.5
  11.0 16.8 %copy-start.6 = (s32[32,2]{0,1:T(2,128)S(1)}, s32[32,2]{0,1:T(2,128)}, u32[]{:S(2)}) copy-start(s32[32,2]{0,1:T(2,128)} %param.7) | copy-start | bytes 772
  22.5 28.7 %copy-start = (f32[2,4,64,256]{3,2,1,0:T(8,128)}, f32[2,4,64,256]{3,2,1,0:T(8,128)S(1)}, u32[]{:S(2)}) copy-start(f32[2,4,64,256]{3,2,1,0:T(8,128)S(1)} %get-tuple-element.39.refs_1_) | copy-start | bytes 1572868
  22.5 2.0 %collective-permute-start.3 = (f32[512,256]{1,0:T(8,128)S(1)}, f32[512,256]{1,0:T(8,128)S(1)}, u32[]{:S(2)}, u32[]{:S(2)}) collective-permute-start(f32[512,256]{1,0:T(8,128)S(1)} %get-tuple-element.32), channel_id=1, source_target_pairs={{0,1},{1,0},{2,3},{3,2},{4,5},{5,4},{6,7},{7,6},{8,9},{9,8},{10,11... | collective-permute-start | bytes 1572872 | tf_op jit(solution)/shard_map/ppermute | solution.py:135
  26.3 9.5 %collective-permute-start.4 = (f32[256,256]{1,0:T(8,128)}, f32[256,256]{1,0:T(8,128)}, u32[]{:S(2)}, u32[]{:S(2)}) collective-permute-start(f32[256,256]{1,0:T(8,128)} %constant_dynamic-slice_fusion.4), channel_id=1, source_target_pairs={{0,2},{1,3},{2,0},{3,1},{4,6},{5,7},{6,4},{7,5},{8,10},{9,11},{10,... | collective-permute-start | bytes 786440 | tf_op jit(solution)/shard_map/ppermute | solution.py:135
  28.1 9.5 %collective-permute-start.6 = (f32[2,4,40,256]{3,2,1,0:T(8,128)S(1)}, f32[2,4,40,256]{3,2,1,0:T(8,128)S(1)}, u32[]{:S(2)}, u32[]{:S(2)}) collective-permute-start(f32[2,4,40,256]{3,2,1,0:T(8,128)S(1)} %get-tuple-element.33.refs_3_), channel_id=1, source_target_pairs={{0,8},{4,12},{8,0},{12,4},{16,24},{20,28},{24,16},{28,20},{1,9},{5... | collective-permute-start | bytes 983048 | tf_op jit(solution)/shard_map/ppermute | solution.py:135
  29.4 9.2 %collective-permute-start.5 = (f32[2,4,40,256]{3,2,1,0:T(8,128)S(1)}, f32[2,4,40,256]{3,2,1,0:T(8,128)S(1)}, u32[]{:S(2)}, u32[]{:S(2)}) collective-permute-start(f32[2,4,40,256]{3,2,1,0:T(8,128)S(1)} %get-tuple-element.33.refs_3_), channel_id=1, source_target_pairs={{0,4},{4,0},{8,12},{12,8},{16,20},{20,16},{24,28},{28,24},{1,5},{5... | collective-permute-start | bytes 983048 | tf_op jit(solution)/shard_map/ppermute | solution.py:135
  31.0 14.1 %collective-permute-start.8 = (f32[2,4,48,256]{3,2,1,0:T(8,128)S(1)}, f32[2,4,48,256]{3,2,1,0:T(8,128)S(1)}, u32[]{:S(2)}, u32[]{:S(2)}) collective-permute-start(f32[2,4,48,256]{3,2,1,0:T(8,128)S(1)} %pad_maximum_fusion), channel_id=1, source_target_pairs={{0,2},{1,3},{2,0},{3,1},{4,6},{5,7},{6,4},{7,5},{8,10},{9,11},{10,... | collective-permute-start | bytes 1179656 | tf_op jit(solution)/shard_map/ppermute | solution.py:135
  38.6 6.4 %collective-permute-start.7 = (f32[128,256]{1,0:T(8,128)S(1)}, f32[128,256]{1,0:T(8,128)S(1)}, u32[]{:S(2)}, u32[]{:S(2)}) collective-permute-start(f32[128,256]{1,0:T(8,128)S(1)} %constant_dynamic-slice_fusion.3), channel_id=1, source_target_pairs={{0,4},{4,0},{8,12},{12,8},{16,20},{20,16},{24,28},{28,24},{1,5},{5... | collective-permute-start | bytes 393224 | tf_op jit(solution)/shard_map/ppermute | solution.py:135
  40.3 10.9 %collective-permute-start.10 = (f32[2,4,40,256]{3,2,1,0:T(8,128)S(1)}, f32[2,4,40,256]{3,2,1,0:T(8,128)S(1)}, u32[]{:S(2)}, u32[]{:S(2)}) collective-permute-start(f32[2,4,40,256]{3,2,1,0:T(8,128)S(1)} %pad_maximum_fusion.3), channel_id=1, source_target_pairs={{0,8},{4,12},{8,0},{12,4},{16,24},{20,28},{24,16},{28,20},{1,9},{5... | collective-permute-start | bytes 983048 | tf_op jit(solution)/shard_map/ppermute | solution.py:135
  40.9 10.2 %collective-permute-start.11 = (f32[2,4,40,256]{3,2,1,0:T(8,128)S(1)}, f32[2,4,40,256]{3,2,1,0:T(8,128)S(1)}, u32[]{:S(2)}, u32[]{:S(2)}) collective-permute-start(f32[2,4,40,256]{3,2,1,0:T(8,128)S(1)} %get-tuple-element.40.refs_5_), channel_id=1, source_target_pairs={{0,4},{4,0},{8,12},{12,8},{16,20},{20,16},{24,28},{28,24},{1,5},{5... | collective-permute-start | bytes 983048 | tf_op jit(solution)/shard_map/ppermute | solution.py:135
  45.1 6.1 %collective-permute-start.9 = (f32[128,256]{1,0:T(8,128)S(1)}, f32[128,256]{1,0:T(8,128)S(1)}, u32[]{:S(2)}, u32[]{:S(2)}) collective-permute-start(f32[128,256]{1,0:T(8,128)S(1)} %get-tuple-element.38), channel_id=1, source_target_pairs={{0,8},{4,12},{8,0},{12,4},{16,24},{20,28},{24,16},{28,20},{1,9},{5... | collective-permute-start | bytes 393224 | tf_op jit(solution)/shard_map/ppermute | solution.py:135
  45.9 13.9 %collective-permute-start.13 = (f32[2,4,48,256]{3,2,1,0:T(8,128)S(1)}, f32[2,4,48,256]{3,2,1,0:T(8,128)S(1)}, u32[]{:S(2)}, u32[]{:S(2)}) collective-permute-start(f32[2,4,48,256]{3,2,1,0:T(8,128)S(1)} %pad_maximum_fusion.1), channel_id=1, source_target_pairs={{0,2},{1,3},{2,0},{3,1},{4,6},{5,7},{6,4},{7,5},{8,10},{9,11},{10,... | collective-permute-start | bytes 1179656 | tf_op jit(solution)/shard_map/ppermute | solution.py:135
  52.0 13.6 %collective-permute-start.15 = (f32[2,4,48,256]{3,2,1,0:T(8,128)}, f32[2,4,48,256]{3,2,1,0:T(8,128)}, u32[]{:S(2)}, u32[]{:S(2)}) collective-permute-start(f32[2,4,48,256]{3,2,1,0:T(8,128)} %pad_maximum_fusion.2), channel_id=1, source_target_pairs={{0,2},{1,3},{2,0},{3,1},{4,6},{5,7},{6,4},{7,5},{8,10},{9,11},{10,... | collective-permute-start | bytes 1179656 | tf_op jit(solution)/shard_map/ppermute | solution.py:135
  52.5 7.3 %collective-permute-start.12 = (f32[128,256]{1,0:T(8,128)S(1)}, f32[128,256]{1,0:T(8,128)S(1)}, u32[]{:S(2)}, u32[]{:S(2)}) collective-permute-start(f32[128,256]{1,0:T(8,128)S(1)} %get-tuple-element.41), channel_id=1, source_target_pairs={{0,16},{4,20},{8,24},{12,28},{16,0},{20,4},{24,8},{28,12},{1,17},{... | collective-permute-start | bytes 393224 | tf_op jit(solution)/shard_map/ppermute | solution.py:135
  59.8 0.8 copy-start.1
  60.6 5.0 %collective-permute-start.14 = (f32[128,256]{1,0:T(8,128)S(1)}, f32[128,256]{1,0:T(8,128)S(1)}, u32[]{:S(2)}, u32[]{:S(2)}) collective-permute-start(f32[128,256]{1,0:T(8,128)S(1)} %get-tuple-element.43), channel_id=1, source_target_pairs={{0,4},{4,0},{8,12},{12,8},{16,20},{20,16},{24,28},{28,24},{1,5},{5... | collective-permute-start | bytes 393224 | tf_op jit(solution)/shard_map/ppermute | solution.py:135
  65.6 6.4 %collective-permute-start.16 = (f32[256,256]{1,0:T(8,128)S(1)}, f32[256,256]{1,0:T(8,128)S(1)}, u32[]{:S(2)}, u32[]{:S(2)}) collective-permute-start(f32[256,256]{1,0:T(8,128)S(1)} %get-tuple-element.46), channel_id=1, source_target_pairs={{0,2},{1,3},{2,0},{3,1},{4,6},{5,7},{6,4},{7,5},{8,10},{9,11},{10,... | collective-permute-start | bytes 786440 | tf_op jit(solution)/shard_map/ppermute | solution.py:135
  72.1 2.0 %collective-permute-start.17 = (f32[512,256]{1,0:T(8,128)S(1)}, f32[512,256]{1,0:T(8,128)S(1)}, u32[]{:S(2)}, u32[]{:S(2)}) collective-permute-start(f32[512,256]{1,0:T(8,128)S(1)} %maximum_select_fusion), channel_id=1, source_target_pairs={{0,1},{1,0},{2,3},{3,2},{4,5},{5,4},{6,7},{7,6},{8,9},{9,8},{10,11... | collective-permute-start | bytes 1572872 | tf_op jit(solution)/shard_map/ppermute | solution.py:135
  74.1 1.0 %copy-start.2 = (f32[2,4,48,256]{3,2,1,0:T(8,128)S(1)}, f32[2,4,48,256]{3,2,1,0:T(8,128)}, u32[]{:S(2)}) copy-start(f32[2,4,48,256]{3,2,1,0:T(8,128)} %copy-done.1) | copy-start | bytes 1179652
  83.6 2.2 %collective-permute-start.18 = (f32[2,256,256]{2,1,0:T(8,128)}, f32[2,256,256]{2,1,0:T(8,128)S(1)}, u32[]{:S(2)}, u32[]{:S(2)}) collective-permute-start(f32[2,256,256]{2,1,0:T(8,128)} %get-tuple-element.53), channel_id=1, source_target_pairs={{0,1},{1,0},{2,3},{3,2},{4,5},{5,4},{6,7},{7,6},{8,9},{9,8},{10,11... | collective-permute-start | bytes 1572872 | tf_op jit(solution)/shard_map/ppermute | solution.py:135

commit v6 on v5

--- a/solution.py
+++ b/solution.py
@@ -297,7 +297,7 @@
 
     steps = [(halve, "tile", b) for b in tile_bits[1:]]
     steps += [(halve, "space", b) for b in space_bits[:1]]
-    steps += [(both, "space", b) for b in space_bits[1:]]
+    steps += [(both, "space", b) for b in space_bits[:0:-1]]
     middle = len(steps) - 2
     steps += [(double, axis, b) for step, axis, b in steps[::-1] if step is halve]
 

time: 86.9 us -> 86.3 us (level)
  waiting for transfers between devices: 32.7 us -> 29.9 us
  starting transfers between devices: 22.1 us -> 24.4 us
    ppermute x19, waiting for transfers between devices: 32.7 us -> 29.9 us  [swap(): return lax.ppermute(value, axis, [(i, i ^ 1 << bit) for i in range(size)])]
    ppermute x19, starting transfers between devices: 22.1 us -> 24.4 us  [swap(): return lax.ppermute(value, axis, [(i, i ^ 1 << bit) for i in range(size)])]
  transfers between devices with their start and end apart: 19 -> 19, of which waited for: 11 -> 12; matrix products, arithmetic and copies ran while one was open for 4% -> 4% of each run, Pallas kernels for 13% -> 13%
where the time goes in v6:
time: 86.3 us; the launch traced here: 86 us
  waiting for transfers between devices  29.9 us (35%)
  starting transfers between devices  24.4 us (28%)
  Pallas kernels  21.2 us (25%)
  local copies, waits for them, and re-layouts  5.52 us (6%)
  other arithmetic  4.09 us (5%)
  between operations  0.95 us (1%)
    ppermute x19, waiting for transfers between devices, swap(): return lax.ppermute(value, axis, [(i, i ^ 1 << bit) for i in range(size)])  29.9 us
    ppermute x19, starting transfers between devices, swap(): return lax.ppermute(value, axis, [(i, i ^ 1 << bit) for i in range(size)])  24.4 us
    pallas_call x1, Pallas kernels, local_gram(): pl.pallas_call(functools.partial(gram_kernel, width=width, norm=norm), in...  11.4 us
    pallas_call x1, Pallas kernels, pair_contraction(): pl.pallas_call(functools.partial(pair_kernel, depths=depths, scale=scale)...  8.45 us
    unnamed x17, local copies, waits for them, and re-layouts  4.6 us
  transfers between devices with their start and end apart: 19, of which 12 were waited for; matrix products, arithmetic and copies ran while one was open for 4% of the time, Pallas kernels for 13%

profile of v6, /device:TPU:0, one launch (start us, length us, event | category | flops | bytes accessed | tf_op | source)
XLA Modules:
  0.0 86.0 jit_solution(12130030977545267072)
XLA Ops:
  0.6 1.2 %copy-done.3 = f32[2,128,1024]{2,1,0:T(8,128)S(1)} copy-done((f32[2,128,1024]{2,1,0:T(8,128)S(1)}, f32[2,128,1024]{2,1,0:T(8,128)}, u32[]{:S(2)}) %copy-start.3) | copy-done | bytes 1048600
  1.9 1.3 %deal.1 = (f32[2,4,40,256]{3,2,1,0:T(8,128)S(1)}, f32[2,4,64,256]{3,2,1,0:T(8,128)S(1)}) custom-call(f32[2,128,1024]{2,1,0:T(8,128)S(1)} %copy-done.3), custom_call_target="tpu_custom_call" | custom-call | tf_op jit(solution)/shard_map/deal/pallas_call | solution.py:227
  3.2 4.1 %collective-permute-start.2 = (f32[2,4,40,256]{3,2,1,0:T(8,128)S(1)}, f32[2,4,40,256]{3,2,1,0:T(8,128)S(1)}, u32[]{:S(2)}, u32[]{:S(2)}) collective-permute-start(f32[2,4,40,256]{3,2,1,0:T(8,128)S(1)} %get-tuple-element.28.refs_0_), channel_id=1, source_target_pairs={{0,16},{4,20},{8,24},{12,28},{16,0},{20,4},{24,8},{28,12},{1,17},{... | collective-permute-start | bytes 983048 | tf_op jit(solution)/shard_map/ppermute | solution.py:135
  7.3 1.6 %collective-permute-start.1 = (f32[2,4,40,256]{3,2,1,0:T(8,128)S(1)}, f32[2,4,40,256]{3,2,1,0:T(8,128)S(1)}, u32[]{:S(2)}, u32[]{:S(2)}) collective-permute-start(f32[2,4,40,256]{3,2,1,0:T(8,128)S(1)} %get-tuple-element.28.refs_0_), channel_id=1, source_target_pairs={{0,8},{4,12},{8,0},{12,4},{16,24},{20,28},{24,16},{28,20},{1,9},{5... | collective-permute-start | bytes 983048 | tf_op jit(solution)/shard_map/ppermute | solution.py:135
  8.8 1.5 %collective-permute-start = (f32[2,4,64,256]{3,2,1,0:T(8,128)S(1)}, f32[2,4,64,256]{3,2,1,0:T(8,128)S(1)}, u32[]{:S(2)}, u32[]{:S(2)}) collective-permute-start(f32[2,4,64,256]{3,2,1,0:T(8,128)S(1)} %get-tuple-element.31.refs_0_), channel_id=1, source_target_pairs={{0,4},{4,0},{8,12},{12,8},{16,20},{20,16},{24,28},{28,24},{1,5},{5... | collective-permute-start | bytes 1572872 | tf_op jit(solution)/shard_map/ppermute | solution.py:135
  11.0 11.4 %local_gram.1 = (f32[1,2,256,256]{3,2,1,0:T(8,128)S(1)}, f32[1,2,256,256]{3,2,1,0:T(8,128)}) custom-call(s32[2,3]{1,0:T(2,128)S(1)} %copy-done.5, f32[2,3,256,1024]{3,2,1,0:T(8,128)} %bitcast.11, f32[2,4,40,256]{3,2,1,0:T(8,128)S(1)} %get-tuple-element.28.refs_0_), custom_call_target="tpu_custom_call" | custom-call | flops 9663676416 | bytes 6291456 | tf_op jit(solution)/shard_map/local_gram/pallas_call | solution.py:100
  22.8 1.7 %collective-permute-done.3 = f32[512,256]{1,0:T(8,128)S(1)} collective-permute-done((f32[512,256]{1,0:T(8,128)S(1)}, f32[512,256]{1,0:T(8,128)S(1)}, u32[]{:S(2)}, u32[]{:S(2)}) %collective-permute-start.3) | collective-permute-done | bytes 524320 | tf_op jit(solution)/shard_map/ppermute | solution.py:135
  24.5 1.1 %bitcast_add_fusion = f32[512,256]{1,0:T(8,128)S(1)} fusion(f32[512,256]{1,0:T(8,128)S(1)} %collective-permute-done.3, f32[1,2,256,256]{3,2,1,0:T(8,128)} %get-tuple-element.29), kind=kLoop, calls=%fused_computation.3 | loop fusion | flops 131072 | bytes 1572864 | tf_op jit(solution)/shard_map/add | solution.py:313
  26.3 1.5 %collective-permute-start.4 = (f32[256,256]{1,0:T(8,128)}, f32[256,256]{1,0:T(8,128)}, u32[]{:S(2)}, u32[]{:S(2)}) collective-permute-start(f32[256,256]{1,0:T(8,128)} %constant_dynamic-slice_fusion.4), channel_id=1, source_target_pairs={{0,2},{1,3},{2,0},{3,1},{4,6},{5,7},{6,4},{7,5},{8,10},{9,11},{10,... | collective-permute-start | bytes 786440 | tf_op jit(solution)/shard_map/ppermute | solution.py:135
  28.1 1.3 %collective-permute-start.6 = (f32[2,4,40,256]{3,2,1,0:T(8,128)S(1)}, f32[2,4,40,256]{3,2,1,0:T(8,128)S(1)}, u32[]{:S(2)}, u32[]{:S(2)}) collective-permute-start(f32[2,4,40,256]{3,2,1,0:T(8,128)S(1)} %get-tuple-element.33.refs_3_), channel_id=1, source_target_pairs={{0,8},{4,12},{8,0},{12,4},{16,24},{20,28},{24,16},{28,20},{1,9},{5... | collective-permute-start | bytes 983048 | tf_op jit(solution)/shard_map/ppermute | solution.py:135
  29.4 1.5 %collective-permute-start.5 = (f32[2,4,40,256]{3,2,1,0:T(8,128)S(1)}, f32[2,4,40,256]{3,2,1,0:T(8,128)S(1)}, u32[]{:S(2)}, u32[]{:S(2)}) collective-permute-start(f32[2,4,40,256]{3,2,1,0:T(8,128)S(1)} %get-tuple-element.33.refs_3_), channel_id=1, source_target_pairs={{0,4},{4,0},{8,12},{12,8},{16,20},{20,16},{24,28},{28,24},{1,5},{5... | collective-permute-start | bytes 983048 | tf_op jit(solution)/shard_map/ppermute | solution.py:135
  31.5 4.2 %collective-permute-done.4 = f32[256,256]{1,0:T(8,128)} collective-permute-done((f32[256,256]{1,0:T(8,128)}, f32[256,256]{1,0:T(8,128)}, u32[]{:S(2)}, u32[]{:S(2)}) %collective-permute-start.4) | collective-permute-done | bytes 262176 | tf_op jit(solution)/shard_map/ppermute | solution.py:135
  35.8 1.0 %dynamic-slice_add_fusion.refs_0_ = f32[256,256]{1,0:T(8,128)S(1)} fusion(f32[256,256]{1,0:T(8,128)} %collective-permute-done.4, f32[512,256]{1,0:T(8,128)S(1)} %bitcast_add_fusion, s32[]{:T(128)S(6)} %select_n.86), kind=kLoop, calls=%fused_computation.10 | loop fusion | flops 65536 | bytes 786436 | tf_op jit(solution)/shard_map/add | solution.py:152
  36.8 0.9 %collective-permute-done.6.refs_2_ = f32[2,4,40,256]{3,2,1,0:T(8,128)S(1)} collective-permute-done((f32[2,4,40,256]{3,2,1,0:T(8,128)S(1)}, f32[2,4,40,256]{3,2,1,0:T(8,128)S(1)}, u32[]{:S(2)}, u32[]{:S(2)}) %collective-permute-start.6) | collective-permute-done | bytes 327712 | tf_op jit(solution)/shard_map/ppermute | solution.py:135
  37.7 1.0 %collective-permute-done.5.refs_1_ = f32[2,4,40,256]{3,2,1,0:T(8,128)S(1)} collective-permute-done((f32[2,4,40,256]{3,2,1,0:T(8,128)S(1)}, f32[2,4,40,256]{3,2,1,0:T(8,128)S(1)}, u32[]{:S(2)}, u32[]{:S(2)}) %collective-permute-start.5) | collective-permute-done | bytes 327712 | tf_op jit(solution)/shard_map/ppermute | solution.py:135
  38.6 1.6 %collective-permute-start.7 = (f32[128,256]{1,0:T(8,128)S(1)}, f32[128,256]{1,0:T(8,128)S(1)}, u32[]{:S(2)}, u32[]{:S(2)}) collective-permute-start(f32[128,256]{1,0:T(8,128)S(1)} %constant_dynamic-slice_fusion.3), channel_id=1, source_target_pairs={{0,4},{4,0},{8,12},{12,8},{16,20},{20,16},{24,28},{28,24},{1,5},{5... | collective-permute-start | bytes 393224 | tf_op jit(solution)/shard_map/ppermute | solution.py:135
  40.9 0.8 collective-permute-start.11
  41.7 3.3 %collective-permute-done.7 = f32[128,256]{1,0:T(8,128)S(1)} collective-permute-done((f32[128,256]{1,0:T(8,128)S(1)}, f32[128,256]{1,0:T(8,128)S(1)}, u32[]{:S(2)}, u32[]{:S(2)}) %collective-permute-start.7) | collective-permute-done | bytes 131104 | tf_op jit(solution)/shard_map/ppermute | solution.py:135
  45.1 2.4 %collective-permute-start.9 = (f32[128,256]{1,0:T(8,128)S(1)}, f32[128,256]{1,0:T(8,128)S(1)}, u32[]{:S(2)}, u32[]{:S(2)}) collective-permute-start(f32[128,256]{1,0:T(8,128)S(1)} %get-tuple-element.38), channel_id=1, source_target_pairs={{0,16},{4,20},{8,24},{12,28},{16,0},{20,4},{24,8},{28,12},{1,17},{... | collective-permute-start | bytes 393224 | tf_op jit(solution)/shard_map/ppermute | solution.py:135
  48.1 3.3 %collective-permute-done.9 = f32[128,256]{1,0:T(8,128)S(1)} collective-permute-done((f32[128,256]{1,0:T(8,128)S(1)}, f32[128,256]{1,0:T(8,128)S(1)}, u32[]{:S(2)}, u32[]{:S(2)}) %collective-permute-start.9) | collective-permute-done | bytes 131104 | tf_op jit(solution)/shard_map/ppermute | solution.py:135
  52.9 2.0 %collective-permute-start.12 = (f32[128,256]{1,0:T(8,128)S(1)}, f32[128,256]{1,0:T(8,128)S(1)}, u32[]{:S(2)}, u32[]{:S(2)}) collective-permute-start(f32[128,256]{1,0:T(8,128)S(1)} %get-tuple-element.41), channel_id=1, source_target_pairs={{0,8},{4,12},{8,0},{12,4},{16,24},{20,28},{24,16},{28,20},{1,9},{5... | collective-permute-start | bytes 393224 | tf_op jit(solution)/shard_map/ppermute | solution.py:135
  54.9 3.0 %collective-permute-done.12 = f32[128,256]{1,0:T(8,128)S(1)} collective-permute-done((f32[128,256]{1,0:T(8,128)S(1)}, f32[128,256]{1,0:T(8,128)S(1)}, u32[]{:S(2)}, u32[]{:S(2)}) %collective-permute-start.12) | collective-permute-done | bytes 131104 | tf_op jit(solution)/shard_map/ppermute | solution.py:135
  57.9 0.8 collective-permute-done.13.refs_1_
  58.8 0.8 copy-done.1
  59.5 2.5 %collective-permute-start.14 = (f32[128,256]{1,0:T(8,128)S(1)}, f32[128,256]{1,0:T(8,128)S(1)}, u32[]{:S(2)}, u32[]{:S(2)}) collective-permute-start(f32[128,256]{1,0:T(8,128)S(1)} %get-tuple-element.43), channel_id=1, source_target_pairs={{0,4},{4,0},{8,12},{12,8},{16,20},{20,16},{24,28},{28,24},{1,5},{5... | collective-permute-start | bytes 393224 | tf_op jit(solution)/shard_map/ppermute | solution.py:135
  62.0 2.9 %collective-permute-done.14 = f32[128,256]{1,0:T(8,128)S(1)} collective-permute-done((f32[128,256]{1,0:T(8,128)S(1)}, f32[128,256]{1,0:T(8,128)S(1)}, u32[]{:S(2)}, u32[]{:S(2)}) %collective-permute-start.14) | collective-permute-done | bytes 131104 | tf_op jit(solution)/shard_map/ppermute | solution.py:135
  65.8 5.7 %collective-permute-done.16 = f32[256,256]{1,0:T(8,128)S(1)} collective-permute-done((f32[256,256]{1,0:T(8,128)S(1)}, f32[256,256]{1,0:T(8,128)S(1)}, u32[]{:S(2)}, u32[]{:S(2)}) %collective-permute-start.16) | collective-permute-done | bytes 262176 | tf_op jit(solution)/shard_map/ppermute | solution.py:135
  71.6 1.9 %collective-permute-done.17 = f32[512,256]{1,0:T(8,128)S(1)} collective-permute-done((f32[512,256]{1,0:T(8,128)S(1)}, f32[512,256]{1,0:T(8,128)S(1)}, u32[]{:S(2)}, u32[]{:S(2)}) %collective-permute-start.17) | collective-permute-done | bytes 524320 | tf_op jit(solution)/shard_map/ppermute | solution.py:135
  73.5 1.0 %copy-done.2 = f32[2,4,48,256]{3,2,1,0:T(8,128)S(1)} copy-done((f32[2,4,48,256]{3,2,1,0:T(8,128)S(1)}, f32[2,4,48,256]{3,2,1,0:T(8,128)}, u32[]{:S(2)}) %copy-start.2) | copy-done | bytes 393240
  74.5 8.4 %pair_contraction.1 = (f32[2,256,256]{2,1,0:T(8,128)}, f32[2,256,256]{2,1,0:T(8,128)S(1)}, f32[2,2,64,32]{3,2,1,0:T(8,128)S(1)}) custom-call(s32[2,2]{1,0:T(2,128)S(1)} %get-tuple-element.35.blocks, f32[1,2,256,256]{3,2,1,0:T(8,128)S(1)} %bitcast.8, f32[1,2,256,256]{3,2,1,0:T(8,128)S(1)} %bitcast.9, bf16[512,512]{1,0:T(8,128)(2,1)S(1)} %get-tuple-element.47.order, ...), custom_call_target="tpu_custom_call" | custom-call | tf_op jit(solution)/shard_map/pair_contraction/pallas_call | solution.py:431
  83.8 1.3 %collective-permute-done.18 = f32[2,256,256]{2,1,0:T(8,128)S(1)} collective-permute-done((f32[2,256,256]{2,1,0:T(8,128)}, f32[2,256,256]{2,1,0:T(8,128)S(1)}, u32[]{:S(2)}, u32[]{:S(2)}) %collective-permute-start.18) | collective-permute-done | bytes 524320 | tf_op jit(solution)/shard_map/ppermute | solution.py:135
  85.1 0.9 %add_bitcast_fusion = f32[1,2,256,256]{3,2,1,0:T(8,128)} fusion(f32[2,256,256]{2,1,0:T(8,128)S(1)} %get-tuple-element.52, f32[2,256,256]{2,1,0:T(8,128)S(1)} %collective-permute-done.18), kind=kLoop, calls=%fused_computation.4 | loop fusion | flops 131072 | bytes 1572864 | tf_op jit(solution)/shard_map/broadcast_in_dim | solution.py:475
  (59 shorter events, 7.3 us)
Async XLA Ops:
  0.6 1.2 %copy-start.3 = (f32[2,128,1024]{2,1,0:T(8,128)S(1)}, f32[2,128,1024]{2,1,0:T(8,128)}, u32[]{:S(2)}) copy-start(f32[2,128,1024]{2,1,0:T(8,128)} %tau.1) | copy-start | bytes 3145732
  3.2 19.3 %copy-start.4 = (f32[2,4,64,256]{3,2,1,0:T(8,128)}, f32[2,4,64,256]{3,2,1,0:T(8,128)S(1)}, u32[]{:S(2)}) copy-start(f32[2,4,64,256]{3,2,1,0:T(8,128)S(1)} %get-tuple-element.31.refs_0_) | copy-start | bytes 1572868
  3.2 19.3 %collective-permute-start.2 = (f32[2,4,40,256]{3,2,1,0:T(8,128)S(1)}, f32[2,4,40,256]{3,2,1,0:T(8,128)S(1)}, u32[]{:S(2)}, u32[]{:S(2)}) collective-permute-start(f32[2,4,40,256]{3,2,1,0:T(8,128)S(1)} %get-tuple-element.28.refs_0_), channel_id=1, source_target_pairs={{0,16},{4,20},{8,24},{12,28},{16,0},{20,4},{24,8},{28,12},{1,17},{... | collective-permute-start | bytes 983048 | tf_op jit(solution)/shard_map/ppermute | solution.py:135
  7.3 15.2 %collective-permute-start.1 = (f32[2,4,40,256]{3,2,1,0:T(8,128)S(1)}, f32[2,4,40,256]{3,2,1,0:T(8,128)S(1)}, u32[]{:S(2)}, u32[]{:S(2)}) collective-permute-start(f32[2,4,40,256]{3,2,1,0:T(8,128)S(1)} %get-tuple-element.28.refs_0_), channel_id=1, source_target_pairs={{0,8},{4,12},{8,0},{12,4},{16,24},{20,28},{24,16},{28,20},{1,9},{5... | collective-permute-start | bytes 983048 | tf_op jit(solution)/shard_map/ppermute | solution.py:135
  8.8 13.6 %collective-permute-start = (f32[2,4,64,256]{3,2,1,0:T(8,128)S(1)}, f32[2,4,64,256]{3,2,1,0:T(8,128)S(1)}, u32[]{:S(2)}, u32[]{:S(2)}) collective-permute-start(f32[2,4,64,256]{3,2,1,0:T(8,128)S(1)} %get-tuple-element.31.refs_0_), channel_id=1, source_target_pairs={{0,4},{4,0},{8,12},{12,8},{16,20},{20,16},{24,28},{28,24},{1,5},{5... | collective-permute-start | bytes 1572872 | tf_op jit(solution)/shard_map/ppermute | solution.py:135
  10.3 0.7 copy-start.5
  11.0 16.8 %copy-start.6 = (s32[32,2]{0,1:T(2,128)S(1)}, s32[32,2]{0,1:T(2,128)}, u32[]{:S(2)}) copy-start(s32[32,2]{0,1:T(2,128)} %param.7) | copy-start | bytes 772
  22.5 29.0 %copy-start = (f32[2,4,64,256]{3,2,1,0:T(8,128)}, f32[2,4,64,256]{3,2,1,0:T(8,128)S(1)}, u32[]{:S(2)}) copy-start(f32[2,4,64,256]{3,2,1,0:T(8,128)S(1)} %get-tuple-element.39.refs_1_) | copy-start | bytes 1572868
  22.5 2.0 %collective-permute-start.3 = (f32[512,256]{1,0:T(8,128)S(1)}, f32[512,256]{1,0:T(8,128)S(1)}, u32[]{:S(2)}, u32[]{:S(2)}) collective-permute-start(f32[512,256]{1,0:T(8,128)S(1)} %get-tuple-element.32), channel_id=1, source_target_pairs={{0,1},{1,0},{2,3},{3,2},{4,5},{5,4},{6,7},{7,6},{8,9},{9,8},{10,11... | collective-permute-start | bytes 1572872 | tf_op jit(solution)/shard_map/ppermute | solution.py:135
  26.3 9.5 %collective-permute-start.4 = (f32[256,256]{1,0:T(8,128)}, f32[256,256]{1,0:T(8,128)}, u32[]{:S(2)}, u32[]{:S(2)}) collective-permute-start(f32[256,256]{1,0:T(8,128)} %constant_dynamic-slice_fusion.4), channel_id=1, source_target_pairs={{0,2},{1,3},{2,0},{3,1},{4,6},{5,7},{6,4},{7,5},{8,10},{9,11},{10,... | collective-permute-start | bytes 786440 | tf_op jit(solution)/shard_map/ppermute | solution.py:135
  28.1 9.5 %collective-permute-start.6 = (f32[2,4,40,256]{3,2,1,0:T(8,128)S(1)}, f32[2,4,40,256]{3,2,1,0:T(8,128)S(1)}, u32[]{:S(2)}, u32[]{:S(2)}) collective-permute-start(f32[2,4,40,256]{3,2,1,0:T(8,128)S(1)} %get-tuple-element.33.refs_3_), channel_id=1, source_target_pairs={{0,8},{4,12},{8,0},{12,4},{16,24},{20,28},{24,16},{28,20},{1,9},{5... | collective-permute-start | bytes 983048 | tf_op jit(solution)/shard_map/ppermute | solution.py:135
  29.4 9.2 %collective-permute-start.5 = (f32[2,4,40,256]{3,2,1,0:T(8,128)S(1)}, f32[2,4,40,256]{3,2,1,0:T(8,128)S(1)}, u32[]{:S(2)}, u32[]{:S(2)}) collective-permute-start(f32[2,4,40,256]{3,2,1,0:T(8,128)S(1)} %get-tuple-element.33.refs_3_), channel_id=1, source_target_pairs={{0,4},{4,0},{8,12},{12,8},{16,20},{20,16},{24,28},{28,24},{1,5},{5... | collective-permute-start | bytes 983048 | tf_op jit(solution)/shard_map/ppermute | solution.py:135
  31.0 14.1 %collective-permute-start.8 = (f32[2,4,48,256]{3,2,1,0:T(8,128)S(1)}, f32[2,4,48,256]{3,2,1,0:T(8,128)S(1)}, u32[]{:S(2)}, u32[]{:S(2)}) collective-permute-start(f32[2,4,48,256]{3,2,1,0:T(8,128)S(1)} %pad_maximum_fusion), channel_id=1, source_target_pairs={{0,2},{1,3},{2,0},{3,1},{4,6},{5,7},{6,4},{7,5},{8,10},{9,11},{10,... | collective-permute-start | bytes 1179656 | tf_op jit(solution)/shard_map/ppermute | solution.py:135
  38.6 6.4 %collective-permute-start.7 = (f32[128,256]{1,0:T(8,128)S(1)}, f32[128,256]{1,0:T(8,128)S(1)}, u32[]{:S(2)}, u32[]{:S(2)}) collective-permute-start(f32[128,256]{1,0:T(8,128)S(1)} %constant_dynamic-slice_fusion.3), channel_id=1, source_target_pairs={{0,4},{4,0},{8,12},{12,8},{16,20},{20,16},{24,28},{28,24},{1,5},{5... | collective-permute-start | bytes 393224 | tf_op jit(solution)/shard_map/ppermute | solution.py:135
  40.3 11.1 %collective-permute-start.10 = (f32[2,4,40,256]{3,2,1,0:T(8,128)S(1)}, f32[2,4,40,256]{3,2,1,0:T(8,128)S(1)}, u32[]{:S(2)}, u32[]{:S(2)}) collective-permute-start(f32[2,4,40,256]{3,2,1,0:T(8,128)S(1)} %pad_maximum_fusion.3), channel_id=1, source_target_pairs={{0,8},{4,12},{8,0},{12,4},{16,24},{20,28},{24,16},{28,20},{1,9},{5... | collective-permute-start | bytes 983048 | tf_op jit(solution)/shard_map/ppermute | solution.py:135
  40.9 10.5 %collective-permute-start.11 = (f32[2,4,40,256]{3,2,1,0:T(8,128)S(1)}, f32[2,4,40,256]{3,2,1,0:T(8,128)S(1)}, u32[]{:S(2)}, u32[]{:S(2)}) collective-permute-start(f32[2,4,40,256]{3,2,1,0:T(8,128)S(1)} %get-tuple-element.40.refs_5_), channel_id=1, source_target_pairs={{0,4},{4,0},{8,12},{12,8},{16,20},{20,16},{24,28},{28,24},{1,5},{5... | collective-permute-start | bytes 983048 | tf_op jit(solution)/shard_map/ppermute | solution.py:135
  45.1 6.3 %collective-permute-start.9 = (f32[128,256]{1,0:T(8,128)S(1)}, f32[128,256]{1,0:T(8,128)S(1)}, u32[]{:S(2)}, u32[]{:S(2)}) collective-permute-start(f32[128,256]{1,0:T(8,128)S(1)} %get-tuple-element.38), channel_id=1, source_target_pairs={{0,16},{4,20},{8,24},{12,28},{16,0},{20,4},{24,8},{28,12},{1,17},{... | collective-permute-start | bytes 393224 | tf_op jit(solution)/shard_map/ppermute | solution.py:135
  47.5 11.2 %collective-permute-start.13 = (f32[2,4,48,256]{3,2,1,0:T(8,128)S(1)}, f32[2,4,48,256]{3,2,1,0:T(8,128)S(1)}, u32[]{:S(2)}, u32[]{:S(2)}) collective-permute-start(f32[2,4,48,256]{3,2,1,0:T(8,128)S(1)} %pad_maximum_fusion.1), channel_id=1, source_target_pairs={{0,2},{1,3},{2,0},{3,1},{4,6},{5,7},{6,4},{7,5},{8,10},{9,11},{10,... | collective-permute-start | bytes 1179656 | tf_op jit(solution)/shard_map/ppermute | solution.py:135
  52.2 12.7 %collective-permute-start.15 = (f32[2,4,48,256]{3,2,1,0:T(8,128)}, f32[2,4,48,256]{3,2,1,0:T(8,128)}, u32[]{:S(2)}, u32[]{:S(2)}) collective-permute-start(f32[2,4,48,256]{3,2,1,0:T(8,128)} %pad_maximum_fusion.2), channel_id=1, source_target_pairs={{0,2},{1,3},{2,0},{3,1},{4,6},{5,7},{6,4},{7,5},{8,10},{9,11},{10,... | collective-permute-start | bytes 1179656 | tf_op jit(solution)/shard_map/ppermute | solution.py:135
  52.9 5.0 %collective-permute-start.12 = (f32[128,256]{1,0:T(8,128)S(1)}, f32[128,256]{1,0:T(8,128)S(1)}, u32[]{:S(2)}, u32[]{:S(2)}) collective-permute-start(f32[128,256]{1,0:T(8,128)S(1)} %get-tuple-element.41), channel_id=1, source_target_pairs={{0,8},{4,12},{8,0},{12,4},{16,24},{20,28},{24,16},{28,20},{1,9},{5... | collective-permute-start | bytes 393224 | tf_op jit(solution)/shard_map/ppermute | solution.py:135
  58.7 0.8 copy-start.1
  59.5 5.4 %collective-permute-start.14 = (f32[128,256]{1,0:T(8,128)S(1)}, f32[128,256]{1,0:T(8,128)S(1)}, u32[]{:S(2)}, u32[]{:S(2)}) collective-permute-start(f32[128,256]{1,0:T(8,128)S(1)} %get-tuple-element.43), channel_id=1, source_target_pairs={{0,4},{4,0},{8,12},{12,8},{16,20},{20,16},{24,28},{28,24},{1,5},{5... | collective-permute-start | bytes 393224 | tf_op jit(solution)/shard_map/ppermute | solution.py:135
  65.0 6.4 %collective-permute-start.16 = (f32[256,256]{1,0:T(8,128)S(1)}, f32[256,256]{1,0:T(8,128)S(1)}, u32[]{:S(2)}, u32[]{:S(2)}) collective-permute-start(f32[256,256]{1,0:T(8,128)S(1)} %get-tuple-element.46), channel_id=1, source_target_pairs={{0,2},{1,3},{2,0},{3,1},{4,6},{5,7},{6,4},{7,5},{8,10},{9,11},{10,... | collective-permute-start | bytes 786440 | tf_op jit(solution)/shard_map/ppermute | solution.py:135
  71.5 2.0 %collective-permute-start.17 = (f32[512,256]{1,0:T(8,128)S(1)}, f32[512,256]{1,0:T(8,128)S(1)}, u32[]{:S(2)}, u32[]{:S(2)}) collective-permute-start(f32[512,256]{1,0:T(8,128)S(1)} %maximum_select_fusion), channel_id=1, source_target_pairs={{0,1},{1,0},{2,3},{3,2},{4,5},{5,4},{6,7},{7,6},{8,9},{9,8},{10,11... | collective-permute-start | bytes 1572872 | tf_op jit(solution)/shard_map/ppermute | solution.py:135
  73.5 1.0 %copy-start.2 = (f32[2,4,48,256]{3,2,1,0:T(8,128)S(1)}, f32[2,4,48,256]{3,2,1,0:T(8,128)}, u32[]{:S(2)}) copy-start(f32[2,4,48,256]{3,2,1,0:T(8,128)} %copy-done.1) | copy-start | bytes 1179652
  82.9 2.2 %collective-permute-start.18 = (f32[2,256,256]{2,1,0:T(8,128)}, f32[2,256,256]{2,1,0:T(8,128)S(1)}, u32[]{:S(2)}, u32[]{:S(2)}) collective-permute-start(f32[2,256,256]{2,1,0:T(8,128)} %get-tuple-element.53), channel_id=1, source_target_pairs={{0,1},{1,0},{2,3},{3,2},{4,5},{5,4},{6,7},{7,6},{8,9},{9,8},{10,11... | collective-permute-start | bytes 1572872 | tf_op jit(solution)/shard_map/ppermute | solution.py:135
